TPU v7x, 128 devices: a whole 4x4x4 slice. The times are simulated.
128 devices in a mesh: ctx: 32 (over x, z, y_lo), head: 4 (over y_hi, core).
Axes of the slice: x: 4, y: 4 (y_hi: 2, y_lo: 2; y = y_hi * 2 + y_lo), z: 4, core: 2. Of those that a mesh axis runs over, the one named last changes fastest.
Arguments:
- latent: bfloat16 [8192, 576], P('ctx'), may hold values from -8 to 8
- query: bfloat16 [8192, 12288], P('ctx', 'head'), may hold values from -300 to 300
- d_out: bfloat16 [8192, 8192], P('ctx', 'head'), may hold values from -6 to 6
- w_uk: bfloat16 [64, 128, 512], P('head'), may hold values from -0.5 to 0.5
- w_uv: bfloat16 [64, 128, 512], P('head'), may hold values from -0.25 to 0.25
- block_mask: int32 [32, 32], replicated, may hold values 0 or 1
- segments: int32 [8192], replicated, may hold values from 0 to 15, never falling along the last dimension, each value on 1 to 1536 neighbouring positions
Outputs:
- attended: bfloat16 [8192, 8192], P('ctx', 'head')
- d_query: bfloat16 [8192, 12288], P('ctx', 'head')
- d_latent: float32 [8192, 576], P('ctx')
- d_w_uk: float32 [64, 128, 512], P('head')
- d_w_uv: float32 [64, 128, 512], P('head')
Inputs may be any that keep to these rules, and one draw needn't show every extreme that they name: block_mask[a, b] = 1 lets every token of block a read every earlier token of block b whatever their dialogues. `segments`: dialogue ids never fall along the sequence; each dialogue holds 1 to 1536 tokens and one holds exactly 1536.
All inputs are finite; a program needn't handle non-finite values.
Results may differ from a plain program's by a relative error of at most 0.012.
The roundings to bfloat16 on the way count: a program that leaves them out, or rounds other values in their place, can miss the bound.
Values may be sent and summed in bfloat16 or wider, within the bound.
No kernel may reach another device: no remote copies, remote signals or barrier semaphores. Data moves between devices by JAX's collectives and lax.ppermute only.
A program may use at most 256 MiB of HBM per device.

v0:
```python
import math

import jax
import jax.numpy as jnp
from jax import lax
from jax.sharding import PartitionSpec as P

SPAN = 2


def shifted(block, axis, distance):
    devices = range(lax.axis_size(axis))
    route = [(i - distance, i) for i in devices if i - distance in devices]
    return lax.ppermute(block, axis, route)


def body(latent, query, d_out, w_uk, w_uv, block_mask, segments):
    tok_rows = latent.shape[0]
    lat_width = latent.shape[1]
    heads_here = w_uk.shape[0]
    nope_width = w_uk.shape[1]
    rank_width = w_uk.shape[2]
    value_width = w_uv.shape[1]
    query_width = query.shape[1] // heads_here
    rope_width = query_width - nope_width
    inv_root = 1.0 / math.sqrt(query_width)
    position = lax.axis_index("ctx")
    queries = query.reshape(tok_rows, heads_here, query_width)
    q_nope = queries[:, :, :nope_width]
    q_rope = queries[:, :, nope_width:]
    absorbed = jnp.einsum("thn,hnr->thr", q_nope, w_uk, preferred_element_type=jnp.float32).astype(
        jnp.bfloat16
    )
    q_full = jnp.concatenate([absorbed, q_rope], axis=2)
    key_blocks = [latent]
    current = latent
    for cycle_step in range(SPAN):
        current = shifted(current, "ctx", 1)
        key_blocks.append(current)
    offsets = jnp.arange(tok_rows, dtype=jnp.int32)
    seg_query = lax.dynamic_slice_in_dim(segments, position * tok_rows, tok_rows)
    q_pos = position * tok_rows + offsets
    masks = []
    actives = []
    for cycle_step in range(SPAN + 1):
        key_block = position - cycle_step
        clamped = jnp.maximum(key_block, 0)
        seg_key = lax.dynamic_slice_in_dim(segments, clamped * tok_rows, tok_rows)
        granted = block_mask[position, clamped]
        k_pos = key_block * tok_rows + offsets
        allowed = (
            (key_block >= 0)
            & (k_pos[None, :] <= q_pos[:, None])
            & ((seg_query[:, None] == seg_key[None, :]) | (granted == 1))
        )
        masks.append(allowed)
        if cycle_step == 0:
            actives.append(jnp.array(True))
        else:
            actives.append(
                (key_block >= 0) & ((granted == 1) | (seg_key[tok_rows - 1] == seg_query[0]))
            )
    score_list = []
    for cycle_step in range(SPAN + 1):

        def score_fn(block_keys=key_blocks[cycle_step]):
            return (
                jnp.einsum("thl,kl->htk", q_full, block_keys, preferred_element_type=jnp.float32)
                * inv_root
            )

        raw_scores = score_fn()
        score_list.append(jnp.where(masks[cycle_step][None], raw_scores, -jnp.inf))
    scores = jnp.concatenate(score_list, axis=2)
    row_max = jnp.max(scores, axis=2, keepdims=True)
    weights = jnp.exp(scores - row_max)
    probs = weights / jnp.sum(weights, axis=2, keepdims=True)
    probs_low = probs.astype(jnp.bfloat16)
    prob_blocks = [
        probs_low[:, :, cycle_step * tok_rows : (cycle_step + 1) * tok_rows]
        for cycle_step in range(SPAN + 1)
    ]
    out_shape = (tok_rows, heads_here, rank_width)
    latent_sum = jnp.zeros(out_shape, jnp.float32)
    for cycle_step in range(SPAN + 1):

        def value_fn(block_probs=prob_blocks[cycle_step], block_keys=key_blocks[cycle_step]):
            return jnp.einsum(
                "htk,kr->thr",
                block_probs,
                block_keys[:, :rank_width],
                preferred_element_type=jnp.float32,
            )

        latent_sum = latent_sum + value_fn()
    latent_out = latent_sum.astype(jnp.bfloat16)
    attended = jnp.einsum(
        "thr,hvr->thv", latent_out, w_uv, preferred_element_type=jnp.float32
    ).astype(jnp.bfloat16)
    grads = d_out.reshape(tok_rows, heads_here, value_width)
    d_latent_out = jnp.einsum(
        "thv,hvr->thr", grads, w_uv, preferred_element_type=jnp.float32
    ).astype(jnp.bfloat16)
    grad_uv = jnp.einsum("thv,thr->hvr", grads, latent_out, preferred_element_type=jnp.float32)
    dprob_list = []
    for cycle_step in range(SPAN + 1):

        def dprob_fn(block_keys=key_blocks[cycle_step]):
            return jnp.einsum(
                "thr,kr->htk",
                d_latent_out,
                block_keys[:, :rank_width],
                preferred_element_type=jnp.float32,
            )

        dprob_list.append(dprob_fn())
    d_probs = jnp.concatenate(dprob_list, axis=2)
    delta = jnp.sum(probs * d_probs, axis=2, keepdims=True)
    d_scores = (probs * (d_probs - delta) * inv_root).astype(jnp.bfloat16)
    dscore_blocks = [
        d_scores[:, :, cycle_step * tok_rows : (cycle_step + 1) * tok_rows]
        for cycle_step in range(SPAN + 1)
    ]
    full_shape = (tok_rows, heads_here, lat_width)
    d_full = jnp.zeros(full_shape, jnp.float32)
    key_parts = []
    for cycle_step in range(SPAN + 1):

        def dquery_fn(block_grads=dscore_blocks[cycle_step], block_keys=key_blocks[cycle_step]):
            return jnp.einsum(
                "htk,kl->thl", block_grads, block_keys, preferred_element_type=jnp.float32
            )

        def dkey_fn(block_grads=dscore_blocks[cycle_step], block_probs=prob_blocks[cycle_step]):
            from_scores = jnp.einsum(
                "htk,thl->kl", block_grads, q_full, preferred_element_type=jnp.float32
            )
            from_values = jnp.einsum(
                "htk,thr->kr", block_probs, d_latent_out, preferred_element_type=jnp.float32
            )
            return from_scores + jnp.pad(from_values, ((0, 0), (0, rope_width)))

        d_full = d_full + dquery_fn()
        key_parts.append(dkey_fn())
    d_absorbed = d_full[:, :, :rank_width].astype(jnp.bfloat16)
    d_nope = jnp.einsum("thr,hnr->thn", d_absorbed, w_uk, preferred_element_type=jnp.float32)
    d_query = jnp.concatenate([d_nope, d_full[:, :, rank_width:]], axis=2).astype(jnp.bfloat16)
    grad_uk = jnp.einsum("thn,thr->hnr", q_nope, d_absorbed, preferred_element_type=jnp.float32)
    returned = jnp.zeros((tok_rows, lat_width), jnp.float32)
    for cycle_step in range(1, SPAN + 1):
        returned = returned + shifted(
            key_parts[cycle_step].astype(jnp.bfloat16), "ctx", -cycle_step
        ).astype(jnp.float32)
    d_latent = lax.psum(key_parts[0] + returned, "head")
    d_w_uk, d_w_uv = lax.psum((grad_uk, grad_uv), "ctx")
    return (
        attended.reshape(tok_rows, heads_here * value_width),
        d_query.reshape(tok_rows, heads_here * query_width),
        d_latent,
        d_w_uk,
        d_w_uv,
    )


def solution(mesh):
    in_specs = (
        P("ctx", None),
        P("ctx", "head"),
        P("ctx", "head"),
        P("head", None, None),
        P("head", None, None),
        P(),
        P(),
    )
    out_specs = (
        P("ctx", "head"),
        P("ctx", "head"),
        P("ctx", None),
        P("head", None, None),
        P("head", None, None),
    )
    return jax.shard_map(body, mesh=mesh, in_specs=in_specs, out_specs=out_specs, check_vma=False)
```

profile of v0, /device:TPU:1, one launch (start us, length us, event | category | flops | bytes accessed | tf_op | source)
XLA Modules:
  0.0 555.5 jit_solution(8285977508498312817)
XLA Ops:
  7.2 4.9 collective-permute-start
  15.5 2.6 copy.46
  20.0 5.2 convert_bitcast_fusion
  28.4 2.1 fusion.125
  30.5 3.3 fusion.25
  33.9 2.8 collective-permute-start.1
  36.6 3.0 fusion.126
  39.6 4.5 fusion.28
  48.2 2.1 fusion.121
  53.1 5.5 fusion.51
  58.6 5.6 %fusion.8 = bf16[256,16,512]{2,0,1:T(8,128)(2,1)S(1)} fusion(f32[16,256,512]{2,1,0:T(8,128)S(1)} %fusion.54, f32[16,256,512]{2,1,0:T(8,128)} %fusion.51, bf16[16,256,768]{1,2,0:T(8,128)(2,1)} %copy-done.5, bf16[256,576]{0,1:T(8,128)(2,1)S(1)} %collective-permute-done.1), kind=kOutput, calls=%fused_computation.13 | convolution fusion | flops 1080033280 | bytes 23330816 | tf_op jit(solution)/shard_map/htk,kr->thr/dot_general | solution.py:88
  64.2 3.4 convolution_bitcast_fusion
  67.7 3.3 fusion.31
  71.0 20.9 %multiply_convert_fusion = bf16[16,256,768]{1,2,0:T(8,128)(2,1)} fusion(f32[16,256,256]{1,2,0:T(8,128)} %fusion.31, f32[16,256,256]{1,2,0:T(8,128)} %fusion.28, f32[16,256,256]{1,2,0:T(8,128)} %fusion.25, f32[16,256]{1,0:T(8,128)S(1)} %fusion.6, f32[16,256]{1,0:T(8,128)S(1)} %maximum_maximum_fusion, f32[16,256,256]{1,2,0:T(8,128)} %copy-done.9, ...), kind=kOutput, calls=%fused_computation.4 | output fusion | flops 53482240 | bytes 31490048 | tf_op jit(solution)/shard_map/sub | solution.py:119
  91.9 3.1 fusion.46
  95.3 6.0 %fusion.42 = f32[16,256,576]{1,2,0:T(8,128)} fusion(bf16[16,256,768]{1,2,0:T(8,128)(2,1)S(1)} %copy-done.10, bf16[256,576]{0,1:T(8,128)(2,1)} %collective-permute-done), kind=kOutput, calls=%fused_computation.45 | convolution fusion | flops 1207959552 | bytes 11829248 | tf_op jit(solution)/shard_map/htk,kl->thl/dot_general | solution.py:130
  101.3 6.2 %fusion.7 = bf16[256,16,576]{0,2,1:T(8,128)(2,1)S(1)} fusion(f32[16,256,576]{1,2,0:T(8,128)S(1)} %fusion.46, f32[16,256,576]{1,2,0:T(8,128)} %fusion.42, bf16[16,256,768]{1,2,0:T(8,128)(2,1)} %multiply_convert_fusion, bf16[256,576]{0,1:T(8,128)(2,1)S(1)} %collective-permute-done.1), kind=kOutput, calls=%fused_computation.11 | convolution fusion | flops 1215037440 | bytes 25985024 | tf_op jit(solution)/shard_map/htk,kl->thl/dot_general | solution.py:130
  107.5 2.2 copy-done.6
  109.7 3.2 fusion.34
  113.1 4.3 fusion.76
  117.4 3.9 fusion.95
  122.5 2.9 fusion.81
  125.4 3.9 fusion.98
  133.8 4.3 fusion.71
  138.1 2.6 collective-permute-done.3
  140.7 3.9 add_add_fusion
  144.6 3.6 fusion.59
  149.5 2.6 copy.78
  152.0 347.6 %all-reduce.9.cloned.1.call-done = (f32[16,128,512]{1,2,0:T(8,128)}, f32[16,128,512]{1,2,0:T(8,128)}) async-done(((f32[16,128,512]{1,2,0:T(8,128)}, f32[16,128,512]{1,2,0:T(8,128)}), (f32[16,128,512]{1,2,0:T(8,128)}, f32[16,128,512]{1,2,0:T(8,128)})) %all-reduce.9.cloned.1.call-update) | async-done | bytes 8388624 | tf_op jit(solution)/shard_map/psum | solution.py:155
  499.6 5.3 copy.79
  505.0 5.3 copy.80
  510.3 36.5 %all-reduce.7.cloned.1.call-done = f32[256,576]{0,1:T(8,128)} async-done(((f32[256,576]{0,1:T(8,128)}), f32[256,576]{0,1:T(8,128)}) %all-reduce.7.cloned.1.call-update) | async-done | bytes 589840 | tf_op jit(solution)/shard_map/psum | solution.py:154
  (68 shorter events, 22.6 us)
Async XLA Ops:
  7.2 18.0 %copy-start = (bf16[16,128,512]{2,1,0:T(8,128)(2,1)S(1)}, bf16[16,128,512]{2,1,0:T(8,128)(2,1)}, u32[]{:S(2)}) copy-start(bf16[16,128,512]{2,1,0:T(8,128)(2,1)} %param.11) | copy-start | bytes 6291460
  7.2 492.5 %all-reduce.9.cloned.1.call-start = ((), (), s32[]{:S(2)}) async-start(), calls=%async_computation.1 | async-start | bytes 16777216 | tf_op jit(solution)/shard_map/psum | solution.py:155
  7.2 26.6 %collective-permute-start = (bf16[256,576]{0,1:T(8,128)(2,1)}, bf16[256,576]{0,1:T(8,128)(2,1)}, u32[]{:S(2)}, u32[]{:S(2)}) collective-permute-start(bf16[256,576]{0,1:T(8,128)(2,1)} %param.7), channel_id=1, source_target_pairs={{0,4},{4,8},{8,12},{12,16},{16,20},{20,24},{24,28},{28,32},{32,36}... | collective-permute-start | bytes 884744 | tf_op jit(solution)/shard_map/ppermute | solution.py:14
  18.0 7.2 %copy-start.12 = (bf16[256,2048]{1,0:T(8,128)(2,1)S(1)}, bf16[256,2048]{1,0:T(8,128)(2,1)}, u32[]{:S(2)}) copy-start(bf16[256,2048]{1,0:T(8,128)(2,1)} %param.9) | copy-start | bytes 3145732
  25.2 3.2 copy-start.16
  25.2 3.2 copy-start.13
  25.2 3.2 copy-start.19
  26.5 41.1 %copy-start.1 = (bf16[16,512,256]{2,1,0:T(8,128)(2,1)}, bf16[16,512,256]{2,1,0:T(8,128)(2,1)S(1)}, u32[]{:S(2)}) copy-start(bf16[16,512,256]{2,1,0:T(8,128)(2,1)S(1)} %convolution_convert_fusion) | copy-start | bytes 12582916
  30.5 17.6 %copy-start.7 = (f32[16,256,256]{1,2,0:T(8,128)}, f32[16,256,256]{1,2,0:T(8,128)S(1)}, u32[]{:S(2)}) copy-start(f32[16,256,256]{1,2,0:T(8,128)S(1)} %get-tuple-element.30) | copy-start | bytes 12582916
  33.9 10.3 %collective-permute-start.1 = (bf16[256,576]{0,1:T(8,128)(2,1)}, bf16[256,576]{0,1:T(8,128)(2,1)S(1)}, u32[]{:S(2)}, u32[]{:S(2)}) collective-permute-start(bf16[256,576]{0,1:T(8,128)(2,1)} %collective-permute-done), channel_id=1, source_target_pairs={{0,4},{4,8},{8,12},{12,16},{16,20},{20,24},{24,28},{28,32},{32,36}... | collective-permute-start | bytes 884744 | tf_op jit(solution)/shard_map/ppermute | solution.py:14
  39.6 8.5 %copy-start.8 = (f32[16,256,256]{1,2,0:T(8,128)}, f32[16,256,256]{1,2,0:T(8,128)S(1)}, u32[]{:S(2)}) copy-start(f32[16,256,256]{1,2,0:T(8,128)S(1)} %get-tuple-element.32) | copy-start | bytes 12582916
  46.3 2.0 copy-start.9
  48.2 2.1 copy-start.17
  50.4 2.7 copy-start.5
  64.2 3.5 copy-start.3
  71.0 20.9 %copy-start.18 = (bf16[256,576]{0,1:T(8,128)(2,1)S(1)}, bf16[256,576]{0,1:T(8,128)(2,1)}, u32[]{:S(2)}) copy-start(bf16[256,576]{0,1:T(8,128)(2,1)} %param.7) | copy-start | bytes 884740
  91.9 3.4 copy-start.10
  101.3 8.4 %copy-start.11 = (bf16[256,3072]{0,1:T(8,128)(2,1)S(1)}, bf16[256,3072]{0,1:T(8,128)(2,1)}, u32[]{:S(2)}) copy-start(bf16[256,3072]{0,1:T(8,128)(2,1)} %copy.46) | copy-start | bytes 4718596
  107.5 2.2 copy-start.6
  113.0 4.3 copy-start.20
  113.0 433.8 %all-reduce.7.cloned.1.call-start = ((), (), s32[]{:S(2)}) async-start(), calls=%async_computation | async-start | bytes 1179648 | tf_op jit(solution)/shard_map/psum | solution.py:154
  113.1 4.3 copy-start.14
  117.4 5.2 copy-start.2
  121.2 16.8 %collective-permute-start.2 = (bf16[256,576]{0,1:T(8,128)(2,1)}, bf16[256,576]{0,1:T(8,128)(2,1)S(1)}, u32[]{:S(2)}, u32[]{:S(2)}) collective-permute-start(bf16[256,576]{0,1:T(8,128)(2,1)} %fusion.95), channel_id=1, source_target_pairs={{4,0},{8,4},{12,8},{16,12},{20,16},{24,20},{28,24},{32,28},{36,32}... | collective-permute-start | bytes 884744 | tf_op jit(solution)/shard_map/ppermute | solution.py:14
  125.4 5.2 copy-start.4
  129.3 11.4 %collective-permute-start.3 = (bf16[256,576]{0,1:T(8,128)(2,1)}, bf16[256,576]{0,1:T(8,128)(2,1)}, u32[]{:S(2)}, u32[]{:S(2)}) collective-permute-start(bf16[256,576]{0,1:T(8,128)(2,1)} %fusion.98), channel_id=1, source_target_pairs={{8,0},{12,4},{16,8},{20,12},{24,16},{28,20},{32,24},{36,28},{40,32... | collective-permute-start | bytes 884744 | tf_op jit(solution)/shard_map/ppermute | solution.py:14
  133.8 6.9 %copy-start.15 = (bf16[256,16,512]{0,2,1:T(8,128)(2,1)S(1)}, bf16[256,16,512]{0,2,1:T(8,128)(2,1)}, u32[]{:S(2)}) copy-start(bf16[256,16,512]{0,2,1:T(8,128)(2,1)} %convert_bitcast_fusion) | copy-start | bytes 12582916
  133.8 6.9 %copy-start.21 = (bf16[256,16,64]{0,2,1:T(8,128)(2,1)S(1)}, bf16[256,16,64]{0,2,1:T(8,128)(2,1)}, u32[]{:S(2)}) copy-start(bf16[256,16,64]{0,2,1:T(8,128)(2,1)} %slice.58) | copy-start | bytes 1572868
  144.6 3.7 slice-start
Sparse Core Ops, SparseCore 0:
  113.1 386.4 all-reduce.8
  502.7 44.0 all-reduce.6
where the time goes:
time: 556 us
  waiting for transfers between devices  387 us (70%)
  matrix products  87.4 us (16%)
  other arithmetic  27.9 us (5%)
  local copies, waits for them, and re-layouts  26.9 us (5%)
  between operations  16.4 us (3%)
  starting transfers between devices  10.3 us (2%)
    psum x1, waiting for transfers between devices, body(): d_w_uk, d_w_uv = lax.psum((grad_uk, grad_uv), 'ctx')  348 us
    psum x1, waiting for transfers between devices, body(): d_latent = lax.psum(key_parts[0] + returned, 'head')  36.5 us
    unnamed x50, local copies, waits for them, and re-layouts  23.5 us
    sub x1, other arithmetic, body(): d_scores = (probs * (d_probs - delta) * inv_root).astype(jnp.bfloat16)  20.9 us
    dot_general x3, matrix products, dquery_fn(): jnp.einsum('htk,kl->thl', block_grads, block_keys, preferred_element_type...  15.4 us
    dot_general x3, matrix products, value_fn(): jnp.einsum('htk,kr->thr', block_probs, block_keys[:, :rank_width], prefer...  12.4 us
    dot_general x3, matrix products, dkey_fn(): jnp.einsum('htk,thl->kl', block_grads, q_full, preferred_element_type=jnp...  11.6 us
    dot_general x3, matrix products, dkey_fn(): jnp.einsum('htk,thr->kr', block_probs, d_latent_out, preferred_element_ty...  11.4 us
  transfers between devices with their start and end apart: 6, of which 3 were waited for; matrix products, arithmetic and copies ran while one was open for 13% of the time, Pallas kernels for 0%

commit v1 on v0

v1 whole, which is shorter than its diff:
```python
import functools
import math

import jax
import jax.numpy as jnp
from jax import lax
from jax.experimental import pallas as pl
from jax.experimental.pallas import tpu as pltpu
from jax.sharding import PartitionSpec as P

SPAN = 2
LOG2E = 1.4426950408889634
VMEM_LIMIT = 56 * 1024 * 1024


def shifted(block, axis, distance):
    devices = range(lax.axis_size(axis))
    route = [(i - distance, i) for i in devices if i - distance in devices]
    return lax.ppermute(block, axis, route)


def dot(a, b):
    return lax.dot_general(a, b, (((1,), (0,)), ((), ())), preferred_element_type=jnp.float32)


def dot_nt(a, b):
    return lax.dot_general(a, b, (((1,), (1,)), ((), ())), preferred_element_type=jnp.float32)


def prepare_kernel(query_ref, dout_ref, wuk_ref, wuv_ref, qfull_ref, dlo_ref, dout_t_ref, nope_t_ref):
    nope = wuk_ref.shape[1]
    value = wuv_ref.shape[1]
    width = query_ref.shape[1] // 2
    rank = wuk_ref.shape[2]
    query_t = query_ref[...].T
    dout_t = dout_ref[...].T
    for n in range(2):
        q_nope = query_t[n * width : n * width + nope]
        grads = dout_t[n * value : (n + 1) * value]
        nope_t_ref[n] = q_nope
        dout_t_ref[n] = grads
        qfull_ref[n, :rank] = dot(wuk_ref[n].T, q_nope).astype(jnp.bfloat16)
        qfull_ref[n, rank:] = query_t[n * width + nope : (n + 1) * width]
        dlo_ref[n] = dot(wuv_ref[n].T, grads).astype(jnp.bfloat16)


def prepare(query, d_out, w_uk, w_uv):
    toks = query.shape[0]
    heads, nope, rank = w_uk.shape
    value = w_uv.shape[1]
    width = query.shape[1] // heads
    lat = rank + width - nope
    shape = lambda rows: jax.ShapeDtypeStruct((heads, rows, toks), jnp.bfloat16)
    block = lambda rows: pl.BlockSpec((2, rows, toks), lambda s: (s, 0, 0))
    return pl.pallas_call(
        prepare_kernel,
        grid=(heads // 2,),
        in_specs=[
            pl.BlockSpec((toks, 2 * width), lambda s: (0, s)),
            pl.BlockSpec((toks, 2 * value), lambda s: (0, s)),
            pl.BlockSpec((2, nope, rank), lambda s: (s, 0, 0)),
            pl.BlockSpec((2, value, rank), lambda s: (s, 0, 0)),
        ],
        out_specs=[block(lat), block(rank), block(value), block(nope)],
        out_shape=[shape(lat), shape(rank), shape(value), shape(nope)],
        compiler_params=pltpu.CompilerParams(vmem_limit_bytes=VMEM_LIMIT),
        cost_estimate=pl.CostEstimate(
            flops=4 * heads * toks * nope * rank, bytes_accessed=16 * 2**20, transcendentals=0
        ),
        name="prepare",
    )(query, d_out, w_uk, w_uv)


def attend_kernel(
    inv_root,
    keys_ref,
    bias_ref,
    qfull_ref,
    dlo_ref,
    dout_t_ref,
    nope_t_ref,
    wuk_ref,
    wuv_ref,
    att_ref,
    dq_ref,
    guk_ref,
    guv_ref,
    dlat_ref,
    keys_t_ref,
):
    step = pl.program_id(0)
    rank = wuk_ref.shape[2]
    nope = wuk_ref.shape[1]
    value = wuv_ref.shape[1]
    width = dq_ref.shape[1] // 2

    @pl.when(step == 0)
    def _():
        keys_t_ref[...] = keys_ref[...].T
        dlat_ref[...] = jnp.zeros_like(dlat_ref)

    for n in range(2):
        qfull = qfull_ref[n]
        dlo = dlo_ref[n]
        scaled = dot(keys_ref[...], qfull) * (inv_root * LOG2E) + bias_ref[...]
        top = jnp.max(scaled, axis=0, keepdims=True)
        weights = jnp.exp2(scaled - top)
        probs = weights * (1.0 / jnp.sum(weights, axis=0, keepdims=True))
        probs_low = probs.astype(jnp.bfloat16)
        latent_out = dot(keys_t_ref[:rank], probs_low).astype(jnp.bfloat16)
        att_ref[:, n * value : (n + 1) * value] = dot(wuv_ref[n], latent_out).T.astype(jnp.bfloat16)
        guv_ref[n] = dot_nt(dout_t_ref[n], latent_out).astype(guv_ref.dtype)
        d_probs = dot(keys_ref[:, :rank], dlo)
        delta = jnp.sum(probs * d_probs, axis=0, keepdims=True)
        d_scores = (probs * (d_probs - delta) * inv_root).astype(jnp.bfloat16)
        d_full = dot(keys_t_ref[...], d_scores)
        d_absorbed = d_full[:rank].astype(jnp.bfloat16)
        d_nope = dot(wuk_ref[n], d_absorbed)
        guk_ref[n] = dot_nt(nope_t_ref[n], d_absorbed).astype(guk_ref.dtype)
        dq_ref[:, n * width : n * width + nope] = d_nope.T.astype(jnp.bfloat16)
        dq_ref[:, n * width + nope : (n + 1) * width] = d_full[rank:].T.astype(jnp.bfloat16)
        dlat_ref[:rank] += dot_nt(qfull[:rank], d_scores) + dot_nt(dlo, probs_low)
        dlat_ref[rank:] += dot_nt(qfull[rank:], d_scores)


def attend(keys, bias, qfull, dlo, dout_t, nope_t, w_uk, w_uv, inv_root):
    heads, nope, rank = w_uk.shape
    value = w_uv.shape[1]
    span, lat = keys.shape
    toks = qfull.shape[2]
    width = nope + lat - rank
    whole = lambda rows, cols: pl.BlockSpec((rows, cols), lambda s: (0, 0))
    pair = lambda rows, cols: pl.BlockSpec((2, rows, cols), lambda s: (s, 0, 0))
    out = jax.ShapeDtypeStruct
    return pl.pallas_call(
        functools.partial(attend_kernel, inv_root),
        grid=(heads // 2,),
        in_specs=[
            whole(span, lat),
            whole(span, toks),
            pair(lat, toks),
            pair(rank, toks),
            pair(value, toks),
            pair(nope, toks),
            pair(nope, rank),
            pair(value, rank),
        ],
        out_specs=[
            pl.BlockSpec((toks, 2 * value), lambda s: (0, s)),
            pl.BlockSpec((toks, 2 * width), lambda s: (0, s)),
            pair(nope, rank),
            pair(value, rank),
            whole(lat, span),
        ],
        out_shape=[
            out((toks, heads * value), jnp.bfloat16),
            out((toks, heads * width), jnp.bfloat16),
            out((heads, nope, rank), jnp.bfloat16),
            out((heads, value, rank), jnp.bfloat16),
            out((lat, span), jnp.float32),
        ],
        scratch_shapes=[pltpu.VMEM((lat, span), jnp.bfloat16)],
        compiler_params=pltpu.CompilerParams(vmem_limit_bytes=VMEM_LIMIT),
        cost_estimate=pl.CostEstimate(
            flops=heads * toks * (span * 4 * (rank + lat) + span * 2 * (rank + lat) + 8 * nope * rank),
            bytes_accessed=30 * 2**20,
            transcendentals=heads * toks * span,
        ),
        name="attend",
    )(keys, bias, qfull, dlo, dout_t, nope_t, w_uk, w_uv)


def summed_over_ctx(grads):
    rows, cols = grads.shape
    parts = lax.axis_size("ctx")
    pieces = lax.all_to_all(grads.reshape(parts, rows // parts, cols), "ctx", 0, 0, tiled=True)
    mine = jnp.sum(pieces.astype(jnp.float32), axis=0).astype(grads.dtype)
    sent = jnp.broadcast_to(mine[None], (parts,) + mine.shape)
    return lax.all_to_all(sent, "ctx", 0, 0, tiled=True).reshape(rows, cols)


def body(latent, query, d_out, w_uk, w_uv, block_mask, segments):
    toks, lat = latent.shape
    heads, nope, rank = w_uk.shape
    value = w_uv.shape[1]
    width = query.shape[1] // heads
    inv_root = 1.0 / math.sqrt(width)
    position = lax.axis_index("ctx")
    earlier = [shifted(latent, "ctx", distance) for distance in (2, 1)]
    qfull, dlo, dout_t, nope_t = prepare(query, d_out, w_uk, w_uv)

    offsets = jnp.arange(toks, dtype=jnp.int32)
    seg_query = lax.dynamic_slice_in_dim(segments, position * toks, toks)
    bias = []
    for distance in (2, 1, 0):
        block = position - distance
        clamped = jnp.maximum(block, 0)
        seg_key = lax.dynamic_slice_in_dim(segments, clamped * toks, toks)
        granted = block_mask[position, clamped]
        allowed = (
            (block >= 0)
            & (offsets[:, None] - distance * toks <= offsets[None, :])
            & ((seg_key[:, None] == seg_query[None, :]) | (granted == 1))
        )
        bias.append(jnp.where(allowed, 0.0, -jnp.inf).astype(jnp.float32))
    bias = jnp.concatenate(bias, axis=0)
    keys = jnp.concatenate(earlier + [latent], axis=0)
    attended, d_query, guk, guv, dlat_t = attend(
        keys, bias, qfull, dlo, dout_t, nope_t, w_uk, w_uv, inv_root
    )
    dlat = dlat_t.T
    returned = [
        shifted(dlat[part * toks : (part + 1) * toks].astype(jnp.bfloat16), "ctx", part - SPAN)
        for part in range(SPAN)
    ]
    own = dlat[SPAN * toks :] + (returned[0].astype(jnp.float32) + returned[1].astype(jnp.float32))
    d_latent = lax.psum(own, "head")
    grads = jnp.concatenate([guk.reshape(heads * nope, rank), guv.reshape(heads * value, rank)], axis=0)
    grads = summed_over_ctx(grads).astype(jnp.float32)
    d_w_uk = grads[: heads * nope].reshape(w_uk.shape)
    d_w_uv = grads[heads * nope :].reshape(w_uv.shape)
    return attended, d_query, d_latent, d_w_uk, d_w_uv


def solution(mesh):
    in_specs = (
        P("ctx", None),
        P("ctx", "head"),
        P("ctx", "head"),
        P("head", None, None),
        P("head", None, None),
        P(),
        P(),
    )
    out_specs = (
        P("ctx", "head"),
        P("ctx", "head"),
        P("ctx", None),
        P("head", None, None),
        P("head", None, None),
    )
    return jax.shard_map(body, mesh=mesh, in_specs=in_specs, out_specs=out_specs, check_vma=False)
```

time: 556 us -> 282 us (0.51)
  waiting for transfers between devices: 387 us -> 99.2 us
  matrix products: 87.4 us -> 0 us
  Pallas kernels: 0 us -> 69.7 us
  blocking collectives: 0 us -> 56.5 us
  other arithmetic: 27.9 us -> 8.54 us
  local copies, waits for them, and re-layouts: 26.9 us -> 14.7 us
  starting transfers between devices: 10.3 us -> 16.3 us
    psum x2 -> x1, waiting for transfers between devices: 384 us -> 46.2 us  [body(): d_latent = lax.psum(own, 'head')]
    dot_general x24 -> x0, matrix products: 87.4 us -> none  [the longest x3 15.4 us: dquery_fn(): jnp.einsum('htk,kl->thl', block_grads, block_keys, preferred_element_type...]
    pallas_call x0 -> x2, Pallas kernels: none -> 69.7 us  [the longest x1 58.9 us: attend(): pl.pallas_call(functools.partial(attend_kernel, inv_root), grid=(heads //...]
    all_to_all x0 -> x1, blocking collectives: none -> 56.5 us  [summed_over_ctx(): lax.all_to_all(grads.reshape(parts, rows // parts, cols), 'ctx', 0, 0, ti...]
    ppermute x4, waiting for transfers between devices: 2.6 us -> 53 us  [shifted(): return lax.ppermute(block, axis, route)]
    sub x1, other arithmetic: 20.9 us -> 0.01 us  [body(): offsets[:, None] - distance * toks <= offsets[None, :]]
    unnamed x50 -> x4, local copies, waits for them, and re-layouts: 23.5 us -> 3.08 us
    all_to_all x0 -> x1, starting transfers between devices: none -> 6.08 us  [summed_over_ctx(): return lax.all_to_all(sent, 'ctx', 0, 0, tiled=True).reshape(rows, cols)]
  transfers between devices with their start and end apart: 6 -> 6, of which waited for: 3 -> 3; matrix products, arithmetic and copies ran while one was open for 13% -> 4% of each run, Pallas kernels for 0% -> 4%
where the time goes in v1:
time: 282 us; the launch traced here: 281 us
  waiting for transfers between devices  99.2 us (35%)
  Pallas kernels  69.7 us (25%)
  blocking collectives  56.5 us (20%)
  starting transfers between devices  16.3 us (6%)
  between operations  16.1 us (6%)
  local copies, waits for them, and re-layouts  14.7 us (5%)
  other arithmetic  8.54 us (3%)
    pallas_call x1, Pallas kernels, attend(): pl.pallas_call(functools.partial(attend_kernel, inv_root), grid=(heads //...  58.9 us
    all_to_all x1, blocking collectives, summed_over_ctx(): lax.all_to_all(grads.reshape(parts, rows // parts, cols), 'ctx', 0, 0, ti...  56.5 us
    ppermute x4, waiting for transfers between devices, shifted(): return lax.ppermute(block, axis, route)  53 us
    psum x1, waiting for transfers between devices, body(): d_latent = lax.psum(own, 'head')  46.2 us
    pallas_call x1, Pallas kernels, prepare(): pl.pallas_call(prepare_kernel, grid=(heads // 2,), in_specs=[pl.BlockSpec...  10.8 us
    ppermute x4, starting transfers between devices, shifted(): return lax.ppermute(block, axis, route)  10.2 us
    slice x1, local copies, waits for them, and re-layouts, body(): d_w_uv = grads[heads * nope:].reshape(w_uv.shape)  6.76 us
    all_to_all x1, starting transfers between devices, summed_over_ctx(): return lax.all_to_all(sent, 'ctx', 0, 0, tiled=True).reshape(rows, cols)  6.08 us
  transfers between devices with their start and end apart: 6, of which 3 were waited for; matrix products, arithmetic and copies ran while one was open for 4% of the time, Pallas kernels for 4%

profile of v1, /device:TPU:1, one launch (start us, length us, event | category | flops | bytes accessed | tf_op | source)
XLA Modules:
  0.0 281.1 jit_solution(17594950167631576074)
XLA Ops:
  7.2 1.2 copy.12
  8.3 4.0 %collective-permute-start.1 = (bf16[256,576]{1,0:T(8,128)(2,1)S(1)}, bf16[256,576]{1,0:T(8,128)(2,1)S(1)}, u32[]{:S(2)}, u32[]{:S(2)}) collective-permute-start(bf16[256,576]{1,0:T(8,128)(2,1)S(1)} %copy.12), channel_id=1, source_target_pairs={{0,4},{4,8},{8,12},{12,16},{16,20},{20,24},{24,28},{28,32},{32,36}... | collective-permute-start | bytes 884744 | tf_op jit(solution)/shard_map/ppermute | solution.py:19
  12.4 3.5 %collective-permute-start = (bf16[256,576]{1,0:T(8,128)(2,1)S(1)}, bf16[256,576]{1,0:T(8,128)(2,1)S(1)}, u32[]{:S(2)}, u32[]{:S(2)}) collective-permute-start(bf16[256,576]{1,0:T(8,128)(2,1)S(1)} %copy.12), channel_id=1, source_target_pairs={{0,8},{4,12},{8,16},{12,20},{16,24},{20,28},{24,32},{28,36},{32,40... | collective-permute-start | bytes 884744 | tf_op jit(solution)/shard_map/ppermute | solution.py:19
  16.0 1.4 fusion.12
  19.3 0.9 fusion.11
  20.2 0.3 fusion.2
  20.5 10.8 %prepare.1 = (bf16[16,576,256]{2,1,0:T(8,128)(2,1)}, bf16[16,512,256]{2,1,0:T(8,128)(2,1)}, bf16[16,128,256]{2,1,0:T(8,128)(2,1)}, bf16[16,128,256]{2,1,0:T(8,128)(2,1)}) custom-call(bf16[256,3072]{1,0:T(8,128)(2,1)} %query_ref.1, bf16[256,2048]{1,0:T(8,128)(2,1)} %dout_ref.1, bf16[16,128,512]{2,1,0:T(8,128)(2,1)} %wuk_ref.3, bf16[16,128,512]{2,1,0:T(8,128)(2,1)} %wuv_ref.3), custom_call_target="tpu_custom_call" | custom-call | flops 1073741824 | bytes 16777216 | tf_op jit(solution)/shard_map/prepare/pallas_call | solution.py:55
  31.3 0.9 pad_maximum_fusion.2.bias_ref
  32.3 0.0 collective-permute-done.1
  32.3 0.0 collective-permute-done
  32.3 1.1 pad_maximum_fusion.1.keys_ref
  33.4 58.9 %attend.1 = (bf16[256,2048]{1,0:T(8,128)(2,1)}, bf16[256,3072]{1,0:T(8,128)(2,1)}, bf16[16,128,512]{2,1,0:T(8,128)(2,1)}, bf16[16,128,512]{2,1,0:T(8,128)(2,1)}, f32[576,768]{1,0:T(8,128)}) custom-call(bf16[768,576]{1,0:T(8,128)(2,1)} %pad_maximum_fusion.1.keys_ref, f32[768,256]{1,0:T(8,128)} %pad_maximum_fusion.2.bias_ref, ...), custom_call_target="tpu_custom_call" | custom-call | flops 22682796032 | bytes 31457280 | tf_op jit(solution)/shard_map/attend/pallas_call | solution.py:135
  92.2 2.5 pad_maximum_fusion
  94.7 56.5 %all_to_all.10 = bf16[32,128,512]{2,1,0:T(8,128)(2,1)} all-to-all(bf16[32,128,512]{2,1,0:T(8,128)(2,1)S(1)} %bitcast.8), channel_id=1, replica_groups=mesh['ctx'=32,'head'=4] {'ctx'}, dimensions={0} | all-to-all | bytes 8388608 | tf_op jit(solution)/shard_map/all_to_all | solution.py:176
  151.3 2.8 reduce_sum.12
  154.1 2.5 broadcast_in_dim.16
  156.6 0.0 copy-start
  156.6 6.1 %all-to-all-start.1 = ((bf16[32,128,512]{2,1,0:T(8,128)(2,1)}), bf16[32,128,512]{2,1,0:T(8,128)(2,1)}, u32[]{:S(2)}, u32[]{:S(2)}) async-start(bf16[32,128,512]{2,1,0:T(8,128)(2,1)} %broadcast_in_dim.16), calls=%async_computation.1 | async-start | bytes 8388608 | tf_op jit(solution)/shard_map/all_to_all | solution.py:179
  162.7 0.0 all-reduce.2.cloned.1.call-start
  162.7 0.0 copy-done
  162.7 0.1 bitcast_convert_fusion
  162.9 1.3 collective-permute-start.2
  164.2 1.3 collective-permute-start.3
  165.5 48.3 %collective-permute-done.2 = bf16[256,576]{0,1:T(8,128)(2,1)S(1)} collective-permute-done((bf16[256,576]{0,1:T(8,128)(2,1)S(1)}, bf16[256,576]{0,1:T(8,128)(2,1)S(1)}, u32[]{:S(2)}, u32[]{:S(2)}) %collective-permute-start.2) | collective-permute-done | bytes 294944 | tf_op jit(solution)/shard_map/ppermute | solution.py:19
  213.8 4.6 %collective-permute-done.3 = bf16[256,576]{0,1:T(8,128)(2,1)S(1)} collective-permute-done((bf16[256,576]{0,1:T(8,128)(2,1)S(1)}, bf16[256,576]{0,1:T(8,128)(2,1)S(1)}, u32[]{:S(2)}, u32[]{:S(2)}) %collective-permute-start.3) | collective-permute-done | bytes 294944 | tf_op jit(solution)/shard_map/ppermute | solution.py:19
  218.4 0.9 slice_add_fusion
  219.3 0.0 all-reduce.2.cloned.1.call-update
  219.4 0.0 all-to-all-done.1
  219.4 6.8 %fusion.9 = (f32[16,128,512]{2,1,0:T(8,128)}, f32[16,128,512]{2,1,0:T(8,128)}) fusion(bf16[32,128,512]{2,1,0:T(8,128)(2,1)} %all-to-all-done.1), kind=kLoop, calls=%fused_computation.19 | loop fusion | bytes 16777216 | tf_op jit(solution)/shard_map/slice | solution.py:221
  226.1 46.2 %all-reduce.2.cloned.1.call-done = f32[256,576]{0,1:T(8,128)} async-done(((f32[256,576]{0,1:T(8,128)}), f32[256,576]{0,1:T(8,128)}) %all-reduce.2.cloned.1.call-update) | async-done | bytes 589840 | tf_op jit(solution)/shard_map/psum | solution.py:217
  272.3 1.9 copy.16
  (2 shorter events, 0.0 us)
Async XLA Ops:
  8.3 24.0 %collective-permute-start.1 = (bf16[256,576]{1,0:T(8,128)(2,1)S(1)}, bf16[256,576]{1,0:T(8,128)(2,1)S(1)}, u32[]{:S(2)}, u32[]{:S(2)}) collective-permute-start(bf16[256,576]{1,0:T(8,128)(2,1)S(1)} %copy.12), channel_id=1, source_target_pairs={{0,4},{4,8},{8,12},{12,16},{16,20},{20,24},{24,28},{28,32},{32,36}... | collective-permute-start | bytes 884744 | tf_op jit(solution)/shard_map/ppermute | solution.py:19
  12.4 19.9 %collective-permute-start = (bf16[256,576]{1,0:T(8,128)(2,1)S(1)}, bf16[256,576]{1,0:T(8,128)(2,1)S(1)}, u32[]{:S(2)}, u32[]{:S(2)}) collective-permute-start(bf16[256,576]{1,0:T(8,128)(2,1)S(1)} %copy.12), channel_id=1, source_target_pairs={{0,8},{4,12},{8,16},{12,20},{16,24},{20,28},{24,32},{28,36},{32,40... | collective-permute-start | bytes 884744 | tf_op jit(solution)/shard_map/ppermute | solution.py:19
  156.6 6.1 %copy-start = (f32[576,768]{1,0:T(8,128)S(1)}, f32[576,768]{1,0:T(8,128)}, u32[]{:S(2)}) copy-start(f32[576,768]{1,0:T(8,128)} %get-tuple-element.20) | copy-start | bytes 5308420
  156.6 62.8 %all-to-all-start.1 = ((bf16[32,128,512]{2,1,0:T(8,128)(2,1)}), bf16[32,128,512]{2,1,0:T(8,128)(2,1)}, u32[]{:S(2)}, u32[]{:S(2)}) async-start(bf16[32,128,512]{2,1,0:T(8,128)(2,1)} %broadcast_in_dim.16), calls=%async_computation.1 | async-start | bytes 8388608 | tf_op jit(solution)/shard_map/all_to_all | solution.py:179
  162.7 109.7 %all-reduce.2.cloned.1.call-start = ((), (), s32[]{:S(2)}) async-start(), calls=%async_computation.2 | async-start | bytes 1179648 | tf_op jit(solution)/shard_map/psum | solution.py:217
  162.9 50.9 %collective-permute-start.2 = (bf16[256,576]{0,1:T(8,128)(2,1)S(1)}, bf16[256,576]{0,1:T(8,128)(2,1)S(1)}, u32[]{:S(2)}, u32[]{:S(2)}) collective-permute-start(bf16[256,576]{0,1:T(8,128)(2,1)S(1)} %get-tuple-element.25), channel_id=1, source_target_pairs={{8,0},{12,4},{16,8},{20,12},{24,16},{28,20},{32,24},{36,28},{40,32... | collective-permute-start | bytes 884744 | tf_op jit(solution)/shard_map/ppermute | solution.py:19
  164.2 54.3 %collective-permute-start.3 = (bf16[256,576]{0,1:T(8,128)(2,1)S(1)}, bf16[256,576]{0,1:T(8,128)(2,1)S(1)}, u32[]{:S(2)}, u32[]{:S(2)}) collective-permute-start(bf16[256,576]{0,1:T(8,128)(2,1)S(1)} %get-tuple-element.26), channel_id=1, source_target_pairs={{4,0},{8,4},{12,8},{16,12},{20,16},{24,20},{28,24},{32,28},{36,32}... | collective-permute-start | bytes 884744 | tf_op jit(solution)/shard_map/ppermute | solution.py:19
Sparse Core Ops, SparseCore 0:
  219.5 52.7 all-reduce.1

commit v2 on v1

v2 whole, which is shorter than its diff:
```python
import functools
import math

import jax
import jax.numpy as jnp
from jax import lax
from jax.experimental import pallas as pl
from jax.experimental.pallas import tpu as pltpu
from jax.sharding import PartitionSpec as P

SPAN = 2
CHUNKS = 2
GROUP = 4
LOG2E = 1.4426950408889634
MIB = 2**20
LARGE = 56 * MIB
BRIEF = pl.CostEstimate(flops=2**20, bytes_accessed=2**20, transcendentals=0)


def shifted(block, axis, distance):
    devices = range(lax.axis_size(axis))
    route = [(i - distance, i) for i in devices if i - distance in devices]
    return lax.ppermute(block, axis, route)


def dot(a, b):
    return lax.dot_general(a, b, (((1,), (0,)), ((), ())), preferred_element_type=jnp.float32)


def dot_nt(a, b):
    return lax.dot_general(a, b, (((1,), (1,)), ((), ())), preferred_element_type=jnp.float32)


def prepare_kernel(query_ref, dout_ref, wuk_ref, wuv_ref, qfull_ref, dlo_ref, dout_t_ref, nope_t_ref):
    nope = wuk_ref.shape[1]
    value = wuv_ref.shape[1]
    width = query_ref.shape[1] // wuk_ref.shape[0]
    rank = wuk_ref.shape[2]
    query_t = query_ref[...].T
    dout_t = dout_ref[...].T
    for n in range(wuk_ref.shape[0]):
        q_nope = query_t[n * width : n * width + nope]
        grads = dout_t[n * value : (n + 1) * value]
        nope_t_ref[n] = q_nope
        dout_t_ref[n] = grads
        qfull_ref[n, :rank] = dot(wuk_ref[n].T, q_nope).astype(jnp.bfloat16)
        qfull_ref[n, rank:] = query_t[n * width + nope : (n + 1) * width]
        dlo_ref[n] = dot(wuv_ref[n].T, grads).astype(jnp.bfloat16)


def prepare(query, d_out, w_uk, w_uv):
    toks = query.shape[0]
    heads, nope, rank = w_uk.shape
    value = w_uv.shape[1]
    width = query.shape[1] // heads
    lat = rank + width - nope
    shape = lambda rows: jax.ShapeDtypeStruct((heads, rows, toks), jnp.bfloat16)
    block = lambda rows: pl.BlockSpec((GROUP, rows, toks), lambda s: (s, 0, 0))
    return pl.pallas_call(
        prepare_kernel,
        grid=(heads // GROUP,),
        in_specs=[
            pl.BlockSpec((toks, GROUP * width), lambda s: (0, s)),
            pl.BlockSpec((toks, GROUP * value), lambda s: (0, s)),
            pl.BlockSpec((GROUP, nope, rank), lambda s: (s, 0, 0)),
            pl.BlockSpec((GROUP, value, rank), lambda s: (s, 0, 0)),
        ],
        out_specs=[block(lat), block(rank), block(value), block(nope)],
        out_shape=[shape(lat), shape(rank), shape(value), shape(nope)],
        compiler_params=pltpu.CompilerParams(vmem_limit_bytes=LARGE),
        cost_estimate=pl.CostEstimate(
            flops=4 * heads * toks * nope * rank, bytes_accessed=16 * 2**20, transcendentals=0
        ),
        name="prepare",
    )(query, d_out, w_uk, w_uv)


def score_kernel(
    inv_root,
    block_refs,
    bias_ref,
    qfull_ref,
    dlo_ref,
    dout_t_ref,
    nope_t_ref,
    *rest,
):
    probs_ref, dscore_ref, lout_ref, dfull_ref, grad_ref, keys_ref, keys_t_ref = rest[-7:]
    rank = dlo_ref.shape[1]
    nope = nope_t_ref.shape[1]
    group = range(qfull_ref.shape[0])

    @pl.when(pl.program_id(0) == 0)
    def _():
        for n, block_ref in enumerate(block_refs):
            toks = block_ref.shape[1]
            keys_t_ref[:, n * toks : (n + 1) * toks] = block_ref[...]
            keys_ref[n * toks : (n + 1) * toks] = block_ref[...].T

    scores = [dot(keys_ref[...], qfull_ref[n]) for n in group]
    probs = []
    for n in group:
        scaled = scores[n] * (inv_root * LOG2E) + bias_ref[...]
        weights = jnp.exp2(scaled - jnp.max(scaled, axis=0, keepdims=True))
        probs.append(weights * (1.0 / jnp.sum(weights, axis=0, keepdims=True)))
        probs_ref[n] = probs[n].astype(jnp.bfloat16)
    d_probs = [dot(keys_ref[:, :rank], dlo_ref[n]) for n in group]
    for n in group:
        lout_ref[n] = dot(keys_t_ref[:rank], probs_ref[n]).astype(jnp.bfloat16)
    for n in group:
        delta = jnp.sum(probs[n] * d_probs[n], axis=0, keepdims=True)
        dscore_ref[n] = (probs[n] * (d_probs[n] - delta) * inv_root).astype(jnp.bfloat16)
    for n in group:
        grad_ref[n, nope:] = dot_nt(dout_t_ref[n], lout_ref[n]).astype(jnp.bfloat16)
    for n in group:
        dfull_ref[n] = dot(keys_t_ref[...], dscore_ref[n]).astype(jnp.bfloat16)
    for n in group:
        grad_ref[n, :nope] = dot_nt(nope_t_ref[n], dfull_ref[n, :rank]).astype(jnp.bfloat16)


def score(blocks, bias, qfull, dlo, dout_t, nope_t, inv_root, start, count, carried, after):
    heads, lat, toks = qfull.shape
    span = bias.shape[0]
    rank = dlo.shape[1]
    value, nope = dout_t.shape[1], nope_t.shape[1]
    base = start // GROUP
    whole = lambda rows, cols: pl.BlockSpec((rows, cols), lambda s: (0, 0))
    heads_of = lambda rows: pl.BlockSpec((GROUP, rows, toks), lambda s: (s + base, 0, 0))
    out = lambda rows: jax.ShapeDtypeStruct((heads, rows, toks), jnp.bfloat16)
    return pl.pallas_call(
        functools.partial(score_kernel, inv_root),
        grid=(count // GROUP,),
        in_specs=[
            [whole(lat, toks)] * len(blocks),
            whole(span, toks),
            heads_of(lat),
            heads_of(rank),
            heads_of(value),
            heads_of(nope),
        ]
        + [pl.BlockSpec(memory_space=pl.ANY)] * (len(carried) + len(after)),
        out_specs=[
            heads_of(span),
            heads_of(span),
            heads_of(rank),
            heads_of(lat),
            pl.BlockSpec((GROUP, nope + value, rank), lambda s: (s, 0, 0)),
        ],
        out_shape=[
            out(span),
            out(span),
            out(rank),
            out(lat),
            jax.ShapeDtypeStruct((count, nope + value, rank), jnp.bfloat16),
        ],
        input_output_aliases={5 + len(blocks) + n: n for n in range(len(carried))},
        scratch_shapes=[pltpu.VMEM((span, lat), jnp.bfloat16), pltpu.VMEM((lat, span), jnp.bfloat16)],
        compiler_params=pltpu.CompilerParams(vmem_limit_bytes=LARGE),
        cost_estimate=pl.CostEstimate(
            flops=8 * count * toks * span * (rank + lat),
            bytes_accessed=3 * count * 2**20,
            transcendentals=count * toks * span,
        ),
        name="score",
    )(blocks, bias, qfull, dlo, dout_t, nope_t, *carried, *after)


def key_kernel(last, core_ref, qfull_ref, dlo_ref, probs_ref, dscore_ref, *rest):
    total_ref = rest[-1]
    rank = dlo_ref.shape[1]
    step = pl.program_id(0)

    @pl.when(step == 0)
    def _():
        total_ref[...] = rest[0][...] if last else jnp.zeros_like(total_ref)

    content = 0.0
    rope = 0.0
    for n in range(qfull_ref.shape[0]):
        content += dot_nt(qfull_ref[n, :rank], dscore_ref[n]) + dot_nt(dlo_ref[n], probs_ref[n])
        rope += dot_nt(qfull_ref[n, rank:], dscore_ref[n])
    total_ref[:rank] += content
    total_ref[rank:] += rope

    if last:
        keep_ref, send_ref = rest[-3:-1]
        rows = keep_ref.shape[0]

        @pl.when(step == pl.num_programs(0) - 1)
        def _():
            keep_ref[...] = total_ref[pl.ds(pl.multiple_of(core_ref[0] * rows, rows), rows)]
            send_ref[...] = total_ref[pl.ds(pl.multiple_of((1 - core_ref[0]) * rows, rows), rows)]


def key_gradient(core, qfull, dlo, probs, dscore, start, count, last, carried, after):
    lat, toks = qfull.shape[1:]
    rank = dlo.shape[1]
    span = probs.shape[1]
    base = start // GROUP
    heads_of = lambda rows: pl.BlockSpec((GROUP, rows, toks), lambda s: (s + base, 0, 0))
    whole = lambda rows: pl.BlockSpec((rows, span), lambda s: (0, 0))
    out = lambda rows: jax.ShapeDtypeStruct((rows, span), jnp.float32)
    outputs = [lat // 2, lat // 2] if last else [lat]
    return pl.pallas_call(
        functools.partial(key_kernel, last),
        grid=(count // GROUP,),
        in_specs=[pl.BlockSpec(memory_space=pltpu.SMEM)]
        + [heads_of(lat), heads_of(rank), heads_of(span), heads_of(span)]
        + [whole(lat)] * len(carried)
        + [pl.BlockSpec(memory_space=pl.ANY)] * len(after),
        out_specs=[whole(rows) for rows in outputs],
        out_shape=[out(rows) for rows in outputs],
        scratch_shapes=[pltpu.VMEM((lat, span), jnp.float32)] if last else [],
        compiler_params=pltpu.CompilerParams(vmem_limit_bytes=LARGE),
        cost_estimate=BRIEF,
        name="key_gradient",
    )(core, qfull, dlo, probs, dscore, *carried, *after)


def split_kernel(keep_ref, got_ref, own_ref, *part_refs):
    toks = own_ref.shape[1]
    for part, part_ref in enumerate(part_refs):
        span = slice(part * toks, (part + 1) * toks)
        total = keep_ref[:, span] + got_ref[:, span]
        part_ref[...] = total.astype(part_ref.dtype)
        if part == len(part_refs) - 1:
            own_ref[...] = total


def split(keep, got, toks):
    rows, span = keep.shape
    out = lambda dtype: jax.ShapeDtypeStruct((rows, toks), dtype)
    return pl.pallas_call(
        split_kernel,
        out_shape=[out(jnp.float32)] + [out(jnp.bfloat16)] * (span // toks),
        compiler_params=pltpu.CompilerParams(vmem_limit_bytes=12 * MIB),
        cost_estimate=BRIEF,
        name="split",
    )(keep, got)


def merge_kernel(own_ref, *rest):
    total = own_ref[...]
    for part_ref in rest[:-2]:
        total += part_ref[...].astype(jnp.float32)
    rest[-1][...] = total


def merge(own, parts, after):
    whole = pl.BlockSpec(memory_space=pltpu.VMEM)
    return pl.pallas_call(
        merge_kernel,
        in_specs=[whole] * (1 + len(parts)) + [pl.BlockSpec(memory_space=pl.ANY)],
        out_specs=whole,
        out_shape=jax.ShapeDtypeStruct(own.shape, own.dtype),
        compiler_params=pltpu.CompilerParams(vmem_limit_bytes=12 * MIB),
        cost_estimate=BRIEF,
        name="merge",
    )(own, *parts, after)


def assemble_kernel(core_ref, mine_ref, other_ref, out_ref):
    rows = mine_ref.shape[0]
    core = core_ref[0]
    out_ref[pl.ds(pl.multiple_of(core * rows, rows), rows)] = mine_ref[...]
    out_ref[pl.ds(pl.multiple_of((1 - core) * rows, rows), rows)] = other_ref[...]


def assemble(core, mine, other):
    rows, toks = mine.shape
    whole = pl.BlockSpec(memory_space=pltpu.VMEM)
    return pl.pallas_call(
        assemble_kernel,
        in_specs=[pl.BlockSpec(memory_space=pltpu.SMEM), whole, whole],
        out_specs=whole,
        out_shape=jax.ShapeDtypeStruct((2 * rows, toks), jnp.float32),
        compiler_params=pltpu.CompilerParams(vmem_limit_bytes=12 * MIB),
        cost_estimate=BRIEF,
        name="assemble",
    )(core, mine, other)


def project_kernel(lout_ref, dfull_ref, wuk_ref, wuv_ref, att_ref, dq_ref):
    group = range(lout_ref.shape[0])
    rank = lout_ref.shape[1]
    value = wuv_ref.shape[1]
    width = dq_ref.shape[1] // len(group)
    for n in group:
        attended = dot(wuv_ref[n], lout_ref[n]).astype(jnp.bfloat16)
        att_ref[:, n * value : (n + 1) * value] = attended.T
        d_nope = dot(wuk_ref[n], dfull_ref[n, :rank]).astype(jnp.bfloat16)
        dq_ref[:, n * width : (n + 1) * width] = jnp.concatenate([d_nope, dfull_ref[n, rank:]], axis=0).T


def project(lout, dfull, w_uk, w_uv):
    heads, lat, toks = dfull.shape
    nope, rank = w_uk.shape[1:]
    value = w_uv.shape[1]
    width = nope + lat - rank
    heads_of = lambda rows, cols: pl.BlockSpec((GROUP, rows, cols), lambda s: (s, 0, 0))
    out = lambda cols: jax.ShapeDtypeStruct((toks, heads * cols), jnp.bfloat16)
    return pl.pallas_call(
        project_kernel,
        grid=(heads // GROUP,),
        in_specs=[heads_of(rank, toks), heads_of(lat, toks), heads_of(nope, rank), heads_of(value, rank)],
        out_specs=[
            pl.BlockSpec((toks, GROUP * value), lambda s: (0, s)),
            pl.BlockSpec((toks, GROUP * width), lambda s: (0, s)),
        ],
        out_shape=[out(value), out(width)],
        compiler_params=pltpu.CompilerParams(vmem_limit_bytes=LARGE),
        cost_estimate=BRIEF,
        name="project",
    )(lout, dfull, w_uk, w_uv)


def add_kernel(*refs):
    *piece_refs, _, _, out_ref = refs
    for chunk, piece_ref in enumerate(piece_refs):
        total = jnp.sum(piece_ref[...].astype(jnp.float32), axis=0).astype(out_ref.dtype)
        out_ref[:, chunk] = jnp.broadcast_to(total[None], piece_ref.shape)


def add_pieces(pieces, after):
    parts, rows, cols = pieces[0].shape
    tall = 16
    return pl.pallas_call(
        add_kernel,
        grid=(rows // tall,),
        in_specs=[pl.BlockSpec((parts, tall, cols), lambda s: (0, s, 0))] * len(pieces)
        + [pl.BlockSpec(memory_space=pl.ANY)] * len(after),
        out_specs=pl.BlockSpec((parts, len(pieces), tall, cols), lambda s: (0, 0, s, 0)),
        out_shape=jax.ShapeDtypeStruct((parts, len(pieces), rows, cols), jnp.bfloat16),
        compiler_params=pltpu.CompilerParams(vmem_limit_bytes=14 * MIB),
        cost_estimate=pl.CostEstimate(flops=2**21, bytes_accessed=8 * 2**20, transcendentals=0),
        name="add_pieces",
    )(*pieces, *after)


def widen_kernel(sums_ref, uk_ref, uv_ref):
    uk_ref[...] = sums_ref[:, 0, :, 0].astype(jnp.float32)
    uv_ref[...] = sums_ref[:, 1, :, 0].astype(jnp.float32)


def widen(sums, heads):
    parts, chunks, rows, cols = sums.shape
    per_chunk = heads // chunks
    half = parts // per_chunk // 2
    view = sums.reshape(per_chunk, 2, half, chunks, rows, cols)
    step = 2
    out = jax.ShapeDtypeStruct((heads, half, rows, cols), jnp.float32)
    place = lambda c, s: (c * (per_chunk // step) + s, 0, 0, 0)
    uk, uv = pl.pallas_call(
        widen_kernel,
        grid=(chunks, per_chunk // step),
        in_specs=[pl.BlockSpec((step, 2, half, 1, rows, cols), lambda c, s: (s, 0, 0, c, 0, 0))],
        out_specs=[pl.BlockSpec((step, half, rows, cols), place)] * 2,
        out_shape=[out, out],
        compiler_params=pltpu.CompilerParams(vmem_limit_bytes=14 * MIB),
        cost_estimate=pl.CostEstimate(flops=2**21, bytes_accessed=12 * 2**20, transcendentals=0),
        name="widen",
    )(view)
    return uk.reshape(heads, half * rows, cols), uv.reshape(heads, half * rows, cols)


def scattered(grads):
    parts = lax.axis_size("ctx")
    return lax.all_to_all(grads.reshape(parts, -1, grads.shape[-1]), "ctx", 0, 0, tiled=True)


def swap_core(block):
    return lax.ppermute(block, "head", [(0, 1), (1, 0), (2, 3), (3, 2)])


def returned(block, distance, across):
    blocks, heads = lax.axis_size("ctx"), lax.axis_size("head")
    route = [
        (c * heads + h, (c - distance) * heads + (h ^ 2 if across else h))
        for c in range(distance, blocks)
        for h in range(heads)
    ]
    return lax.ppermute(block, ("ctx", "head"), route)


def latent_gradient(core, keep, send, toks, after):
    own, *parts = split(keep, swap_core(send), toks)
    arrived = [returned(parts[SPAN], 0, True)]
    for distance in range(1, SPAN + 1):
        for across in (False, True):
            arrived.append(returned(parts[SPAN - distance], distance, across))
    mine = merge(own, arrived, after)
    return assemble(core, mine, swap_core(mine))


def body(latent, query, d_out, w_uk, w_uv, block_mask, segments):
    toks, lat = latent.shape
    heads, nope, rank = w_uk.shape
    width = query.shape[1] // heads
    inv_root = 1.0 / math.sqrt(width)
    position = lax.axis_index("ctx")
    latent_t = latent.T
    blocks = [shifted(latent_t, "ctx", distance) for distance in (2, 1)] + [latent_t]
    qfull, dlo, dout_t, nope_t = prepare(query, d_out, w_uk, w_uv)

    offsets = jnp.arange(toks, dtype=jnp.int32)
    seg_query = lax.dynamic_slice_in_dim(segments, position * toks, toks)
    bias = []
    for distance in (2, 1, 0):
        block = position - distance
        clamped = jnp.maximum(block, 0)
        seg_key = lax.dynamic_slice_in_dim(segments, clamped * toks, toks)
        granted = block_mask[position, clamped]
        allowed = (
            (block >= 0)
            & (offsets[:, None] - distance * toks <= offsets[None, :])
            & ((seg_key[:, None] == seg_query[None, :]) | (granted == 1))
        )
        bias.append(jnp.where(allowed, 0.0, -jnp.inf).astype(jnp.float32))
    bias = jnp.concatenate(bias, axis=0)
    core = (lax.axis_index("head") % 2).astype(jnp.int32).reshape(1)
    carried = []
    pieces = []
    dlat_t = []
    count = heads // CHUNKS
    for start in range(0, heads, count):
        *carried, grads = score(
            blocks, bias, qfull, dlo, dout_t, nope_t, inv_root, start, count, carried, dlat_t
        )
        pieces.append(scattered(grads))
        probs, dscore, lout, dfull = carried
        last = start + count == heads
        dlat_t = key_gradient(core, qfull, dlo, probs, dscore, start, count, last, dlat_t, pieces[:-1])
    attended, d_query = project(lout, dfull, w_uk, w_uv)
    d_latent_t = latent_gradient(core, *dlat_t, toks, attended)
    sums = add_pieces(pieces, (d_latent_t, attended))
    sums = lax.all_to_all(sums, "ctx", 0, 0, tiled=True)
    d_w_uk, d_w_uv = widen(sums, heads)
    return attended, d_query, d_latent_t.T, d_w_uk, d_w_uv


def solution(mesh):
    in_specs = (
        P("ctx", None),
        P("ctx", "head"),
        P("ctx", "head"),
        P("head", None, None),
        P("head", None, None),
        P(),
        P(),
    )
    out_specs = (
        P("ctx", "head"),
        P("ctx", "head"),
        P("ctx", None),
        P("head", None, None),
        P("head", None, None),
    )
    return jax.shard_map(body, mesh=mesh, in_specs=in_specs, out_specs=out_specs, check_vma=False)
```

time: 282 us -> 195 us (0.69)
  waiting for transfers between devices: 99.2 us -> 17.8 us
  starting transfers between devices: 16.3 us -> 34.1 us
  between operations: 16.1 us -> 2.75 us
  local copies, waits for them, and re-layouts: 14.7 us -> 6.58 us
  other arithmetic: 8.54 us -> 1.21 us
  Pallas kernels: 69.7 us -> 73.7 us
    ppermute x4 -> x2, waiting for transfers between devices: 53 us -> 0.01 us  [shifted(): return lax.ppermute(block, axis, route)]
    psum x1 -> x0, waiting for transfers between devices: 46.2 us -> none  [body(): d_latent = lax.psum(own, 'head')]
    ppermute x0 -> x7, waiting for transfers between devices: none -> 16 us  [the longest x5 12.6 us: returned(): return lax.ppermute(block, ('ctx', 'head'), route)]
    all_to_all x1 -> x2, starting transfers between devices: 6.08 us -> 16.3 us  [scattered(): lax.all_to_all(grads.reshape(parts, -1, grads.shape[-1]), 'ctx', 0, 0, ti...]
    ppermute x0 -> x7, starting transfers between devices: none -> 10.1 us  [the longest x5 7.87 us: returned(): return lax.ppermute(block, ('ctx', 'head'), route)]
    slice x2 -> x0, local copies, waits for them, and re-layouts: 6.8 us -> none  [the longest x1 6.76 us: body(): d_w_uv = grads[heads * nope:].reshape(w_uv.shape)]
    pallas_call x2 -> x11, Pallas kernels: 69.7 us -> 73.7 us  [the longest x2 31.6 us: score(): pl.pallas_call(functools.partial(score_kernel, inv_root), grid=(count //...]
    concatenate x2 -> x0, other arithmetic: 3.54 us -> none  [the longest x1 2.49 us: body(): jnp.concatenate([guk.reshape(heads * nope, rank), guv.reshape(heads * val...]
  transfers between devices with their start and end apart: 6 -> 11, of which waited for: 3 -> 6; matrix products, arithmetic and copies ran while one was open for 4% -> 2% of each run, Pallas kernels for 4% -> 26%
where the time goes in v2:
time: 195 us; the launch traced here: 193 us
  Pallas kernels  73.7 us (38%)
  blocking collectives  57 us (29%)
  starting transfers between devices  34.1 us (17%)
  waiting for transfers between devices  17.8 us (9%)
  local copies, waits for them, and re-layouts  6.58 us (3%)
  between operations  2.75 us (1%)
    all_to_all x1, blocking collectives, body(): sums = lax.all_to_all(sums, 'ctx', 0, 0, tiled=True)  57 us
    pallas_call x2, Pallas kernels, score(): pl.pallas_call(functools.partial(score_kernel, inv_root), grid=(count //...  31.6 us
    pallas_call x2, Pallas kernels, key_gradient(): pl.pallas_call(functools.partial(key_kernel, last), grid=(count // GROUP,...  17.9 us
    all_to_all x2, starting transfers between devices, scattered(): lax.all_to_all(grads.reshape(parts, -1, grads.shape[-1]), 'ctx', 0, 0, ti...  16.3 us
    ppermute x5, waiting for transfers between devices, returned(): return lax.ppermute(block, ('ctx', 'head'), route)  12.6 us
    pallas_call x1, Pallas kernels, prepare(): pl.pallas_call(prepare_kernel, grid=(heads // GROUP,), in_specs=[pl.Block...  8.31 us
    ppermute x5, starting transfers between devices, returned(): return lax.ppermute(block, ('ctx', 'head'), route)  7.87 us
    ppermute x2, starting transfers between devices, shifted(): return lax.ppermute(block, axis, route)  7.6 us
  transfers between devices with their start and end apart: 11, of which 6 were waited for; matrix products, arithmetic and copies ran while one was open for 2% of the time, Pallas kernels for 26%

profile of v2, /device:TPU:1, one launch (start us, length us, event | category | flops | bytes accessed | tf_op | source)
XLA Modules:
  0.0 193.1 jit_solution(6475529540155562577)
XLA Ops:
  0.6 4.0 %collective-permute-start.1 = (bf16[576,256]{1,0:T(8,128)(2,1)}, bf16[576,256]{1,0:T(8,128)(2,1)S(1)}, u32[]{:S(2)}, u32[]{:S(2)}) collective-permute-start(bf16[576,256]{1,0:T(8,128)(2,1)} %bitcast.17), channel_id=1, source_target_pairs={{0,4},{4,8},{8,12},{12,16},{16,20},{20,24},{24,28},{28,32},{32,36}... | collective-permute-start | bytes 884744 | tf_op jit(solution)/shard_map/ppermute | solution.py:23
  4.7 3.5 %collective-permute-start = (bf16[576,256]{1,0:T(8,128)(2,1)}, bf16[576,256]{1,0:T(8,128)(2,1)S(1)}, u32[]{:S(2)}, u32[]{:S(2)}) collective-permute-start(bf16[576,256]{1,0:T(8,128)(2,1)} %bitcast.18), channel_id=1, source_target_pairs={{0,8},{4,12},{8,16},{12,20},{16,24},{20,28},{24,32},{28,36},{32,40... | collective-permute-start | bytes 884744 | tf_op jit(solution)/shard_map/ppermute | solution.py:23
  8.3 1.4 fusion.10
  11.6 0.9 fusion.9
  12.8 8.3 %prepare.1 = (bf16[16,576,256]{2,1,0:T(8,128)(2,1)}, bf16[16,512,256]{2,1,0:T(8,128)(2,1)}, bf16[16,128,256]{2,1,0:T(8,128)(2,1)}, bf16[16,128,256]{2,1,0:T(8,128)(2,1)}) custom-call(bf16[256,3072]{1,0:T(8,128)(2,1)} %query_ref.1, bf16[256,2048]{1,0:T(8,128)(2,1)} %dout_ref.1, bf16[16,128,512]{2,1,0:T(8,128)(2,1)} %wuk_ref.3, bf16[16,128,512]{2,1,0:T(8,128)(2,1)} %wuv_ref.3), custom_call_target="tpu_custom_call" | custom-call | flops 1073741824 | bytes 16777216 | tf_op jit(solution)/shard_map/prepare/pallas_call | solution.py:59
  21.1 0.9 pad_maximum_fusion.bias_ref
  22.9 15.6 %score.2 = (bf16[16,768,256]{2,1,0:T(8,128)(2,1)}, bf16[16,768,256]{2,1,0:T(8,128)(2,1)}, bf16[16,512,256]{2,1,0:T(8,128)(2,1)}, bf16[16,576,256]{2,1,0:T(8,128)(2,1)}, bf16[8,256,512]{2,1,0:T(8,128)(2,1)}) custom-call(bf16[576,256]{1,0:T(8,128)(2,1)} %copy-done.7, bf16[576,256]{1,0:T(8,128)(2,1)} %copy-done.6, bf16[576,256]{1,0:T(8,128)(2,1)} %bitcast.19, ...), custom_call_target="tpu_custom_call" | custom-call | flops 13690208256 | bytes 25165824 | tf_op jit(solution)/shard_map/score/pallas_call | solution.py:130
  38.5 7.5 %all-to-all-start = ((bf16[32,64,512]{2,1,0:T(8,128)(2,1)}), bf16[32,64,512]{2,1,0:T(8,128)(2,1)S(1)}, u32[]{:S(2)}, u32[]{:S(2)}) async-start(bf16[32,64,512]{2,1,0:T(8,128)(2,1)} %bitcast.14), calls=%async_computation | async-start | bytes 4194304 | tf_op jit(solution)/shard_map/all_to_all | solution.py:368
  46.0 8.5 %key_gradient.2.rest_4_.rest_0_ = f32[576,768]{1,0:T(8,128)} custom-call(s32[1]{0:T(128)} %bitcast.4.core_ref, bf16[16,576,256]{2,1,0:T(8,128)(2,1)} %get-tuple-element.29.qfull_ref, bf16[16,512,256]{2,1,0:T(8,128)(2,1)} %get-tuple-element.30.dlo_ref, bf16[16,768,256]{2,1,0:T(8,128)(2,1)} %get-tuple-element.33.probs_ref.rest_0_, ...), custom_call_target="tpu_custom_call" | custom-call | flops 1048576 | bytes 1048576 | tf_op jit(solution)/shard_map/key_gradient/pallas_call | solution.py:204
  54.5 16.0 %score.3 = (bf16[16,768,256]{2,1,0:T(8,128)(2,1)}, bf16[16,768,256]{2,1,0:T(8,128)(2,1)}, bf16[16,512,256]{2,1,0:T(8,128)(2,1)}, bf16[16,576,256]{2,1,0:T(8,128)(2,1)}, bf16[8,256,512]{2,1,0:T(8,128)(2,1)}) custom-call(bf16[576,256]{1,0:T(8,128)(2,1)} %copy-done.7, ...), custom_call_target="tpu_custom_call", output_to_operand_aliasing={{0}: (8, {}), {1}: (9, {}), {2}: (10, {}), {3}: (11, {})} | custom-call | flops 13690208256 | bytes 25165824 | tf_op jit(solution)/shard_map/score/pallas_call | solution.py:130
  70.5 1.7 all-to-all-done.rest_1_.refs_0_
  72.2 8.8 %all-to-all-start.1 = ((bf16[32,64,512]{2,1,0:T(8,128)(2,1)}), bf16[32,64,512]{2,1,0:T(8,128)(2,1)}, u32[]{:S(2)}, u32[]{:S(2)}) async-start(bf16[32,64,512]{2,1,0:T(8,128)(2,1)} %bitcast.13), calls=%async_computation.1 | async-start | bytes 4194304 | tf_op jit(solution)/shard_map/all_to_all | solution.py:368
  81.0 9.4 %key_gradient.3 = (f32[288,768]{1,0:T(8,128)}, f32[288,768]{1,0:T(8,128)}) custom-call(s32[1]{0:T(128)} %bitcast.4.core_ref, bf16[16,576,256]{2,1,0:T(8,128)(2,1)} %get-tuple-element.29.qfull_ref, bf16[16,512,256]{2,1,0:T(8,128)(2,1)} %get-tuple-element.30.dlo_ref, bf16[16,768,256]{2,1,0:T(8,128)(2,1)} %get-tuple-element.41.probs_ref, ...), custom_call_target="tpu_custom_call" | custom-call | flops 1048576 | bytes 1048576 | tf_op jit(solution)/shard_map/key_gradient/pallas_call | solution.py:204
  91.2 2.3 %collective-permute-done.2.got_ref = f32[288,768]{1,0:T(8,128)S(1)} collective-permute-done((f32[288,768]{1,0:T(8,128)}, f32[288,768]{1,0:T(8,128)S(1)}, u32[]{:S(2)}, u32[]{:S(2)}) %collective-permute-start.2) | collective-permute-done | bytes 884768 | tf_op jit(solution)/shard_map/ppermute | solution.py:372
  93.5 1.2 copy-done.5
  94.7 2.7 %collective-permute-start.3 = (bf16[288,256]{1,0:T(8,128)(2,1)S(1)}, bf16[288,256]{1,0:T(8,128)(2,1)S(1)}, u32[]{:S(2)}, u32[]{:S(2)}) collective-permute-start(bf16[288,256]{1,0:T(8,128)(2,1)S(1)} %get-tuple-element.47), channel_id=1, source_target_pairs={{0,2},{1,3},{2,0},{3,1},{4,6},{5,7},{6,4},{7,5},{8,10},{9,11},{10,... | collective-permute-start | bytes 442376 | tf_op jit(solution)/shard_map/ppermute | solution.py:382
  97.4 1.3 collective-permute-start.5
  98.7 1.3 collective-permute-start.4
  100.0 1.3 collective-permute-start.7
  101.3 1.3 collective-permute-start.6
  102.6 7.3 %project.1 = (bf16[256,2048]{1,0:T(8,128)(2,1)}, bf16[256,3072]{1,0:T(8,128)(2,1)}) custom-call(bf16[16,512,256]{2,1,0:T(8,128)(2,1)} %get-tuple-element.37.lout_ref, bf16[16,576,256]{2,1,0:T(8,128)(2,1)} %get-tuple-element.38.dfull_ref, bf16[16,128,512]{2,1,0:T(8,128)(2,1)} %wuk_ref.3, bf16[16,128,512]{2,1,0:T(8,128)(2,1)} %wuv_ref.3), custom_call_target="tpu_custom_call" | custom-call | flops 1048576 | bytes 1048576 | tf_op jit(solution)/shard_map/project/pallas_call | solution.py:302
  109.9 2.1 %collective-permute-done.3.rest_0_ = bf16[288,256]{1,0:T(8,128)(2,1)S(1)} collective-permute-done((bf16[288,256]{1,0:T(8,128)(2,1)S(1)}, bf16[288,256]{1,0:T(8,128)(2,1)S(1)}, u32[]{:S(2)}, u32[]{:S(2)}) %collective-permute-start.3) | collective-permute-done | bytes 147488 | tf_op jit(solution)/shard_map/ppermute | solution.py:382
  112.1 3.2 %collective-permute-done.4.rest_1_ = bf16[288,256]{1,0:T(8,128)(2,1)S(1)} collective-permute-done((bf16[288,256]{1,0:T(8,128)(2,1)S(1)}, bf16[288,256]{1,0:T(8,128)(2,1)S(1)}, u32[]{:S(2)}, u32[]{:S(2)}) %collective-permute-start.4) | collective-permute-done | bytes 147488 | tf_op jit(solution)/shard_map/ppermute | solution.py:382
  115.3 7.2 %collective-permute-done.7.rest_4_ = bf16[288,256]{1,0:T(8,128)(2,1)S(1)} collective-permute-done((bf16[288,256]{1,0:T(8,128)(2,1)S(1)}, bf16[288,256]{1,0:T(8,128)(2,1)S(1)}, u32[]{:S(2)}, u32[]{:S(2)}) %collective-permute-start.7) | collective-permute-done | bytes 147488 | tf_op jit(solution)/shard_map/ppermute | solution.py:382
  122.5 1.2 copy-done.2
  123.8 1.5 collective-permute-start.8
  125.3 1.2 collective-permute-done.8.other_ref
  126.6 0.9 assemble.1.refs_2_
  127.4 1.1 copy-done.4
  128.5 3.1 %add_pieces.1 = bf16[32,2,64,512]{3,2,1,0:T(8,128)(2,1)S(1)} custom-call(bf16[32,64,512]{2,1,0:T(8,128)(2,1)S(1)} %copy-done.1, bf16[32,64,512]{2,1,0:T(8,128)(2,1)} %all-to-all-done.1.refs_1_, f32[576,256]{1,0:T(8,128)S(1)} %copy-done.4, bf16[256,2048]{1,0:T(8,128)(2,1)S(1)} %copy-done.3), custom_call_target="tpu_custom_call" | custom-call | flops 2097152 | bytes 8388608 | tf_op jit(solution)/shard_map/add_pieces/pallas_call | solution.py:327
  131.6 57.0 %all_to_all.15 = bf16[32,2,64,512]{3,2,1,0:T(8,128)(2,1)S(1)} all-to-all(bf16[32,2,64,512]{3,2,1,0:T(8,128)(2,1)S(1)} %add_pieces.1), channel_id=1, replica_groups=mesh['ctx'=32,'head'=4] {'ctx'}, dimensions={0} | all-to-all | bytes 8388608 | tf_op jit(solution)/shard_map/all_to_all | solution.py:436
  188.6 4.5 %widen.1 = (f32[16,2,64,512]{3,2,1,0:T(8,128)}, f32[16,2,64,512]{3,2,1,0:T(8,128)}) custom-call(bf16[8,2,2,2,64,512]{5,4,3,2,1,0:T(8,128)(2,1)S(1)} %bitcast.11), custom_call_target="tpu_custom_call" | custom-call | flops 2097152 | bytes 12582912 | tf_op jit(solution)/shard_map/widen/pallas_call | solution.py:353
  (23 shorter events, 2.1 us)
Async XLA Ops:
  0.6 21.4 %collective-permute-start.1 = (bf16[576,256]{1,0:T(8,128)(2,1)}, bf16[576,256]{1,0:T(8,128)(2,1)S(1)}, u32[]{:S(2)}, u32[]{:S(2)}) collective-permute-start(bf16[576,256]{1,0:T(8,128)(2,1)} %bitcast.17), channel_id=1, source_target_pairs={{0,4},{4,8},{8,12},{12,16},{16,20},{20,24},{24,28},{28,32},{32,36}... | collective-permute-start | bytes 884744 | tf_op jit(solution)/shard_map/ppermute | solution.py:23
  4.7 17.4 %collective-permute-start = (bf16[576,256]{1,0:T(8,128)(2,1)}, bf16[576,256]{1,0:T(8,128)(2,1)S(1)}, u32[]{:S(2)}, u32[]{:S(2)}) collective-permute-start(bf16[576,256]{1,0:T(8,128)(2,1)} %bitcast.18), channel_id=1, source_target_pairs={{0,8},{4,12},{8,16},{12,20},{16,24},{20,28},{24,32},{28,36},{32,40... | collective-permute-start | bytes 884744 | tf_op jit(solution)/shard_map/ppermute | solution.py:23
  22.1 0.7 copy-start.6
  22.1 0.8 copy-start.7
  38.5 33.8 %all-to-all-start = ((bf16[32,64,512]{2,1,0:T(8,128)(2,1)}), bf16[32,64,512]{2,1,0:T(8,128)(2,1)S(1)}, u32[]{:S(2)}, u32[]{:S(2)}) async-start(bf16[32,64,512]{2,1,0:T(8,128)(2,1)} %bitcast.14), calls=%async_computation | async-start | bytes 4194304 | tf_op jit(solution)/shard_map/all_to_all | solution.py:368
  72.2 8.8 %copy-start = (bf16[32,64,512]{2,1,0:T(8,128)(2,1)}, bf16[32,64,512]{2,1,0:T(8,128)(2,1)S(1)}, u32[]{:S(2)}) copy-start(bf16[32,64,512]{2,1,0:T(8,128)(2,1)S(1)} %all-to-all-done.rest_1_.refs_0_) | copy-start | bytes 6291460
  72.2 55.2 %all-to-all-start.1 = ((bf16[32,64,512]{2,1,0:T(8,128)(2,1)}), bf16[32,64,512]{2,1,0:T(8,128)(2,1)}, u32[]{:S(2)}, u32[]{:S(2)}) async-start(bf16[32,64,512]{2,1,0:T(8,128)(2,1)} %bitcast.13), calls=%async_computation.1 | async-start | bytes 4194304 | tf_op jit(solution)/shard_map/all_to_all | solution.py:368
  90.4 3.0 %collective-permute-start.2 = (f32[288,768]{1,0:T(8,128)}, f32[288,768]{1,0:T(8,128)S(1)}, u32[]{:S(2)}, u32[]{:S(2)}) collective-permute-start(f32[288,768]{1,0:T(8,128)} %get-tuple-element.45), channel_id=1, source_target_pairs={{0,1},{1,0},{2,3},{3,2},{4,5},{5,4},{6,7},{7,6},{8,9},{9,8},{10,11... | collective-permute-start | bytes 2654216 | tf_op jit(solution)/shard_map/ppermute | solution.py:372
  93.5 1.2 copy-start.5
  94.7 17.3 %collective-permute-start.3 = (bf16[288,256]{1,0:T(8,128)(2,1)S(1)}, bf16[288,256]{1,0:T(8,128)(2,1)S(1)}, u32[]{:S(2)}, u32[]{:S(2)}) collective-permute-start(bf16[288,256]{1,0:T(8,128)(2,1)S(1)} %get-tuple-element.47), channel_id=1, source_target_pairs={{0,2},{1,3},{2,0},{3,1},{4,6},{5,7},{6,4},{7,5},{8,10},{9,11},{10,... | collective-permute-start | bytes 442376 | tf_op jit(solution)/shard_map/ppermute | solution.py:382
  97.4 14.6 %collective-permute-start.5 = (bf16[288,256]{1,0:T(8,128)(2,1)S(1)}, bf16[288,256]{1,0:T(8,128)(2,1)S(1)}, u32[]{:S(2)}, u32[]{:S(2)}) collective-permute-start(bf16[288,256]{1,0:T(8,128)(2,1)S(1)} %get-tuple-element.48), channel_id=1, source_target_pairs={{4,2},{5,3},{6,0},{7,1},{8,6},{9,7},{10,4},{11,5},{12,10},{13,11},... | collective-permute-start | bytes 442376 | tf_op jit(solution)/shard_map/ppermute | solution.py:382
  98.7 16.5 %collective-permute-start.4 = (bf16[288,256]{1,0:T(8,128)(2,1)S(1)}, bf16[288,256]{1,0:T(8,128)(2,1)S(1)}, u32[]{:S(2)}, u32[]{:S(2)}) collective-permute-start(bf16[288,256]{1,0:T(8,128)(2,1)S(1)} %get-tuple-element.48), channel_id=1, source_target_pairs={{4,0},{5,1},{6,2},{7,3},{8,4},{9,5},{10,6},{11,7},{12,8},{13,9},{1... | collective-permute-start | bytes 442376 | tf_op jit(solution)/shard_map/ppermute | solution.py:382
  100.0 22.5 %collective-permute-start.7 = (bf16[288,256]{1,0:T(8,128)(2,1)S(1)}, bf16[288,256]{1,0:T(8,128)(2,1)S(1)}, u32[]{:S(2)}, u32[]{:S(2)}) collective-permute-start(bf16[288,256]{1,0:T(8,128)(2,1)S(1)} %get-tuple-element.49), channel_id=1, source_target_pairs={{8,2},{9,3},{10,0},{11,1},{12,6},{13,7},{14,4},{15,5},{16,10},{17,... | collective-permute-start | bytes 442376 | tf_op jit(solution)/shard_map/ppermute | solution.py:382
  101.3 21.2 %collective-permute-start.6 = (bf16[288,256]{1,0:T(8,128)(2,1)S(1)}, bf16[288,256]{1,0:T(8,128)(2,1)S(1)}, u32[]{:S(2)}, u32[]{:S(2)}) collective-permute-start(bf16[288,256]{1,0:T(8,128)(2,1)S(1)} %get-tuple-element.49), channel_id=1, source_target_pairs={{8,0},{9,1},{10,2},{11,3},{12,4},{13,5},{14,6},{15,7},{16,8},{17,9... | collective-permute-start | bytes 442376 | tf_op jit(solution)/shard_map/ppermute | solution.py:382
  109.9 17.5 %copy-start.1 = (bf16[32,64,512]{2,1,0:T(8,128)(2,1)S(1)}, bf16[32,64,512]{2,1,0:T(8,128)(2,1)}, u32[]{:S(2)}) copy-start(bf16[32,64,512]{2,1,0:T(8,128)(2,1)} %copy-done) | copy-start | bytes 6291460
  122.5 1.2 copy-start.2
  123.7 3.7 %copy-start.3 = (bf16[256,2048]{1,0:T(8,128)(2,1)S(1)}, bf16[256,2048]{1,0:T(8,128)(2,1)}, u32[]{:S(2)}) copy-start(bf16[256,2048]{1,0:T(8,128)(2,1)} %get-tuple-element.24.rest_5_.refs_3_) | copy-start | bytes 3145732
  123.8 2.7 %collective-permute-start.8 = (f32[288,256]{1,0:T(8,128)S(1)}, f32[288,256]{1,0:T(8,128)S(1)}, u32[]{:S(2)}, u32[]{:S(2)}) collective-permute-start(f32[288,256]{1,0:T(8,128)S(1)} %merge.1.mine_ref), channel_id=1, source_target_pairs={{0,1},{1,0},{2,3},{3,2},{4,5},{5,4},{6,7},{7,6},{8,9},{9,8},{10,11... | collective-permute-start | bytes 884744 | tf_op jit(solution)/shard_map/ppermute | solution.py:372
  127.4 1.1 copy-start.4

commit v3 on v2

v3 whole, which is shorter than its diff:
```python
import functools
import math

import jax
import jax.numpy as jnp
from jax import lax
from jax.experimental import pallas as pl
from jax.experimental.pallas import tpu as pltpu
from jax.sharding import PartitionSpec as P

SPAN = 2
CHUNKS = 2
HOPS = (0, 1, -1, 2)
GROUP = 4
LOG2E = 1.4426950408889634
MIB = 2**20
LARGE = 56 * MIB
BRIEF = pl.CostEstimate(flops=2**20, bytes_accessed=2**20, transcendentals=0)


def shifted(block, axis, distance):
    devices = range(lax.axis_size(axis))
    route = [(i - distance, i) for i in devices if i - distance in devices]
    return lax.ppermute(block, axis, route)


def dot(a, b):
    return lax.dot_general(a, b, (((1,), (0,)), ((), ())), preferred_element_type=jnp.float32)


def dot_nt(a, b):
    return lax.dot_general(a, b, (((1,), (1,)), ((), ())), preferred_element_type=jnp.float32)


def prepare_kernel(query_ref, dout_ref, wuk_ref, wuv_ref, qfull_ref, dlo_ref, dout_t_ref, nope_t_ref):
    nope = wuk_ref.shape[1]
    value = wuv_ref.shape[1]
    width = query_ref.shape[1] // wuk_ref.shape[0]
    rank = wuk_ref.shape[2]
    query_t = query_ref[...].T
    dout_t = dout_ref[...].T
    for n in range(wuk_ref.shape[0]):
        q_nope = query_t[n * width : n * width + nope]
        grads = dout_t[n * value : (n + 1) * value]
        nope_t_ref[n] = q_nope
        dout_t_ref[n] = grads
        qfull_ref[n, :rank] = dot(wuk_ref[n].T, q_nope).astype(jnp.bfloat16)
        qfull_ref[n, rank:] = query_t[n * width + nope : (n + 1) * width]
        dlo_ref[n] = dot(wuv_ref[n].T, grads).astype(jnp.bfloat16)


def prepare(query, d_out, w_uk, w_uv):
    toks = query.shape[0]
    heads, nope, rank = w_uk.shape
    value = w_uv.shape[1]
    width = query.shape[1] // heads
    lat = rank + width - nope
    shape = lambda rows: jax.ShapeDtypeStruct((heads, rows, toks), jnp.bfloat16)
    block = lambda rows: pl.BlockSpec((GROUP, rows, toks), lambda s: (s, 0, 0))
    return pl.pallas_call(
        prepare_kernel,
        grid=(heads // GROUP,),
        in_specs=[
            pl.BlockSpec((toks, GROUP * width), lambda s: (0, s)),
            pl.BlockSpec((toks, GROUP * value), lambda s: (0, s)),
            pl.BlockSpec((GROUP, nope, rank), lambda s: (s, 0, 0)),
            pl.BlockSpec((GROUP, value, rank), lambda s: (s, 0, 0)),
        ],
        out_specs=[block(lat), block(rank), block(value), block(nope)],
        out_shape=[shape(lat), shape(rank), shape(value), shape(nope)],
        compiler_params=pltpu.CompilerParams(vmem_limit_bytes=LARGE),
        cost_estimate=pl.CostEstimate(
            flops=4 * heads * toks * nope * rank, bytes_accessed=16 * 2**20, transcendentals=0
        ),
        name="prepare",
    )(query, d_out, w_uk, w_uv)


def score_kernel(
    inv_root,
    which,
    place_ref,
    mask_ref,
    segments_ref,
    block_refs,
    qfull_ref,
    dlo_ref,
    dout_t_ref,
    nope_t_ref,
    *rest,
):
    probs_ref, dscore_ref, lout_ref, dfull_ref, *slab_refs, grad_ref, keys_ref, keys_t_ref, bias_ref = rest[-12:]
    rank = dlo_ref.shape[1]
    group = range(qfull_ref.shape[0])
    step = pl.program_id(0)

    @pl.when(step == 0)
    def _():
        for n, block_ref in enumerate(block_refs):
            toks = block_ref.shape[1]
            keys_t_ref[:, n * toks : (n + 1) * toks] = block_ref[...]
            keys_ref[n * toks : (n + 1) * toks] = block_ref[...].T
        position = place_ref[0]
        seg_query = segments_ref[pl.ds(position, 1)].astype(jnp.float32)
        for n in range(len(block_refs)):
            distance = len(block_refs) - 1 - n
            block = jnp.maximum(position - distance, 0)
            seg_row = segments_ref[pl.ds(block, 1)].astype(jnp.float32)
            seg_key = jnp.broadcast_to(seg_row, (toks, toks)).T
            granted = jnp.broadcast_to(mask_ref[position, block], (toks, toks)) == 1
            allowed = (seg_key == seg_query) | granted
            if distance == 0:
                key, query = (lax.broadcasted_iota(jnp.int32, (toks, toks), axis) for axis in (0, 1))
                allowed &= key <= query
            else:
                allowed &= jnp.broadcast_to(position, (toks, toks)) >= distance
            bias_ref[n * toks : (n + 1) * toks] = jnp.where(allowed, 0.0, -jnp.inf)

    scores = [dot(keys_ref[...], qfull_ref[n]) for n in group]
    probs = []
    for n in group:
        scaled = scores[n] * (inv_root * LOG2E) + bias_ref[...]
        weights = jnp.exp2(scaled - jnp.max(scaled, axis=0, keepdims=True))
        probs.append(weights * (1.0 / jnp.sum(weights, axis=0, keepdims=True)))
        probs_ref[n] = probs[n].astype(jnp.bfloat16)
    d_probs = [dot(keys_ref[:, :rank], dlo_ref[n]) for n in group]
    for n in group:
        lout_ref[n] = dot(keys_t_ref[:rank], probs_ref[n]).astype(jnp.bfloat16)
    for n in group:
        delta = jnp.sum(probs[n] * d_probs[n], axis=0, keepdims=True)
        dscore_ref[n] = (probs[n] * (d_probs[n] - delta) * inv_root).astype(jnp.bfloat16)
    def slab(n):
        return (step * (len(group) // 2) + n // 2 + 4 - place_ref[which]) % 4

    for n in group:
        grad_ref[slab(n), n % 2, 1] = dot_nt(dout_t_ref[n], lout_ref[n]).astype(jnp.bfloat16)
    for n in group:
        dfull_ref[n] = dot(keys_t_ref[...], dscore_ref[n]).astype(jnp.bfloat16)
    for n in group:
        grad_ref[slab(n), n % 2, 0] = dot_nt(nope_t_ref[n], dfull_ref[n, :rank]).astype(jnp.bfloat16)

    @pl.when(step == pl.num_programs(0) - 1)
    def _():
        for hop, slab_ref in zip(HOPS, slab_refs):
            slab_ref[...] = grad_ref[hop % 4].reshape(slab_ref.shape)


def score(which, place, block_mask, segments, blocks, qfull, dlo, dout_t, nope_t, inv_root, start, count, carried):
    heads, lat, toks = qfull.shape
    span = len(blocks) * toks
    rank = dlo.shape[1]
    value, nope = dout_t.shape[1], nope_t.shape[1]
    base = start // GROUP
    whole = lambda rows, cols: pl.BlockSpec((rows, cols), lambda s: (0, 0))
    heads_of = lambda rows: pl.BlockSpec((GROUP, rows, toks), lambda s: (s + base, 0, 0))
    out = lambda rows: jax.ShapeDtypeStruct((heads, rows, toks), jnp.bfloat16)
    return pl.pallas_call(
        functools.partial(score_kernel, inv_root, which),
        grid=(count // GROUP,),
        in_specs=[
            pl.BlockSpec(memory_space=pltpu.SMEM),
            pl.BlockSpec(memory_space=pltpu.SMEM),
            whole(*segments.shape),
            [whole(lat, toks)] * len(blocks),
            heads_of(lat),
            heads_of(rank),
            heads_of(value),
            heads_of(nope),
        ]
        + [pl.BlockSpec(memory_space=pl.ANY)] * len(carried),
        out_specs=[
            heads_of(span),
            heads_of(span),
            heads_of(rank),
            heads_of(lat),
        ]
        + [whole(4 * nope, rank)] * len(HOPS),
        out_shape=[
            out(span),
            out(span),
            out(rank),
            out(lat),
        ]
        + [jax.ShapeDtypeStruct((4 * nope, rank), jnp.bfloat16)] * len(HOPS),
        input_output_aliases={7 + len(blocks) + n: n for n in range(len(carried))},
        scratch_shapes=[
            pltpu.VMEM((4, 2, 2, nope, rank), jnp.bfloat16),
            pltpu.VMEM((span, lat), jnp.bfloat16),
            pltpu.VMEM((lat, span), jnp.bfloat16),
            pltpu.VMEM((span, toks), jnp.float32),
        ],
        compiler_params=pltpu.CompilerParams(vmem_limit_bytes=LARGE),
        cost_estimate=pl.CostEstimate(
            flops=8 * count * toks * span * (rank + lat),
            bytes_accessed=3 * count * 2**20,
            transcendentals=count * toks * span,
        ),
        name="score",
    )(place, block_mask, segments, blocks, qfull, dlo, dout_t, nope_t, *carried)


def key_kernel(qfull_ref, dlo_ref, probs_ref, dscore_ref, _, total_ref):
    rank = dlo_ref.shape[1]

    @pl.when(pl.program_id(0) == 0)
    def _():
        total_ref[...] = jnp.zeros_like(total_ref)

    content = 0.0
    rope = 0.0
    for n in range(qfull_ref.shape[0]):
        content += dot_nt(qfull_ref[n, :rank], dscore_ref[n]) + dot_nt(dlo_ref[n], probs_ref[n])
        rope += dot_nt(qfull_ref[n, rank:], dscore_ref[n])
    total_ref[:rank] += content
    total_ref[rank:] += rope


def key_gradient(qfull, dlo, probs, dscore, after):
    heads, lat, toks = qfull.shape
    rank = dlo.shape[1]
    span = probs.shape[1]
    heads_of = lambda rows: pl.BlockSpec((GROUP, rows, toks), lambda s: (s, 0, 0))
    return pl.pallas_call(
        key_kernel,
        grid=(heads // GROUP,),
        in_specs=[heads_of(lat), heads_of(rank), heads_of(span), heads_of(span)]
        + [pl.BlockSpec(memory_space=pl.ANY)],
        out_specs=pl.BlockSpec((lat, span), lambda s: (0, 0)),
        out_shape=jax.ShapeDtypeStruct((lat, span), jnp.float32),
        compiler_params=pltpu.CompilerParams(vmem_limit_bytes=LARGE),
        cost_estimate=pl.CostEstimate(
            flops=4 * heads * toks * span * (rank + lat), bytes_accessed=24 * MIB, transcendentals=0
        ),
        name="key_gradient",
    )(qfull, dlo, probs, dscore, after)


def split_kernel(keep_ref, got_ref, own_ref, *part_refs):
    toks = own_ref.shape[1]
    for part, part_ref in enumerate(part_refs + (own_ref,)):
        span = slice(part * toks, (part + 1) * toks)
        part_ref[...] = (keep_ref[:, span] + got_ref[:, span]).astype(part_ref.dtype)


def split(keep, got, toks):
    rows, span = keep.shape
    out = lambda dtype: jax.ShapeDtypeStruct((rows, toks), dtype)
    return pl.pallas_call(
        split_kernel,
        out_shape=[out(jnp.float32)] + [out(jnp.bfloat16)] * SPAN,
        compiler_params=pltpu.CompilerParams(vmem_limit_bytes=12 * MIB),
        cost_estimate=BRIEF,
        name="split",
    )(keep, got)


def merge_kernel(own_ref, *rest):
    *part_refs, out_ref = rest
    total = own_ref[...]
    for part_ref in part_refs:
        total += part_ref[...].astype(jnp.float32)
    out_ref[...] = total.astype(out_ref.dtype)


def merge(own, parts):
    return pl.pallas_call(
        merge_kernel,
        out_shape=jax.ShapeDtypeStruct(own.shape, jnp.bfloat16),
        compiler_params=pltpu.CompilerParams(vmem_limit_bytes=12 * MIB),
        cost_estimate=BRIEF,
        name="merge",
    )(own, *parts)


def finish_kernel(own_ref, far_ref, out_ref):
    out_ref[...] = own_ref[...].astype(jnp.float32) + far_ref[...].astype(jnp.float32)


def finish(own, far):
    return pl.pallas_call(
        finish_kernel,
        out_shape=jax.ShapeDtypeStruct(own.shape, jnp.float32),
        compiler_params=pltpu.CompilerParams(vmem_limit_bytes=12 * MIB),
        cost_estimate=BRIEF,
        name="finish",
    )(own, far)


def assemble_kernel(core_ref, mine_ref, other_ref, out_ref):
    rows = mine_ref.shape[0]
    core = core_ref[0]
    out_ref[pl.ds(pl.multiple_of(core * rows, rows), rows)] = mine_ref[...]
    out_ref[pl.ds(pl.multiple_of((1 - core) * rows, rows), rows)] = other_ref[...]


def assemble(core, mine, other):
    rows, toks = mine.shape
    whole = pl.BlockSpec(memory_space=pltpu.VMEM)
    return pl.pallas_call(
        assemble_kernel,
        in_specs=[pl.BlockSpec(memory_space=pltpu.SMEM), whole, whole],
        out_specs=whole,
        out_shape=jax.ShapeDtypeStruct((2 * rows, toks), jnp.float32),
        compiler_params=pltpu.CompilerParams(vmem_limit_bytes=12 * MIB),
        cost_estimate=BRIEF,
        name="assemble",
    )(core, mine, other)


def project_kernel(lout_ref, dfull_ref, wuk_ref, wuv_ref, _, att_ref, dq_ref):
    group = range(lout_ref.shape[0])
    rank = lout_ref.shape[1]
    value = wuv_ref.shape[1]
    width = dq_ref.shape[1] // len(group)
    for n in group:
        attended = dot(wuv_ref[n], lout_ref[n]).astype(jnp.bfloat16)
        att_ref[:, n * value : (n + 1) * value] = attended.T
        d_nope = dot(wuk_ref[n], dfull_ref[n, :rank]).astype(jnp.bfloat16)
        dq_ref[:, n * width : (n + 1) * width] = jnp.concatenate([d_nope, dfull_ref[n, rank:]], axis=0).T


def project(lout, dfull, w_uk, w_uv, after):
    heads, lat, toks = dfull.shape
    nope, rank = w_uk.shape[1:]
    value = w_uv.shape[1]
    width = nope + lat - rank
    heads_of = lambda rows, cols: pl.BlockSpec((GROUP, rows, cols), lambda s: (s, 0, 0))
    out = lambda cols: jax.ShapeDtypeStruct((toks, heads * cols), jnp.bfloat16)
    return pl.pallas_call(
        project_kernel,
        grid=(heads // GROUP,),
        in_specs=[heads_of(rank, toks), heads_of(lat, toks), heads_of(nope, rank), heads_of(value, rank)]
        + [pl.BlockSpec(memory_space=pl.ANY)],
        out_specs=[
            pl.BlockSpec((toks, GROUP * value), lambda s: (0, s)),
            pl.BlockSpec((toks, GROUP * width), lambda s: (0, s)),
        ],
        out_shape=[out(value), out(width)],
        compiler_params=pltpu.CompilerParams(vmem_limit_bytes=16 * MIB),
        cost_estimate=BRIEF,
        name="project",
    )(lout, dfull, w_uk, w_uv, after)


def reduce_kernel(which, place_ref, *refs):
    *slab_refs, _, own_ref, up_ref, down_ref, far_ref = refs
    rows = own_ref.shape[0]
    for hop, out_ref in zip(HOPS, (own_ref, up_ref, down_ref, far_ref)):
        span = pl.ds(pl.multiple_of(((place_ref[which] + hop + 4) % 4) * rows, rows), rows)
        total = 0.0
        for slab_ref in slab_refs:
            total += slab_ref[span].astype(jnp.float32)
        out_ref[...] = total.astype(out_ref.dtype)


def reduced(which, place, slabs, after):
    whole = pl.BlockSpec(memory_space=pltpu.VMEM)
    rows, cols = slabs[0].shape
    return pl.pallas_call(
        functools.partial(reduce_kernel, which),
        in_specs=[pl.BlockSpec(memory_space=pltpu.SMEM)]
        + [whole] * len(slabs)
        + [pl.BlockSpec(memory_space=pl.ANY)],
        out_specs=[whole] * 4,
        out_shape=[jax.ShapeDtypeStruct((rows // 4, cols), jnp.bfloat16)] * 4,
        compiler_params=pltpu.CompilerParams(vmem_limit_bytes=16 * MIB),
        cost_estimate=BRIEF,
        name="reduced",
    )(place, *slabs, after)


def cut_kernel(core_ref, total_ref, _, keep_ref, send_ref):
    rows = keep_ref.shape[0]
    keep_ref[...] = total_ref[pl.ds(pl.multiple_of(core_ref[0] * rows, rows), rows)]
    send_ref[...] = total_ref[pl.ds(pl.multiple_of((1 - core_ref[0]) * rows, rows), rows)]


def cut(core, total, after):
    rows, cols = total.shape
    whole = pl.BlockSpec(memory_space=pltpu.VMEM)
    return pl.pallas_call(
        cut_kernel,
        in_specs=[pl.BlockSpec(memory_space=pltpu.SMEM), whole, pl.BlockSpec(memory_space=pl.ANY)],
        out_specs=[whole] * 2,
        out_shape=[jax.ShapeDtypeStruct((rows // 2, cols), jnp.float32)] * 2,
        compiler_params=pltpu.CompilerParams(vmem_limit_bytes=12 * MIB),
        cost_estimate=BRIEF,
        name="cut",
    )(core, total, after)


def total_kernel(*refs):
    *in_refs, _, out_ref = refs
    rows = in_refs[0].shape[0]
    half = len(in_refs) // 2
    for n, group in enumerate((in_refs[:half], in_refs[half:])):
        total = 0.0
        for in_ref in group:
            total += in_ref[...].astype(jnp.float32)
        out_ref[n * rows : (n + 1) * rows] = total.astype(out_ref.dtype)


def totals(first, second, after):
    whole = pl.BlockSpec(memory_space=pltpu.VMEM)
    rows, cols = first[0].shape
    return pl.pallas_call(
        total_kernel,
        in_specs=[whole] * 2 * len(first) + [pl.BlockSpec(memory_space=pl.ANY)],
        out_specs=whole,
        out_shape=jax.ShapeDtypeStruct((2 * rows, cols), jnp.bfloat16),
        compiler_params=pltpu.CompilerParams(vmem_limit_bytes=16 * MIB),
        cost_estimate=BRIEF,
        name="totals",
    )(*first, *second, after)


def pair_kernel(mine_ref, other_ref, first_ref, second_ref):
    total = mine_ref[...].astype(jnp.float32) + other_ref[...].astype(jnp.float32)
    rows = first_ref.shape[0]
    first_ref[...] = total[:rows].astype(first_ref.dtype)
    second_ref[...] = total[rows:].astype(second_ref.dtype)


def pair_up(mine, other):
    whole = pl.BlockSpec(memory_space=pltpu.VMEM)
    rows, cols = mine.shape
    return pl.pallas_call(
        pair_kernel,
        in_specs=[whole, whole],
        out_specs=[whole, whole],
        out_shape=[jax.ShapeDtypeStruct((rows // 2, cols), mine.dtype)] * 2,
        compiler_params=pltpu.CompilerParams(vmem_limit_bytes=16 * MIB),
        cost_estimate=BRIEF,
        name="pair_up",
    )(mine, other)


def stack_kernel(*refs):
    *in_refs, _, first_ref, second_ref = refs
    rows = in_refs[0].shape[0]
    half = len(in_refs) // 2
    for out_ref, group in ((first_ref, in_refs[:half]), (second_ref, in_refs[half:])):
        for n, in_ref in enumerate(group):
            out_ref[n * rows : (n + 1) * rows] = in_ref[...]


def stack(first, second, after):
    whole = pl.BlockSpec(memory_space=pltpu.VMEM)
    rows, cols = first[0].shape
    return pl.pallas_call(
        stack_kernel,
        in_specs=[whole] * 2 * len(first) + [pl.BlockSpec(memory_space=pl.ANY)],
        out_specs=[whole, whole],
        out_shape=[jax.ShapeDtypeStruct((len(first) * rows, cols), first[0].dtype)] * 2,
        compiler_params=pltpu.CompilerParams(vmem_limit_bytes=16 * MIB),
        cost_estimate=BRIEF,
        name="stack",
    )(*first, *second, after)


def widen_kernel(place_ref, *refs):
    *slab_refs, _, _, uk_ref, uv_ref, wide_ref, sems = refs
    rows = slab_refs[0].shape[0] // len(HOPS)
    copies = []
    for n, slab_ref in enumerate(slab_refs):
        chunk, hop = n // len(HOPS), HOPS[n % len(HOPS)]
        outer, inner = place_ref[1 + chunk], place_ref[2 - chunk]
        for m, inner_hop in enumerate(HOPS):
            source = (inner - inner_hop + 4) % 4
            piece = slab_ref[m * rows : (m + 1) * rows].astype(jnp.float32)
            wide_ref[n, source % 2, source // 2] = piece
        head = 2 * (4 * chunk + (outer - hop + 4) % 4)
        for kind, out_ref in enumerate((uk_ref, uv_ref)):
            copy = pltpu.make_async_copy(wide_ref.at[n, kind], out_ref.at[pl.ds(head, 2)], sems.at[n, kind])
            copy.start()
            copies.append(copy)
    for copy in copies:
        copy.wait()


def widen(place, slabs, heads, height, after):
    cols = slabs[0].shape[1]
    whole = pl.BlockSpec(memory_space=pltpu.VMEM)
    somewhere = pl.BlockSpec(memory_space=pl.ANY)
    out = jax.ShapeDtypeStruct((heads, height, cols), jnp.float32)
    return pl.pallas_call(
        widen_kernel,
        in_specs=[pl.BlockSpec(memory_space=pltpu.SMEM)]
        + [whole] * len(slabs)
        + [somewhere] * len(after),
        out_specs=[somewhere] * 2,
        out_shape=[out, out],
        scratch_shapes=[
            pltpu.VMEM((len(slabs), 2, 2, height, cols), jnp.float32),
            pltpu.SemaphoreType.DMA((len(slabs), 2)),
        ],
        compiler_params=pltpu.CompilerParams(vmem_limit_bytes=20 * MIB),
        cost_estimate=pl.CostEstimate(flops=2**21, bytes_accessed=12 * MIB, transcendentals=0),
        name="widen",
    )(place, *slabs, *after)


def moved(block, along, back, far):
    route = []
    for x in range(4):
        for z in range(4):
            for y in range(2):
                to = ((x + along) % 4) * 8 + ((z + back) % 4) * 2 + (y + far) % 2
                route.append((x * 8 + z * 2 + y, to))
    return lax.ppermute(block, "ctx", route)


def along_x(blocks):
    return [moved(block, hop, 0, 0) for block, hop in zip(blocks, HOPS[1:])]


def along_z(blocks):
    return [moved(block, 0, hop, 0) for block, hop in zip(blocks, HOPS[1:])]


def swap_core(block):
    return lax.ppermute(block, "head", [(0, 1), (1, 0), (2, 3), (3, 2)])


def swap_far(block):
    return lax.ppermute(block, "head", [(0, 2), (2, 0), (1, 3), (3, 1)])


def body(latent, query, d_out, w_uk, w_uv, block_mask, segments):
    toks, lat = latent.shape
    heads, nope, rank = w_uk.shape
    width = query.shape[1] // heads
    inv_root = 1.0 / math.sqrt(width)
    position = lax.axis_index("ctx")
    seg_rows = segments.reshape(-1, toks)
    latent_t = latent.T
    blocks = [shifted(latent_t, "ctx", distance) for distance in (2, 1)] + [latent_t]
    qfull, dlo, dout_t, nope_t = prepare(query, d_out, w_uk, w_uv)

    core = (lax.axis_index("head") % 2).astype(jnp.int32).reshape(1)
    carried = []
    slabs = []
    count = heads // CHUNKS
    place = jnp.stack([position, position // 8, position // 2 % 4]).astype(jnp.int32)
    for chunk in range(CHUNKS):
        outputs = score(
            1 + chunk,
            place,
            block_mask,
            seg_rows,
            blocks,
            qfull,
            dlo,
            dout_t,
            nope_t,
            inv_root,
            chunk * count,
            count,
            carried,
        )
        carried = outputs[:4]
        slabs.append(outputs[4:])
    probs, dscore, lout, dfull = carried
    first, second = slabs
    first = reduced(2, place, [first[0]] + along_x(first[1:]), probs)
    total = key_gradient(qfull, dlo, probs, dscore, first[0])
    second = reduced(1, place, [second[0]] + along_z(second[1:]), total)
    keep, send = cut(core, total, second[0])
    own, *parts = split(keep, swap_core(send), toks)
    mine = totals([first[0]] + along_z(first[1:]), [second[0]] + along_x(second[1:]), own)
    low = merge(own, [shifted(parts[part], "ctx", part - SPAN) for part in range(SPAN)])
    first, second = pair_up(mine, moved(mine, 0, 0, 1))
    half = finish(low, swap_far(low))
    first, second = stack([first] + along_z([first] * 3), [second] + along_x([second] * 3), half)
    attended, d_query = project(lout, dfull, w_uk, w_uv, first)
    d_latent_t = assemble(core, half, swap_core(half))
    slabs = [first] + along_x([first] * 3) + [second] + along_z([second] * 3)
    d_w_uk, d_w_uv = widen(place, slabs, heads, nope, (attended, d_latent_t))
    return attended, d_query, d_latent_t.T, d_w_uk, d_w_uv


def solution(mesh):
    in_specs = (
        P("ctx", None),
        P("ctx", "head"),
        P("ctx", "head"),
        P("head", None, None),
        P("head", None, None),
        P(),
        P(),
    )
    out_specs = (
        P("ctx", "head"),
        P("ctx", "head"),
        P("ctx", None),
        P("head", None, None),
        P("head", None, None),
    )
    return jax.shard_map(body, mesh=mesh, in_specs=in_specs, out_specs=out_specs, check_vma=False)
```

time: 195 us -> 172 us (0.88)
  blocking collectives: 57 us -> 0 us
  waiting for transfers between devices: 17.8 us -> 42.1 us
  starting transfers between devices: 34.1 us -> 51.1 us
  Pallas kernels: 73.7 us -> 66.5 us
  local copies, waits for them, and re-layouts: 6.58 us -> 9.34 us
    all_to_all x1 -> x0, blocking collectives: 57 us -> none  [body(): sums = lax.all_to_all(sums, 'ctx', 0, 0, tiled=True)]
    ppermute x5 -> x26, starting transfers between devices: 7.87 us -> 32.1 us  [the longest x25 30 us: moved(): return lax.ppermute(block, 'ctx', route)]
    ppermute x5 -> x26, waiting for transfers between devices: 12.6 us -> 34.9 us  [the longest x25 34.9 us: moved(): return lax.ppermute(block, 'ctx', route)]
    all_to_all x2 -> x0, starting transfers between devices: 16.3 us -> none  [scattered(): lax.all_to_all(grads.reshape(parts, -1, grads.shape[-1]), 'ctx', 0, 0, ti...]
    ppermute x2 -> x4, waiting for transfers between devices: 0.01 us -> 7.21 us  [shifted(): return lax.ppermute(block, axis, route)]
    ppermute x2, starting transfers between devices: 2.28 us -> 8.86 us  [swap_core(): return lax.ppermute(block, 'head', [(0, 1), (1, 0), (2, 3), (3, 2)])]
    pallas_call x1, Pallas kernels: 7.3 us -> 3.42 us  [project(): pl.pallas_call(project_kernel, grid=(heads // GROUP,), in_specs=[heads_of...]
    unnamed x16 -> x32, local copies, waits for them, and re-layouts: 4.26 us -> 7.97 us
  transfers between devices with their start and end apart: 11 -> 32, of which waited for: 6 -> 16; matrix products, arithmetic and copies ran while one was open for 2% -> 1% of each run, Pallas kernels for 26% -> 26%
where the time goes in v3:
time: 172 us; the launch traced here: 171 us
  Pallas kernels  66.5 us (39%)
  starting transfers between devices  51.1 us (30%)
  waiting for transfers between devices  42.1 us (24%)
  local copies, waits for them, and re-layouts  9.34 us (5%)
    ppermute x25, waiting for transfers between devices, moved(): return lax.ppermute(block, 'ctx', route)  34.9 us
    pallas_call x2, Pallas kernels, score(): pl.pallas_call(functools.partial(score_kernel, inv_root, which), grid=(co...  34.2 us
    ppermute x25, starting transfers between devices, moved(): return lax.ppermute(block, 'ctx', route)  30 us
    pallas_call x1, Pallas kernels, key_gradient(): pl.pallas_call(key_kernel, grid=(heads // GROUP,), in_specs=[heads_of(lat...  13.5 us
    ppermute x4, starting transfers between devices, shifted(): return lax.ppermute(block, axis, route)  10.2 us
    ppermute x2, starting transfers between devices, swap_core(): return lax.ppermute(block, 'head', [(0, 1), (1, 0), (2, 3), (3, 2)])  8.86 us
    pallas_call x1, Pallas kernels, prepare(): pl.pallas_call(prepare_kernel, grid=(heads // GROUP,), in_specs=[pl.Block...  8.26 us
    unnamed x32, local copies, waits for them, and re-layouts  7.97 us
  transfers between devices with their start and end apart: 32, of which 16 were waited for; matrix products, arithmetic and copies ran while one was open for 1% of the time, Pallas kernels for 26%

profile of v3, /device:TPU:1, one launch (start us, length us, event | category | flops | bytes accessed | tf_op | source)
XLA Modules:
  0.0 170.7 jit_solution(7761046237846635447)
XLA Ops:
  0.6 4.0 %collective-permute-start.1 = (bf16[576,256]{1,0:T(8,128)(2,1)}, bf16[576,256]{1,0:T(8,128)(2,1)S(1)}, u32[]{:S(2)}, u32[]{:S(2)}) collective-permute-start(bf16[576,256]{1,0:T(8,128)(2,1)} %bitcast.9), channel_id=1, source_target_pairs={{0,4},{4,8},{8,12},{12,16},{16,20},{20,24},{24,28},{28,32},{32,36}... | collective-permute-start | bytes 884744 | tf_op jit(solution)/shard_map/ppermute | solution.py:24
  4.7 3.5 %collective-permute-start = (bf16[576,256]{1,0:T(8,128)(2,1)}, bf16[576,256]{1,0:T(8,128)(2,1)S(1)}, u32[]{:S(2)}, u32[]{:S(2)}) collective-permute-start(bf16[576,256]{1,0:T(8,128)(2,1)} %bitcast.10), channel_id=1, source_target_pairs={{0,8},{4,12},{8,16},{12,20},{16,24},{20,28},{24,32},{28,36},{32,40... | collective-permute-start | bytes 884744 | tf_op jit(solution)/shard_map/ppermute | solution.py:24
  9.7 8.3 %prepare.1 = (bf16[16,576,256]{2,1,0:T(8,128)(2,1)}, bf16[16,512,256]{2,1,0:T(8,128)(2,1)}, bf16[16,128,256]{2,1,0:T(8,128)(2,1)}, bf16[16,128,256]{2,1,0:T(8,128)(2,1)}) custom-call(bf16[256,3072]{1,0:T(8,128)(2,1)} %query_ref.1, bf16[256,2048]{1,0:T(8,128)(2,1)} %dout_ref.1, bf16[16,128,512]{2,1,0:T(8,128)(2,1)} %wuk_ref.3, bf16[16,128,512]{2,1,0:T(8,128)(2,1)} %wuv_ref.3), custom_call_target="tpu_custom_call" | custom-call | flops 1073741824 | bytes 16777216 | tf_op jit(solution)/shard_map/prepare/pallas_call | solution.py:60
  20.0 17.1 %score.2 = (bf16[16,768,256]{2,1,0:T(8,128)(2,1)}, bf16[16,768,256]{2,1,0:T(8,128)(2,1)}, bf16[16,512,256]{2,1,0:T(8,128)(2,1)}, bf16[16,576,256]{2,1,0:T(8,128)...) custom-call(s32[3]{0:T(128)} %pad_add_fusion.place_ref, ...), custom_call_target="tpu_custom_call" | custom-call | flops 13690208256 | bytes 25165824 | tf_op jit(solution)/shard_map/score/pallas_call | solution.py:157
  37.1 3.0 %collective-permute-start.2 = (bf16[512,512]{1,0:T(8,128)(2,1)}, bf16[512,512]{1,0:T(8,128)(2,1)S(1)}, u32[]{:S(2)}, u32[]{:S(2)}) collective-permute-start(bf16[512,512]{1,0:T(8,128)(2,1)} %get-tuple-element.57), channel_id=1, source_target_pairs={{0,32},{4,36},{8,40},{12,44},{16,48},{20,52},{24,56},{28,60},{32,6... | collective-permute-start | bytes 1572872 | tf_op jit(solution)/shard_map/ppermute | solution.py:510
  40.1 1.7 %collective-permute-start.3 = (bf16[512,512]{1,0:T(8,128)(2,1)}, bf16[512,512]{1,0:T(8,128)(2,1)S(1)}, u32[]{:S(2)}, u32[]{:S(2)}) collective-permute-start(bf16[512,512]{1,0:T(8,128)(2,1)} %get-tuple-element.58), channel_id=1, source_target_pairs={{0,96},{4,100},{8,104},{12,108},{16,112},{20,116},{24,120},{28,124... | collective-permute-start | bytes 1572872 | tf_op jit(solution)/shard_map/ppermute | solution.py:510
  43.1 17.2 %score.3 = (bf16[16,768,256]{2,1,0:T(8,128)(2,1)}, bf16[16,768,256]{2,1,0:T(8,128)(2,1)}, bf16[16,512,256]{2,1,0:T(8,128)(2,1)}, bf16[16,576,256]{2,1,0:T(8,128)...) custom-call(s32[3]{0:T(128)} %pad_add_fusion.place_ref, ...), custom_call_target="tpu_custom_call", output_to_operand_aliasing={{0}: (10, {}), {1}: (11, {}), {2}: (12, {}), {3}: (13, {})} | custom-call | flops 13690208256 | bytes 25165824 | tf_op jit(solution)/shard_map/score/pallas_call | solution.py:157
  60.7 2.3 %collective-permute-start.9 = (bf16[512,512]{1,0:T(8,128)(2,1)}, bf16[512,512]{1,0:T(8,128)(2,1)S(1)}, u32[]{:S(2)}, u32[]{:S(2)}) collective-permute-start(bf16[512,512]{1,0:T(8,128)(2,1)} %get-tuple-element.67), channel_id=1, source_target_pairs={{0,24},{4,28},{8,0},{12,4},{16,8},{20,12},{24,16},{28,20},{32,56},... | collective-permute-start | bytes 1572872 | tf_op jit(solution)/shard_map/ppermute | solution.py:510
  64.7 2.8 %copy-done.3 = bf16[16,768,256]{2,1,0:T(8,128)(2,1)S(1)} copy-done((bf16[16,768,256]{2,1,0:T(8,128)(2,1)S(1)}, bf16[16,768,256]{2,1,0:T(8,128)(2,1)}, u32[]{:S(2)}) %copy-start.3) | copy-done | bytes 6291480
  69.0 13.5 %key_gradient.1.refs_4_.total_ref = f32[576,768]{1,0:T(8,128)} custom-call(bf16[16,576,256]{2,1,0:T(8,128)(2,1)} %get-tuple-element.46.qfull_ref, bf16[16,512,256]{2,1,0:T(8,128)(2,1)} %get-tuple-element.47.dlo_ref, bf16[16,768,256]{2,1,0:T(8,128)(2,1)} %get-tuple-element.60.refs_4_.probs_ref, bf16[16,768,256]{2,1,0:T(8,128)(2,1)} %get-tuple-element.69.dscore_ref, ...), custom_call_target="tpu_custom_call" | custom-call | flops 13690208256 | bytes 25165824 | tf_op jit(solution)/shard_map/key_gradient/pallas_call | solution.py:223
  82.5 3.6 %collective-permute-done.10.refs_3_ = bf16[512,512]{1,0:T(8,128)(2,1)S(1)} collective-permute-done((bf16[512,512]{1,0:T(8,128)(2,1)}, bf16[512,512]{1,0:T(8,128)(2,1)S(1)}, u32[]{:S(2)}, u32[]{:S(2)}) %collective-permute-start.10) | collective-permute-done | bytes 524320 | tf_op jit(solution)/shard_map/ppermute | solution.py:510
  88.6 2.3 %collective-permute-start.14 = (f32[288,768]{1,0:T(8,128)S(1)}, f32[288,768]{1,0:T(8,128)S(1)}, u32[]{:S(2)}, u32[]{:S(2)}) collective-permute-start(f32[288,768]{1,0:T(8,128)S(1)} %get-tuple-element.75), channel_id=1, source_target_pairs={{0,1},{1,0},{2,3},{3,2},{4,5},{5,4},{6,7},{7,6},{8,9},{9,8},{10,11... | collective-permute-start | bytes 2654216 | tf_op jit(solution)/shard_map/ppermute | solution.py:522
  91.7 1.8 %collective-permute-start.6 = (bf16[128,512]{1,0:T(8,128)(2,1)S(1)}, bf16[128,512]{1,0:T(8,128)(2,1)S(1)}, u32[]{:S(2)}, u32[]{:S(2)}) collective-permute-start(bf16[128,512]{1,0:T(8,128)(2,1)S(1)} %get-tuple-element.63), channel_id=1, source_target_pairs={{0,24},{4,28},{8,0},{12,4},{16,8},{20,12},{24,16},{28,20},{32,56},... | collective-permute-start | bytes 393224 | tf_op jit(solution)/shard_map/ppermute | solution.py:510
  94.4 2.8 %collective-permute-done.5.refs_1_ = bf16[128,512]{1,0:T(8,128)(2,1)S(1)} collective-permute-done((bf16[128,512]{1,0:T(8,128)(2,1)S(1)}, bf16[128,512]{1,0:T(8,128)(2,1)S(1)}, u32[]{:S(2)}, u32[]{:S(2)}) %collective-permute-start.5) | collective-permute-done | bytes 131104 | tf_op jit(solution)/shard_map/ppermute | solution.py:510
  99.5 1.8 %collective-permute-done.12.refs_6_ = bf16[128,512]{1,0:T(8,128)(2,1)S(1)} collective-permute-done((bf16[128,512]{1,0:T(8,128)(2,1)S(1)}, bf16[128,512]{1,0:T(8,128)(2,1)S(1)}, u32[]{:S(2)}, u32[]{:S(2)}) %collective-permute-start.12) | collective-permute-done | bytes 131104 | tf_op jit(solution)/shard_map/ppermute | solution.py:510
  101.3 2.0 %collective-permute-done.13.refs_7_ = bf16[128,512]{1,0:T(8,128)(2,1)S(1)} collective-permute-done((bf16[128,512]{1,0:T(8,128)(2,1)S(1)}, bf16[128,512]{1,0:T(8,128)(2,1)S(1)}, u32[]{:S(2)}, u32[]{:S(2)}) %collective-permute-start.13) | collective-permute-done | bytes 131104 | tf_op jit(solution)/shard_map/ppermute | solution.py:510
  107.0 3.6 %collective-permute-done.22.rest_0_ = bf16[288,256]{1,0:T(8,128)(2,1)S(1)} collective-permute-done((bf16[288,256]{1,0:T(8,128)(2,1)S(1)}, bf16[288,256]{1,0:T(8,128)(2,1)S(1)}, u32[]{:S(2)}, u32[]{:S(2)}) %collective-permute-start.22) | collective-permute-done | bytes 147488 | tf_op jit(solution)/shard_map/ppermute | solution.py:24
  110.6 2.9 %collective-permute-done.23.rest_1_ = bf16[288,256]{1,0:T(8,128)(2,1)S(1)} collective-permute-done((bf16[288,256]{1,0:T(8,128)(2,1)S(1)}, bf16[288,256]{1,0:T(8,128)(2,1)S(1)}, u32[]{:S(2)}, u32[]{:S(2)}) %collective-permute-start.23) | collective-permute-done | bytes 147488 | tf_op jit(solution)/shard_map/ppermute | solution.py:24
  113.6 2.0 %collective-permute-start.24 = (bf16[288,256]{1,0:T(8,128)(2,1)S(1)}, bf16[288,256]{1,0:T(8,128)(2,1)S(1)}, u32[]{:S(2)}, u32[]{:S(2)}) collective-permute-start(bf16[288,256]{1,0:T(8,128)(2,1)S(1)} %merge.1.own_ref), channel_id=1, source_target_pairs={{0,2},{2,0},{1,3},{3,1},{4,6},{6,4},{5,7},{7,5},{8,10},{10,8},{9,1... | collective-permute-start | bytes 442376 | tf_op jit(solution)/shard_map/ppermute | solution.py:526
  115.6 2.4 %collective-permute-start.18 = (bf16[128,512]{1,0:T(8,128)(2,1)S(1)}, bf16[128,512]{1,0:T(8,128)(2,1)S(1)}, u32[]{:S(2)}, u32[]{:S(2)}) collective-permute-start(bf16[128,512]{1,0:T(8,128)(2,1)S(1)} %get-tuple-element.77.refs_0_), channel_id=1, source_target_pairs={{0,16},{4,20},{8,24},{12,28},{16,0},{20,4},{24,8},{28,12},{32,48},... | collective-permute-start | bytes 393224 | tf_op jit(solution)/shard_map/ppermute | solution.py:510
  119.5 2.4 %collective-permute-start.21 = (bf16[128,512]{1,0:T(8,128)(2,1)S(1)}, bf16[128,512]{1,0:T(8,128)(2,1)S(1)}, u32[]{:S(2)}, u32[]{:S(2)}) collective-permute-start(bf16[128,512]{1,0:T(8,128)(2,1)S(1)} %get-tuple-element.78.refs_4_), channel_id=1, source_target_pairs={{0,64},{4,68},{8,72},{12,76},{16,80},{20,84},{24,88},{28,92},{32,9... | collective-permute-start | bytes 393224 | tf_op jit(solution)/shard_map/ppermute | solution.py:510
  121.9 1.7 %collective-permute-start.20 = (bf16[128,512]{1,0:T(8,128)(2,1)S(1)}, bf16[128,512]{1,0:T(8,128)(2,1)S(1)}, u32[]{:S(2)}, u32[]{:S(2)}) collective-permute-start(bf16[128,512]{1,0:T(8,128)(2,1)S(1)} %get-tuple-element.78.refs_4_), channel_id=1, source_target_pairs={{0,96},{4,100},{8,104},{12,108},{16,112},{20,116},{24,120},{28,124... | collective-permute-start | bytes 393224 | tf_op jit(solution)/shard_map/ppermute | solution.py:510
  124.2 1.6 collective-permute-done.16.refs_1_
  126.7 2.2 %collective-permute-done.19.refs_5_ = bf16[128,512]{1,0:T(8,128)(2,1)S(1)} collective-permute-done((bf16[128,512]{1,0:T(8,128)(2,1)S(1)}, bf16[128,512]{1,0:T(8,128)(2,1)S(1)}, u32[]{:S(2)}, u32[]{:S(2)}) %collective-permute-start.19) | collective-permute-done | bytes 131104 | tf_op jit(solution)/shard_map/ppermute | solution.py:510
  129.0 1.5 collective-permute-start.31
  130.5 6.6 %collective-permute-start.25 = (f32[288,256]{1,0:T(8,128)S(1)}, f32[288,256]{1,0:T(8,128)S(1)}, u32[]{:S(2)}, u32[]{:S(2)}) collective-permute-start(f32[288,256]{1,0:T(8,128)S(1)} %finish.1.refs_8_.mine_ref), channel_id=1, source_target_pairs={{0,1},{1,0},{2,3},{3,2},{4,5},{5,4},{6,7},{7,6},{8,9},{9,8},{10,11... | collective-permute-start | bytes 884744 | tf_op jit(solution)/shard_map/ppermute | solution.py:522
  139.2 1.5 collective-permute-start.27
  140.7 3.4 %project.1 = (bf16[256,2048]{1,0:T(8,128)(2,1)}, bf16[256,3072]{1,0:T(8,128)(2,1)}) custom-call(bf16[16,512,256]{2,1,0:T(8,128)(2,1)S(1)} %copy-done.4, bf16[16,576,256]{2,1,0:T(8,128)(2,1)S(1)} %bitcast.7, bf16[16,128,512]{2,1,0:T(8,128)(2,1)S(1)} %copy-done, bf16[16,128,512]{2,1,0:T(8,128)(2,1)S(1)} %copy-done.1, ...), custom_call_target="tpu_custom_call" | custom-call | flops 1048576 | bytes 1048576 | tf_op jit(solution)/shard_map/project/pallas_call | solution.py:329
  145.0 11.2 %collective-permute-done.30.refs_6_ = bf16[512,512]{1,0:T(8,128)(2,1)S(1)} collective-permute-done((bf16[512,512]{1,0:T(8,128)(2,1)S(1)}, bf16[512,512]{1,0:T(8,128)(2,1)S(1)}, u32[]{:S(2)}, u32[]{:S(2)}) %collective-permute-start.30) | collective-permute-done | bytes 524320 | tf_op jit(solution)/shard_map/ppermute | solution.py:510
  156.9 4.8 %collective-permute-done.27.refs_2_ = bf16[512,512]{1,0:T(8,128)(2,1)S(1)} collective-permute-done((bf16[512,512]{1,0:T(8,128)(2,1)S(1)}, bf16[512,512]{1,0:T(8,128)(2,1)S(1)}, u32[]{:S(2)}, u32[]{:S(2)}) %collective-permute-start.27) | collective-permute-done | bytes 524320 | tf_op jit(solution)/shard_map/ppermute | solution.py:510
  161.7 2.5 %collective-permute-done.26.refs_1_ = bf16[512,512]{1,0:T(8,128)(2,1)S(1)} collective-permute-done((bf16[512,512]{1,0:T(8,128)(2,1)S(1)}, bf16[512,512]{1,0:T(8,128)(2,1)S(1)}, u32[]{:S(2)}, u32[]{:S(2)}) %collective-permute-start.26) | collective-permute-done | bytes 524320 | tf_op jit(solution)/shard_map/ppermute | solution.py:510
  166.5 4.0 %widen.1 = (f32[16,128,512]{2,1,0:T(8,128)}, f32[16,128,512]{2,1,0:T(8,128)}) custom-call(s32[3]{0:T(128)S(1)} %copy-done.11, bf16[512,512]{1,0:T(8,128)(2,1)S(1)} %get-tuple-element.81._.refs_0_, bf16[512,512]{1,0:T(8,128)(2,1)S(1)} %collective-permute-done.26.refs_1_, bf16[512,512]{1,0:T(8,128)(2,1)S(1)} %collective-permute-done.27.refs_2_, ...), custom_call_target="tpu_custom_call" | custom-call | flops 2097152 | bytes 12582912 | tf_op jit(solution)/shard_map/widen/pallas_call | solution.py:486
  (83 shorter events, 27.6 us)
Async XLA Ops:
  0.6 17.9 %collective-permute-start.1 = (bf16[576,256]{1,0:T(8,128)(2,1)}, bf16[576,256]{1,0:T(8,128)(2,1)S(1)}, u32[]{:S(2)}, u32[]{:S(2)}) collective-permute-start(bf16[576,256]{1,0:T(8,128)(2,1)} %bitcast.9), channel_id=1, source_target_pairs={{0,4},{4,8},{8,12},{12,16},{16,20},{20,24},{24,28},{28,32},{32,36}... | collective-permute-start | bytes 884744 | tf_op jit(solution)/shard_map/ppermute | solution.py:24
  4.7 14.6 %collective-permute-start = (bf16[576,256]{1,0:T(8,128)(2,1)}, bf16[576,256]{1,0:T(8,128)(2,1)S(1)}, u32[]{:S(2)}, u32[]{:S(2)}) collective-permute-start(bf16[576,256]{1,0:T(8,128)(2,1)} %bitcast.10), channel_id=1, source_target_pairs={{0,8},{4,12},{8,16},{12,20},{16,24},{20,28},{24,32},{28,36},{32,40... | collective-permute-start | bytes 884744 | tf_op jit(solution)/shard_map/ppermute | solution.py:24
  37.1 25.9 %collective-permute-start.2 = (bf16[512,512]{1,0:T(8,128)(2,1)}, bf16[512,512]{1,0:T(8,128)(2,1)S(1)}, u32[]{:S(2)}, u32[]{:S(2)}) collective-permute-start(bf16[512,512]{1,0:T(8,128)(2,1)} %get-tuple-element.57), channel_id=1, source_target_pairs={{0,32},{4,36},{8,40},{12,44},{16,48},{20,52},{24,56},{28,60},{32,6... | collective-permute-start | bytes 1572872 | tf_op jit(solution)/shard_map/ppermute | solution.py:510
  40.1 24.1 %collective-permute-start.3 = (bf16[512,512]{1,0:T(8,128)(2,1)}, bf16[512,512]{1,0:T(8,128)(2,1)S(1)}, u32[]{:S(2)}, u32[]{:S(2)}) collective-permute-start(bf16[512,512]{1,0:T(8,128)(2,1)} %get-tuple-element.58), channel_id=1, source_target_pairs={{0,96},{4,100},{8,104},{12,108},{16,112},{20,116},{24,120},{28,124... | collective-permute-start | bytes 1572872 | tf_op jit(solution)/shard_map/ppermute | solution.py:510
  41.8 23.0 %collective-permute-start.4 = (bf16[512,512]{1,0:T(8,128)(2,1)}, bf16[512,512]{1,0:T(8,128)(2,1)S(1)}, u32[]{:S(2)}, u32[]{:S(2)}) collective-permute-start(bf16[512,512]{1,0:T(8,128)(2,1)} %get-tuple-element.59), channel_id=1, source_target_pairs={{0,64},{4,68},{8,72},{12,76},{16,80},{20,84},{24,88},{28,92},{32,9... | collective-permute-start | bytes 1572872 | tf_op jit(solution)/shard_map/ppermute | solution.py:510
  60.2 22.3 %collective-permute-start.8 = (bf16[512,512]{1,0:T(8,128)(2,1)}, bf16[512,512]{1,0:T(8,128)(2,1)S(1)}, u32[]{:S(2)}, u32[]{:S(2)}) collective-permute-start(bf16[512,512]{1,0:T(8,128)(2,1)} %get-tuple-element.66), channel_id=1, source_target_pairs={{0,8},{4,12},{8,16},{12,20},{16,24},{20,28},{24,0},{28,4},{32,40},... | collective-permute-start | bytes 1572872 | tf_op jit(solution)/shard_map/ppermute | solution.py:510
  60.7 21.8 %collective-permute-start.9 = (bf16[512,512]{1,0:T(8,128)(2,1)}, bf16[512,512]{1,0:T(8,128)(2,1)S(1)}, u32[]{:S(2)}, u32[]{:S(2)}) collective-permute-start(bf16[512,512]{1,0:T(8,128)(2,1)} %get-tuple-element.67), channel_id=1, source_target_pairs={{0,24},{4,28},{8,0},{12,4},{16,8},{20,12},{24,16},{28,20},{32,56},... | collective-permute-start | bytes 1572872 | tf_op jit(solution)/shard_map/ppermute | solution.py:510
  63.0 23.1 %collective-permute-start.10 = (bf16[512,512]{1,0:T(8,128)(2,1)}, bf16[512,512]{1,0:T(8,128)(2,1)S(1)}, u32[]{:S(2)}, u32[]{:S(2)}) collective-permute-start(bf16[512,512]{1,0:T(8,128)(2,1)} %get-tuple-element.68), channel_id=1, source_target_pairs={{0,16},{4,20},{8,24},{12,28},{16,0},{20,4},{24,8},{28,12},{32,48},... | collective-permute-start | bytes 1572872 | tf_op jit(solution)/shard_map/ppermute | solution.py:510
  88.6 9.4 %collective-permute-start.14 = (f32[288,768]{1,0:T(8,128)S(1)}, f32[288,768]{1,0:T(8,128)S(1)}, u32[]{:S(2)}, u32[]{:S(2)}) collective-permute-start(f32[288,768]{1,0:T(8,128)S(1)} %get-tuple-element.75), channel_id=1, source_target_pairs={{0,1},{1,0},{2,3},{3,2},{4,5},{5,4},{6,7},{7,6},{8,9},{9,8},{10,11... | collective-permute-start | bytes 2654216 | tf_op jit(solution)/shard_map/ppermute | solution.py:522
  90.9 6.3 %collective-permute-start.5 = (bf16[128,512]{1,0:T(8,128)(2,1)S(1)}, bf16[128,512]{1,0:T(8,128)(2,1)S(1)}, u32[]{:S(2)}, u32[]{:S(2)}) collective-permute-start(bf16[128,512]{1,0:T(8,128)(2,1)S(1)} %get-tuple-element.62), channel_id=1, source_target_pairs={{0,8},{4,12},{8,16},{12,20},{16,24},{20,28},{24,0},{28,4},{32,40},... | collective-permute-start | bytes 393224 | tf_op jit(solution)/shard_map/ppermute | solution.py:510
  91.7 7.6 %collective-permute-start.6 = (bf16[128,512]{1,0:T(8,128)(2,1)S(1)}, bf16[128,512]{1,0:T(8,128)(2,1)S(1)}, u32[]{:S(2)}, u32[]{:S(2)}) collective-permute-start(bf16[128,512]{1,0:T(8,128)(2,1)S(1)} %get-tuple-element.63), channel_id=1, source_target_pairs={{0,24},{4,28},{8,0},{12,4},{16,8},{20,12},{24,16},{28,20},{32,56},... | collective-permute-start | bytes 393224 | tf_op jit(solution)/shard_map/ppermute | solution.py:510
  93.6 5.9 %collective-permute-start.7 = (bf16[128,512]{1,0:T(8,128)(2,1)S(1)}, bf16[128,512]{1,0:T(8,128)(2,1)S(1)}, u32[]{:S(2)}, u32[]{:S(2)}) collective-permute-start(bf16[128,512]{1,0:T(8,128)(2,1)S(1)} %get-tuple-element.64), channel_id=1, source_target_pairs={{0,16},{4,20},{8,24},{12,28},{16,0},{20,4},{24,8},{28,12},{32,48},... | collective-permute-start | bytes 393224 | tf_op jit(solution)/shard_map/ppermute | solution.py:510
  93.7 5.8 %collective-permute-start.11 = (bf16[128,512]{1,0:T(8,128)(2,1)S(1)}, bf16[128,512]{1,0:T(8,128)(2,1)S(1)}, u32[]{:S(2)}, u32[]{:S(2)}) collective-permute-start(bf16[128,512]{1,0:T(8,128)(2,1)S(1)} %get-tuple-element.71), channel_id=1, source_target_pairs={{0,32},{4,36},{8,40},{12,44},{16,48},{20,52},{24,56},{28,60},{32,6... | collective-permute-start | bytes 393224 | tf_op jit(solution)/shard_map/ppermute | solution.py:510
  97.1 4.2 %collective-permute-start.12 = (bf16[128,512]{1,0:T(8,128)(2,1)S(1)}, bf16[128,512]{1,0:T(8,128)(2,1)S(1)}, u32[]{:S(2)}, u32[]{:S(2)}) collective-permute-start(bf16[128,512]{1,0:T(8,128)(2,1)S(1)} %get-tuple-element.72), channel_id=1, source_target_pairs={{0,96},{4,100},{8,104},{12,108},{16,112},{20,116},{24,120},{28,124... | collective-permute-start | bytes 393224 | tf_op jit(solution)/shard_map/ppermute | solution.py:510
  98.0 5.3 %collective-permute-start.13 = (bf16[128,512]{1,0:T(8,128)(2,1)S(1)}, bf16[128,512]{1,0:T(8,128)(2,1)S(1)}, u32[]{:S(2)}, u32[]{:S(2)}) collective-permute-start(bf16[128,512]{1,0:T(8,128)(2,1)S(1)} %get-tuple-element.73), channel_id=1, source_target_pairs={{0,64},{4,68},{8,72},{12,76},{16,80},{20,84},{24,88},{28,92},{32,9... | collective-permute-start | bytes 393224 | tf_op jit(solution)/shard_map/ppermute | solution.py:510
  103.4 12.1 %collective-permute-start.15 = (bf16[256,512]{1,0:T(8,128)(2,1)S(1)}, bf16[256,512]{1,0:T(8,128)(2,1)S(1)}, u32[]{:S(2)}, u32[]{:S(2)}) collective-permute-start(bf16[256,512]{1,0:T(8,128)(2,1)S(1)} %totals.1.mine_ref), channel_id=1, source_target_pairs={{0,4},{4,0},{8,12},{12,8},{16,20},{20,16},{24,28},{28,24},{32,36},... | collective-permute-start | bytes 786440 | tf_op jit(solution)/shard_map/ppermute | solution.py:510
  104.4 6.2 %collective-permute-start.22 = (bf16[288,256]{1,0:T(8,128)(2,1)S(1)}, bf16[288,256]{1,0:T(8,128)(2,1)S(1)}, u32[]{:S(2)}, u32[]{:S(2)}) collective-permute-start(bf16[288,256]{1,0:T(8,128)(2,1)S(1)} %get-tuple-element.79), channel_id=1, source_target_pairs={{8,0},{12,4},{16,8},{20,12},{24,16},{28,20},{32,24},{36,28},{40,32... | collective-permute-start | bytes 442376 | tf_op jit(solution)/shard_map/ppermute | solution.py:24
  105.7 7.8 %collective-permute-start.23 = (bf16[288,256]{1,0:T(8,128)(2,1)S(1)}, bf16[288,256]{1,0:T(8,128)(2,1)S(1)}, u32[]{:S(2)}, u32[]{:S(2)}) collective-permute-start(bf16[288,256]{1,0:T(8,128)(2,1)S(1)} %get-tuple-element.80), channel_id=1, source_target_pairs={{4,0},{8,4},{12,8},{16,12},{20,16},{24,20},{28,24},{32,28},{36,32}... | collective-permute-start | bytes 442376 | tf_op jit(solution)/shard_map/ppermute | solution.py:24
  113.6 8.3 %collective-permute-start.24 = (bf16[288,256]{1,0:T(8,128)(2,1)S(1)}, bf16[288,256]{1,0:T(8,128)(2,1)S(1)}, u32[]{:S(2)}, u32[]{:S(2)}) collective-permute-start(bf16[288,256]{1,0:T(8,128)(2,1)S(1)} %merge.1.own_ref), channel_id=1, source_target_pairs={{0,2},{2,0},{1,3},{3,1},{4,6},{6,4},{5,7},{7,5},{8,10},{10,8},{9,1... | collective-permute-start | bytes 442376 | tf_op jit(solution)/shard_map/ppermute | solution.py:526
  115.6 8.0 %collective-permute-start.18 = (bf16[128,512]{1,0:T(8,128)(2,1)S(1)}, bf16[128,512]{1,0:T(8,128)(2,1)S(1)}, u32[]{:S(2)}, u32[]{:S(2)}) collective-permute-start(bf16[128,512]{1,0:T(8,128)(2,1)S(1)} %get-tuple-element.77.refs_0_), channel_id=1, source_target_pairs={{0,16},{4,20},{8,24},{12,28},{16,0},{20,4},{24,8},{28,12},{32,48},... | collective-permute-start | bytes 393224 | tf_op jit(solution)/shard_map/ppermute | solution.py:510
  118.0 6.1 %collective-permute-start.17 = (bf16[128,512]{1,0:T(8,128)(2,1)S(1)}, bf16[128,512]{1,0:T(8,128)(2,1)S(1)}, u32[]{:S(2)}, u32[]{:S(2)}) collective-permute-start(bf16[128,512]{1,0:T(8,128)(2,1)S(1)} %get-tuple-element.77.refs_0_), channel_id=1, source_target_pairs={{0,24},{4,28},{8,0},{12,4},{16,8},{20,12},{24,16},{28,20},{32,56},... | collective-permute-start | bytes 393224 | tf_op jit(solution)/shard_map/ppermute | solution.py:510
  119.3 6.4 %collective-permute-start.16 = (bf16[128,512]{1,0:T(8,128)(2,1)S(1)}, bf16[128,512]{1,0:T(8,128)(2,1)S(1)}, u32[]{:S(2)}, u32[]{:S(2)}) collective-permute-start(bf16[128,512]{1,0:T(8,128)(2,1)S(1)} %get-tuple-element.77.refs_0_), channel_id=1, source_target_pairs={{0,8},{4,12},{8,16},{12,20},{16,24},{20,28},{24,0},{28,4},{32,40},... | collective-permute-start | bytes 393224 | tf_op jit(solution)/shard_map/ppermute | solution.py:510
  119.5 6.2 %collective-permute-start.21 = (bf16[128,512]{1,0:T(8,128)(2,1)S(1)}, bf16[128,512]{1,0:T(8,128)(2,1)S(1)}, u32[]{:S(2)}, u32[]{:S(2)}) collective-permute-start(bf16[128,512]{1,0:T(8,128)(2,1)S(1)} %get-tuple-element.78.refs_4_), channel_id=1, source_target_pairs={{0,64},{4,68},{8,72},{12,76},{16,80},{20,84},{24,88},{28,92},{32,9... | collective-permute-start | bytes 393224 | tf_op jit(solution)/shard_map/ppermute | solution.py:510
  121.9 4.8 %collective-permute-start.20 = (bf16[128,512]{1,0:T(8,128)(2,1)S(1)}, bf16[128,512]{1,0:T(8,128)(2,1)S(1)}, u32[]{:S(2)}, u32[]{:S(2)}) collective-permute-start(bf16[128,512]{1,0:T(8,128)(2,1)S(1)} %get-tuple-element.78.refs_4_), channel_id=1, source_target_pairs={{0,96},{4,100},{8,104},{12,108},{16,112},{20,116},{24,120},{28,124... | collective-permute-start | bytes 393224 | tf_op jit(solution)/shard_map/ppermute | solution.py:510
  123.6 5.3 %collective-permute-start.19 = (bf16[128,512]{1,0:T(8,128)(2,1)S(1)}, bf16[128,512]{1,0:T(8,128)(2,1)S(1)}, u32[]{:S(2)}, u32[]{:S(2)}) collective-permute-start(bf16[128,512]{1,0:T(8,128)(2,1)S(1)} %get-tuple-element.78.refs_4_), channel_id=1, source_target_pairs={{0,32},{4,36},{8,40},{12,44},{16,48},{20,52},{24,56},{28,60},{32,6... | collective-permute-start | bytes 393224 | tf_op jit(solution)/shard_map/ppermute | solution.py:510
  129.0 11.7 %collective-permute-start.31 = (bf16[512,512]{1,0:T(8,128)(2,1)S(1)}, bf16[512,512]{1,0:T(8,128)(2,1)S(1)}, u32[]{:S(2)}, u32[]{:S(2)}) collective-permute-start(bf16[512,512]{1,0:T(8,128)(2,1)S(1)} %get-tuple-element.84.refs_4_), channel_id=1, source_target_pairs={{0,16},{4,20},{8,24},{12,28},{16,0},{20,4},{24,8},{28,12},{32,48},... | collective-permute-start | bytes 1572872 | tf_op jit(solution)/shard_map/ppermute | solution.py:510
  130.5 8.6 %collective-permute-start.25 = (f32[288,256]{1,0:T(8,128)S(1)}, f32[288,256]{1,0:T(8,128)S(1)}, u32[]{:S(2)}, u32[]{:S(2)}) collective-permute-start(f32[288,256]{1,0:T(8,128)S(1)} %finish.1.refs_8_.mine_ref), channel_id=1, source_target_pairs={{0,1},{1,0},{2,3},{3,2},{4,5},{5,4},{6,7},{7,6},{8,9},{9,8},{10,11... | collective-permute-start | bytes 884744 | tf_op jit(solution)/shard_map/ppermute | solution.py:522
  137.1 19.2 %collective-permute-start.30 = (bf16[512,512]{1,0:T(8,128)(2,1)S(1)}, bf16[512,512]{1,0:T(8,128)(2,1)S(1)}, u32[]{:S(2)}, u32[]{:S(2)}) collective-permute-start(bf16[512,512]{1,0:T(8,128)(2,1)S(1)} %get-tuple-element.84.refs_4_), channel_id=1, source_target_pairs={{0,24},{4,28},{8,0},{12,4},{16,8},{20,12},{24,16},{28,20},{32,56},... | collective-permute-start | bytes 1572872 | tf_op jit(solution)/shard_map/ppermute | solution.py:510
  138.1 18.8 %collective-permute-start.29 = (bf16[512,512]{1,0:T(8,128)(2,1)S(1)}, bf16[512,512]{1,0:T(8,128)(2,1)S(1)}, u32[]{:S(2)}, u32[]{:S(2)}) collective-permute-start(bf16[512,512]{1,0:T(8,128)(2,1)S(1)} %get-tuple-element.84.refs_4_), channel_id=1, source_target_pairs={{0,8},{4,12},{8,16},{12,20},{16,24},{20,28},{24,0},{28,4},{32,40},... | collective-permute-start | bytes 1572872 | tf_op jit(solution)/shard_map/ppermute | solution.py:510
  138.5 18.4 %collective-permute-start.28 = (bf16[512,512]{1,0:T(8,128)(2,1)S(1)}, bf16[512,512]{1,0:T(8,128)(2,1)S(1)}, u32[]{:S(2)}, u32[]{:S(2)}) collective-permute-start(bf16[512,512]{1,0:T(8,128)(2,1)S(1)} %get-tuple-element.81._.refs_0_), channel_id=1, source_target_pairs={{0,64},{4,68},{8,72},{12,76},{16,80},{20,84},{24,88},{28,92},{32,9... | collective-permute-start | bytes 1572872 | tf_op jit(solution)/shard_map/ppermute | solution.py:510
  139.2 22.6 %collective-permute-start.27 = (bf16[512,512]{1,0:T(8,128)(2,1)S(1)}, bf16[512,512]{1,0:T(8,128)(2,1)S(1)}, u32[]{:S(2)}, u32[]{:S(2)}) collective-permute-start(bf16[512,512]{1,0:T(8,128)(2,1)S(1)} %get-tuple-element.81._.refs_0_), channel_id=1, source_target_pairs={{0,96},{4,100},{8,104},{12,108},{16,112},{20,116},{24,120},{28,124... | collective-permute-start | bytes 1572872 | tf_op jit(solution)/shard_map/ppermute | solution.py:510
  140.7 23.5 %collective-permute-start.26 = (bf16[512,512]{1,0:T(8,128)(2,1)S(1)}, bf16[512,512]{1,0:T(8,128)(2,1)S(1)}, u32[]{:S(2)}, u32[]{:S(2)}) collective-permute-start(bf16[512,512]{1,0:T(8,128)(2,1)S(1)} %get-tuple-element.81._.refs_0_), channel_id=1, source_target_pairs={{0,32},{4,36},{8,40},{12,44},{16,48},{20,52},{24,56},{28,60},{32,6... | collective-permute-start | bytes 1572872 | tf_op jit(solution)/shard_map/ppermute | solution.py:510
  (16 other events, 403.7 us)

commit v4 on v3

--- a/solution.py
+++ b/solution.py
@@ -23,6 +23,19 @@
     route = [(i - distance, i) for i in devices if i - distance in devices]
     return lax.ppermute(block, axis, route)
 
+TOKEN = jax.ShapeDtypeStruct((8, 128), jnp.float32)
+WHOLE = pl.BlockSpec(memory_space=pltpu.VMEM)
+TOKEN_BLOCK = pl.BlockSpec((8, 128), lambda *_: (0, 0))
+
+
+def with_token(kernel, scratch=0):
+    def wrapped(*refs):
+        end = len(refs) - scratch
+        refs[end - 1][...] = jnp.zeros(TOKEN.shape, TOKEN.dtype)
+        kernel(*refs[: end - 1], *refs[end:])
+
+    return wrapped
+
 
 def dot(a, b):
     return lax.dot_general(a, b, (((1,), (0,)), ((), ())), preferred_element_type=jnp.float32)
@@ -37,16 +50,18 @@
     value = wuv_ref.shape[1]
     width = query_ref.shape[1] // wuk_ref.shape[0]
     rank = wuk_ref.shape[2]
+    toks = query_ref.shape[0]
     query_t = query_ref[...].T
     dout_t = dout_ref[...].T
     for n in range(wuk_ref.shape[0]):
         q_nope = query_t[n * width : n * width + nope]
         grads = dout_t[n * value : (n + 1) * value]
-        nope_t_ref[n] = q_nope
-        dout_t_ref[n] = grads
-        qfull_ref[n, :rank] = dot(wuk_ref[n].T, q_nope).astype(jnp.bfloat16)
-        qfull_ref[n, rank:] = query_t[n * width + nope : (n + 1) * width]
-        dlo_ref[n] = dot(wuv_ref[n].T, grads).astype(jnp.bfloat16)
+        span = slice(n * toks, (n + 1) * toks)
+        nope_t_ref[:, span] = q_nope
+        dout_t_ref[:, span] = grads
+        qfull_ref[:rank, span] = dot(wuk_ref[n].T, q_nope).astype(jnp.bfloat16)
+        qfull_ref[rank:, span] = query_t[n * width + nope : (n + 1) * width]
+        dlo_ref[:, span] = dot(wuv_ref[n].T, grads).astype(jnp.bfloat16)
 
 
 def prepare(query, d_out, w_uk, w_uv):
@@ -55,8 +70,8 @@
     value = w_uv.shape[1]
     width = query.shape[1] // heads
     lat = rank + width - nope
-    shape = lambda rows: jax.ShapeDtypeStruct((heads, rows, toks), jnp.bfloat16)
-    block = lambda rows: pl.BlockSpec((GROUP, rows, toks), lambda s: (s, 0, 0))
+    shape = lambda rows: jax.ShapeDtypeStruct((rows, heads * toks), jnp.bfloat16)
+    block = lambda rows: pl.BlockSpec((rows, GROUP * toks), lambda s: (0, s))
     return pl.pallas_call(
         prepare_kernel,
         grid=(heads // GROUP,),
@@ -90,14 +105,14 @@
     *rest,
 ):
     probs_ref, dscore_ref, lout_ref, dfull_ref, *slab_refs, grad_ref, keys_ref, keys_t_ref, bias_ref = rest[-12:]
-    rank = dlo_ref.shape[1]
-    group = range(qfull_ref.shape[0])
+    rank = dlo_ref.shape[0]
+    toks = block_refs[0].shape[1]
+    group = range(qfull_ref.shape[1] // toks)
     step = pl.program_id(0)
 
     @pl.when(step == 0)
     def _():
         for n, block_ref in enumerate(block_refs):
-            toks = block_ref.shape[1]
             keys_t_ref[:, n * toks : (n + 1) * toks] = block_ref[...]
             keys_ref[n * toks : (n + 1) * toks] = block_ref[...].T
         position = place_ref[0]
@@ -116,28 +131,30 @@
                 allowed &= jnp.broadcast_to(position, (toks, toks)) >= distance
             bias_ref[n * toks : (n + 1) * toks] = jnp.where(allowed, 0.0, -jnp.inf)
 
-    scores = [dot(keys_ref[...], qfull_ref[n]) for n in group]
+    def slab(n):
+        return (step * (len(group) // 2) + n // 2 + 4 - place_ref[which]) % 4
+
+    part = lambda ref, n: ref[:, n * toks : (n + 1) * toks]
+    scores = dot(keys_ref[...], qfull_ref[...])
     probs = []
     for n in group:
-        scaled = scores[n] * (inv_root * LOG2E) + bias_ref[...]
+        scaled = scores[:, n * toks : (n + 1) * toks] * (inv_root * LOG2E) + bias_ref[...]
         weights = jnp.exp2(scaled - jnp.max(scaled, axis=0, keepdims=True))
         probs.append(weights * (1.0 / jnp.sum(weights, axis=0, keepdims=True)))
-        probs_ref[n] = probs[n].astype(jnp.bfloat16)
-    d_probs = [dot(keys_ref[:, :rank], dlo_ref[n]) for n in group]
+        probs_ref[:, n * toks : (n + 1) * toks] = probs[n].astype(jnp.bfloat16)
+    d_probs = dot(keys_ref[:, :rank], dlo_ref[...])
+    lout_ref[...] = dot(keys_t_ref[:rank], probs_ref[...]).astype(jnp.bfloat16)
     for n in group:
-        lout_ref[n] = dot(keys_t_ref[:rank], probs_ref[n]).astype(jnp.bfloat16)
+        d_prob = d_probs[:, n * toks : (n + 1) * toks]
+        delta = jnp.sum(probs[n] * d_prob, axis=0, keepdims=True)
+        d_score = probs[n] * (d_prob - delta) * inv_root
+        dscore_ref[:, n * toks : (n + 1) * toks] = d_score.astype(jnp.bfloat16)
     for n in group:
-        delta = jnp.sum(probs[n] * d_probs[n], axis=0, keepdims=True)
-        dscore_ref[n] = (probs[n] * (d_probs[n] - delta) * inv_root).astype(jnp.bfloat16)
-    def slab(n):
-        return (step * (len(group) // 2) + n // 2 + 4 - place_ref[which]) % 4
-
+        grad_ref[slab(n), n % 2, 1] = dot_nt(part(dout_t_ref, n), part(lout_ref, n)).astype(jnp.bfloat16)
+    dfull_ref[...] = dot(keys_t_ref[...], dscore_ref[...]).astype(jnp.bfloat16)
     for n in group:
-        grad_ref[slab(n), n % 2, 1] = dot_nt(dout_t_ref[n], lout_ref[n]).astype(jnp.bfloat16)
-    for n in group:
-        dfull_ref[n] = dot(keys_t_ref[...], dscore_ref[n]).astype(jnp.bfloat16)
-    for n in group:
-        grad_ref[slab(n), n % 2, 0] = dot_nt(nope_t_ref[n], dfull_ref[n, :rank]).astype(jnp.bfloat16)
+        d_absorbed = dfull_ref[:rank, n * toks : (n + 1) * toks]
+        grad_ref[slab(n), n % 2, 0] = dot_nt(part(nope_t_ref, n), d_absorbed).astype(jnp.bfloat16)
 
     @pl.when(step == pl.num_programs(0) - 1)
     def _():
@@ -146,16 +163,17 @@
 
 
 def score(which, place, block_mask, segments, blocks, qfull, dlo, dout_t, nope_t, inv_root, start, count, carried):
-    heads, lat, toks = qfull.shape
+    lat, toks = blocks[0].shape
+    heads = qfull.shape[1] // toks
     span = len(blocks) * toks
-    rank = dlo.shape[1]
-    value, nope = dout_t.shape[1], nope_t.shape[1]
+    rank = dlo.shape[0]
+    value, nope = dout_t.shape[0], nope_t.shape[0]
     base = start // GROUP
     whole = lambda rows, cols: pl.BlockSpec((rows, cols), lambda s: (0, 0))
-    heads_of = lambda rows: pl.BlockSpec((GROUP, rows, toks), lambda s: (s + base, 0, 0))
-    out = lambda rows: jax.ShapeDtypeStruct((heads, rows, toks), jnp.bfloat16)
-    return pl.pallas_call(
-        functools.partial(score_kernel, inv_root, which),
+    heads_of = lambda rows: pl.BlockSpec((rows, GROUP * toks), lambda s: (0, s + base))
+    out = lambda rows: jax.ShapeDtypeStruct((rows, heads * toks), jnp.bfloat16)
+    return pl.pallas_call(
+        with_token(functools.partial(score_kernel, inv_root, which), 4),
         grid=(count // GROUP,),
         in_specs=[
             pl.BlockSpec(memory_space=pltpu.SMEM),
@@ -174,14 +192,16 @@
             heads_of(rank),
             heads_of(lat),
         ]
-        + [whole(4 * nope, rank)] * len(HOPS),
+        + [whole(4 * nope, rank)] * len(HOPS)
+        + [TOKEN_BLOCK],
         out_shape=[
             out(span),
             out(span),
             out(rank),
             out(lat),
         ]
-        + [jax.ShapeDtypeStruct((4 * nope, rank), jnp.bfloat16)] * len(HOPS),
+        + [jax.ShapeDtypeStruct((4 * nope, rank), jnp.bfloat16)] * len(HOPS)
+        + [TOKEN],
         input_output_aliases={7 + len(blocks) + n: n for n in range(len(carried))},
         scratch_shapes=[
             pltpu.VMEM((4, 2, 2, nope, rank), jnp.bfloat16),
@@ -189,7 +209,7 @@
             pltpu.VMEM((lat, span), jnp.bfloat16),
             pltpu.VMEM((span, toks), jnp.float32),
         ],
-        compiler_params=pltpu.CompilerParams(vmem_limit_bytes=LARGE),
+        compiler_params=pltpu.CompilerParams(vmem_limit_bytes=56 * MIB),
         cost_estimate=pl.CostEstimate(
             flops=8 * count * toks * span * (rank + lat),
             bytes_accessed=3 * count * 2**20,
@@ -200,33 +220,27 @@
 
 
 def key_kernel(qfull_ref, dlo_ref, probs_ref, dscore_ref, _, total_ref):
-    rank = dlo_ref.shape[1]
+    rank = dlo_ref.shape[0]
 
     @pl.when(pl.program_id(0) == 0)
     def _():
         total_ref[...] = jnp.zeros_like(total_ref)
 
-    content = 0.0
-    rope = 0.0
-    for n in range(qfull_ref.shape[0]):
-        content += dot_nt(qfull_ref[n, :rank], dscore_ref[n]) + dot_nt(dlo_ref[n], probs_ref[n])
-        rope += dot_nt(qfull_ref[n, rank:], dscore_ref[n])
-    total_ref[:rank] += content
-    total_ref[rank:] += rope
-
-
-def key_gradient(qfull, dlo, probs, dscore, after):
-    heads, lat, toks = qfull.shape
-    rank = dlo.shape[1]
-    span = probs.shape[1]
-    heads_of = lambda rows: pl.BlockSpec((GROUP, rows, toks), lambda s: (s, 0, 0))
-    return pl.pallas_call(
-        key_kernel,
+    total_ref[:rank] += dot_nt(qfull_ref[:rank], dscore_ref[...]) + dot_nt(dlo_ref[...], probs_ref[...])
+    total_ref[rank:] += dot_nt(qfull_ref[rank:], dscore_ref[...])
+
+
+def key_gradient(qfull, dlo, probs, dscore, toks, after):
+    lat, rank, span = qfull.shape[0], dlo.shape[0], probs.shape[0]
+    heads = qfull.shape[1] // toks
+    heads_of = lambda rows: pl.BlockSpec((rows, GROUP * toks), lambda s: (0, s))
+    return pl.pallas_call(
+        with_token(key_kernel),
         grid=(heads // GROUP,),
         in_specs=[heads_of(lat), heads_of(rank), heads_of(span), heads_of(span)]
         + [pl.BlockSpec(memory_space=pl.ANY)],
-        out_specs=pl.BlockSpec((lat, span), lambda s: (0, 0)),
-        out_shape=jax.ShapeDtypeStruct((lat, span), jnp.float32),
+        out_specs=[pl.BlockSpec((lat, span), lambda s: (0, 0)), TOKEN_BLOCK],
+        out_shape=[jax.ShapeDtypeStruct((lat, span), jnp.float32), TOKEN],
         compiler_params=pltpu.CompilerParams(vmem_limit_bytes=LARGE),
         cost_estimate=pl.CostEstimate(
             flops=4 * heads * toks * span * (rank + lat), bytes_accessed=24 * MIB, transcendentals=0
@@ -246,8 +260,8 @@
     rows, span = keep.shape
     out = lambda dtype: jax.ShapeDtypeStruct((rows, toks), dtype)
     return pl.pallas_call(
-        split_kernel,
-        out_shape=[out(jnp.float32)] + [out(jnp.bfloat16)] * SPAN,
+        with_token(split_kernel),
+        out_shape=[out(jnp.float32)] + [out(jnp.bfloat16)] * SPAN + [TOKEN],
         compiler_params=pltpu.CompilerParams(vmem_limit_bytes=12 * MIB),
         cost_estimate=BRIEF,
         name="split",
@@ -278,8 +292,8 @@
 
 def finish(own, far):
     return pl.pallas_call(
-        finish_kernel,
-        out_shape=jax.ShapeDtypeStruct(own.shape, jnp.float32),
+        with_token(finish_kernel),
+        out_shape=[jax.ShapeDtypeStruct(own.shape, jnp.float32), TOKEN],
         compiler_params=pltpu.CompilerParams(vmem_limit_bytes=12 * MIB),
         cost_estimate=BRIEF,
         name="finish",
@@ -297,10 +311,10 @@
     rows, toks = mine.shape
     whole = pl.BlockSpec(memory_space=pltpu.VMEM)
     return pl.pallas_call(
-        assemble_kernel,
+        with_token(assemble_kernel),
         in_specs=[pl.BlockSpec(memory_space=pltpu.SMEM), whole, whole],
-        out_specs=whole,
-        out_shape=jax.ShapeDtypeStruct((2 * rows, toks), jnp.float32),
+        out_specs=[whole] * 2,
+        out_shape=[jax.ShapeDtypeStruct((2 * rows, toks), jnp.float32), TOKEN],
         compiler_params=pltpu.CompilerParams(vmem_limit_bytes=12 * MIB),
         cost_estimate=BRIEF,
         name="assemble",
@@ -308,34 +322,38 @@
 
 
 def project_kernel(lout_ref, dfull_ref, wuk_ref, wuv_ref, _, att_ref, dq_ref):
-    group = range(lout_ref.shape[0])
-    rank = lout_ref.shape[1]
+    group = range(wuk_ref.shape[0])
+    rank = lout_ref.shape[0]
+    toks = att_ref.shape[0]
     value = wuv_ref.shape[1]
     width = dq_ref.shape[1] // len(group)
     for n in group:
-        attended = dot(wuv_ref[n], lout_ref[n]).astype(jnp.bfloat16)
+        attended = dot(wuv_ref[n], lout_ref[:, n * toks : (n + 1) * toks]).astype(jnp.bfloat16)
         att_ref[:, n * value : (n + 1) * value] = attended.T
-        d_nope = dot(wuk_ref[n], dfull_ref[n, :rank]).astype(jnp.bfloat16)
-        dq_ref[:, n * width : (n + 1) * width] = jnp.concatenate([d_nope, dfull_ref[n, rank:]], axis=0).T
+        d_full = dfull_ref[:, n * toks : (n + 1) * toks]
+        d_nope = dot(wuk_ref[n], d_full[:rank]).astype(jnp.bfloat16)
+        dq_ref[:, n * width : (n + 1) * width] = jnp.concatenate([d_nope, d_full[rank:]], axis=0).T
 
 
 def project(lout, dfull, w_uk, w_uv, after):
-    heads, lat, toks = dfull.shape
-    nope, rank = w_uk.shape[1:]
+    heads, nope, rank = w_uk.shape
+    lat, toks = dfull.shape[0], dfull.shape[1] // heads
     value = w_uv.shape[1]
     width = nope + lat - rank
     heads_of = lambda rows, cols: pl.BlockSpec((GROUP, rows, cols), lambda s: (s, 0, 0))
+    wide = lambda rows: pl.BlockSpec((rows, GROUP * toks), lambda s: (0, s))
     out = lambda cols: jax.ShapeDtypeStruct((toks, heads * cols), jnp.bfloat16)
     return pl.pallas_call(
-        project_kernel,
+        with_token(project_kernel),
         grid=(heads // GROUP,),
-        in_specs=[heads_of(rank, toks), heads_of(lat, toks), heads_of(nope, rank), heads_of(value, rank)]
+        in_specs=[wide(rank), wide(lat), heads_of(nope, rank), heads_of(value, rank)]
         + [pl.BlockSpec(memory_space=pl.ANY)],
         out_specs=[
             pl.BlockSpec((toks, GROUP * value), lambda s: (0, s)),
             pl.BlockSpec((toks, GROUP * width), lambda s: (0, s)),
+            TOKEN_BLOCK,
         ],
-        out_shape=[out(value), out(width)],
+        out_shape=[out(value), out(width), TOKEN],
         compiler_params=pltpu.CompilerParams(vmem_limit_bytes=16 * MIB),
         cost_estimate=BRIEF,
         name="project",
@@ -357,12 +375,12 @@
     whole = pl.BlockSpec(memory_space=pltpu.VMEM)
     rows, cols = slabs[0].shape
     return pl.pallas_call(
-        functools.partial(reduce_kernel, which),
+        with_token(functools.partial(reduce_kernel, which)),
         in_specs=[pl.BlockSpec(memory_space=pltpu.SMEM)]
         + [whole] * len(slabs)
         + [pl.BlockSpec(memory_space=pl.ANY)],
-        out_specs=[whole] * 4,
-        out_shape=[jax.ShapeDtypeStruct((rows // 4, cols), jnp.bfloat16)] * 4,
+        out_specs=[whole] * 5,
+        out_shape=[jax.ShapeDtypeStruct((rows // 4, cols), jnp.bfloat16)] * 4 + [TOKEN],
         compiler_params=pltpu.CompilerParams(vmem_limit_bytes=16 * MIB),
         cost_estimate=BRIEF,
         name="reduced",
@@ -448,28 +466,27 @@
     whole = pl.BlockSpec(memory_space=pltpu.VMEM)
     rows, cols = first[0].shape
     return pl.pallas_call(
-        stack_kernel,
+        with_token(stack_kernel),
         in_specs=[whole] * 2 * len(first) + [pl.BlockSpec(memory_space=pl.ANY)],
-        out_specs=[whole, whole],
-        out_shape=[jax.ShapeDtypeStruct((len(first) * rows, cols), first[0].dtype)] * 2,
+        out_specs=[whole] * 3,
+        out_shape=[jax.ShapeDtypeStruct((len(first) * rows, cols), first[0].dtype)] * 2 + [TOKEN],
         compiler_params=pltpu.CompilerParams(vmem_limit_bytes=16 * MIB),
         cost_estimate=BRIEF,
         name="stack",
     )(*first, *second, after)
 
 
-def widen_kernel(place_ref, *refs):
-    *slab_refs, _, _, uk_ref, uv_ref, wide_ref, sems = refs
+def widen_kernel(chunk, place_ref, *refs):
+    slab_refs = refs[: len(HOPS)]
+    uk_ref, uv_ref, wide_ref, sems = refs[-4:]
     rows = slab_refs[0].shape[0] // len(HOPS)
+    outer, inner = place_ref[1 + chunk], place_ref[2 - chunk]
     copies = []
     for n, slab_ref in enumerate(slab_refs):
-        chunk, hop = n // len(HOPS), HOPS[n % len(HOPS)]
-        outer, inner = place_ref[1 + chunk], place_ref[2 - chunk]
-        for m, inner_hop in enumerate(HOPS):
-            source = (inner - inner_hop + 4) % 4
-            piece = slab_ref[m * rows : (m + 1) * rows].astype(jnp.float32)
-            wide_ref[n, source % 2, source // 2] = piece
-        head = 2 * (4 * chunk + (outer - hop + 4) % 4)
+        for m, hop in enumerate(HOPS):
+            source = (inner - hop + 4) % 4
+            wide_ref[n, source % 2, source // 2] = slab_ref[m * rows : (m + 1) * rows].astype(jnp.float32)
+        head = 2 * (4 * chunk + (outer - HOPS[n] + 4) % 4)
         for kind, out_ref in enumerate((uk_ref, uv_ref)):
             copy = pltpu.make_async_copy(wide_ref.at[n, kind], out_ref.at[pl.ds(head, 2)], sems.at[n, kind])
             copy.start()
@@ -478,26 +495,26 @@
         copy.wait()
 
 
-def widen(place, slabs, heads, height, after):
+def widen(chunk, place, slabs, heads, height, after, carried):
     cols = slabs[0].shape[1]
-    whole = pl.BlockSpec(memory_space=pltpu.VMEM)
     somewhere = pl.BlockSpec(memory_space=pl.ANY)
     out = jax.ShapeDtypeStruct((heads, height, cols), jnp.float32)
     return pl.pallas_call(
-        widen_kernel,
+        functools.partial(widen_kernel, chunk),
         in_specs=[pl.BlockSpec(memory_space=pltpu.SMEM)]
-        + [whole] * len(slabs)
-        + [somewhere] * len(after),
+        + [WHOLE] * len(slabs)
+        + [somewhere] * (1 + len(carried)),
         out_specs=[somewhere] * 2,
         out_shape=[out, out],
+        input_output_aliases={2 + len(slabs) + n: n for n in range(len(carried))},
         scratch_shapes=[
             pltpu.VMEM((len(slabs), 2, 2, height, cols), jnp.float32),
             pltpu.SemaphoreType.DMA((len(slabs), 2)),
         ],
-        compiler_params=pltpu.CompilerParams(vmem_limit_bytes=20 * MIB),
-        cost_estimate=pl.CostEstimate(flops=2**21, bytes_accessed=12 * MIB, transcendentals=0),
+        compiler_params=pltpu.CompilerParams(vmem_limit_bytes=12 * MIB),
+        cost_estimate=BRIEF,
         name="widen",
-    )(place, *slabs, *after)
+    )(place, *slabs, after, *carried)
 
 
 def moved(block, along, back, far):
@@ -559,23 +576,24 @@
             carried,
         )
         carried = outputs[:4]
-        slabs.append(outputs[4:])
+        slabs.append(outputs[4:8])
+        token = outputs[8]
     probs, dscore, lout, dfull = carried
     first, second = slabs
-    first = reduced(2, place, [first[0]] + along_x(first[1:]), probs)
-    total = key_gradient(qfull, dlo, probs, dscore, first[0])
-    second = reduced(1, place, [second[0]] + along_z(second[1:]), total)
-    keep, send = cut(core, total, second[0])
-    own, *parts = split(keep, swap_core(send), toks)
-    mine = totals([first[0]] + along_z(first[1:]), [second[0]] + along_x(second[1:]), own)
+    *first, token = reduced(2, place, [first[0]] + along_x(first[1:]), token)
+    total, token = key_gradient(qfull, dlo, probs, dscore, toks, token)
+    *second, token = reduced(1, place, [second[0]] + along_z(second[1:]), token)
+    keep, send = cut(core, total, token)
+    own, *parts, token = split(keep, swap_core(send), toks)
+    mine = totals([first[0]] + along_z(first[1:]), [second[0]] + along_x(second[1:]), token)
     low = merge(own, [shifted(parts[part], "ctx", part - SPAN) for part in range(SPAN)])
     first, second = pair_up(mine, moved(mine, 0, 0, 1))
-    half = finish(low, swap_far(low))
-    first, second = stack([first] + along_z([first] * 3), [second] + along_x([second] * 3), half)
-    attended, d_query = project(lout, dfull, w_uk, w_uv, first)
-    d_latent_t = assemble(core, half, swap_core(half))
-    slabs = [first] + along_x([first] * 3) + [second] + along_z([second] * 3)
-    d_w_uk, d_w_uv = widen(place, slabs, heads, nope, (attended, d_latent_t))
+    half, token = finish(low, swap_far(low))
+    d_latent_t, token = assemble(core, half, swap_core(half))
+    first, second, token = stack([first] + along_z([first] * 3), [second] + along_x([second] * 3), token)
+    attended, d_query, token = project(lout, dfull, w_uk, w_uv, token)
+    grads = widen(0, place, [first] + along_x([first] * 3), heads, nope, token, [])
+    d_w_uk, d_w_uv = widen(1, place, [second] + along_z([second] * 3), heads, nope, token, grads)
     return attended, d_query, d_latent_t.T, d_w_uk, d_w_uv
 
 

time: 172 us -> 170 us (0.988)
  waiting for transfers between devices: 42.1 us -> 34.6 us
  starting transfers between devices: 51.1 us -> 57.8 us
  local copies, waits for them, and re-layouts: 9.34 us -> 5.98 us
  Pallas kernels: 66.5 us -> 69.8 us
    ppermute x25, starting transfers between devices: 30 us -> 38.9 us  [moved(): return lax.ppermute(block, 'ctx', route)]
    ppermute x4, waiting for transfers between devices: 7.21 us -> 0.52 us  [shifted(): return lax.ppermute(block, axis, route)]
    ppermute x25, waiting for transfers between devices: 34.9 us -> 31.4 us  [moved(): return lax.ppermute(block, 'ctx', route)]
    unnamed x32 -> x28, local copies, waits for them, and re-layouts: 7.97 us -> 4.6 us
    pallas_call x11 -> x12, Pallas kernels: 57.8 us -> 61 us  [the longest x2 34.7 us: score(): pl.pallas_call(with_token(functools.partial(score_kernel, inv_root, which...]
    ppermute x2, starting transfers between devices: 8.86 us -> 6.03 us  [swap_core(): return lax.ppermute(block, 'head', [(0, 1), (1, 0), (2, 3), (3, 2)])]
    ppermute x2, waiting for transfers between devices: 0.01 us -> 2.06 us  [swap_core(): return lax.ppermute(block, 'head', [(0, 1), (1, 0), (2, 3), (3, 2)])]
  transfers between devices with their start and end apart: 32 -> 32, of which waited for: 16 -> 15; matrix products, arithmetic and copies ran while one was open for 1% -> 1% of each run, Pallas kernels for 26% -> 29%
where the time goes in v4:
time: 170 us
  Pallas kernels  69.8 us (41%)
  starting transfers between devices  57.8 us (34%)
  waiting for transfers between devices  34.6 us (20%)
  local copies, waits for them, and re-layouts  5.98 us (4%)
    ppermute x25, starting transfers between devices, moved(): return lax.ppermute(block, 'ctx', route)  38.9 us
    pallas_call x2, Pallas kernels, score(): pl.pallas_call(with_token(functools.partial(score_kernel, inv_root, which...  34.7 us
    ppermute x25, waiting for transfers between devices, moved(): return lax.ppermute(block, 'ctx', route)  31.4 us
    pallas_call x1, Pallas kernels, key_gradient(): pl.pallas_call(with_token(key_kernel), grid=(heads // GROUP,), in_specs=[...  13.6 us
    ppermute x4, starting transfers between devices, shifted(): return lax.ppermute(block, axis, route)  10.2 us
    pallas_call x1, Pallas kernels, prepare(): pl.pallas_call(prepare_kernel, grid=(heads // GROUP,), in_specs=[pl.Block...  8.43 us
    ppermute x2, starting transfers between devices, swap_core(): return lax.ppermute(block, 'head', [(0, 1), (1, 0), (2, 3), (3, 2)])  6.03 us
    pallas_call x2, Pallas kernels, widen(): pl.pallas_call(functools.partial(widen_kernel, chunk), in_specs=[pl.Block...  5.41 us
  transfers between devices with their start and end apart: 32, of which 15 were waited for; matrix products, arithmetic and copies ran while one was open for 1% of the time, Pallas kernels for 29%

profile of v4, /device:TPU:1, one launch (start us, length us, event | category | flops | bytes accessed | tf_op | source)
XLA Modules:
  0.0 169.9 jit_solution(10634759236082754563)
XLA Ops:
  0.6 4.0 %collective-permute-start.1 = (bf16[576,256]{1,0:T(8,128)(2,1)}, bf16[576,256]{1,0:T(8,128)(2,1)S(1)}, u32[]{:S(2)}, u32[]{:S(2)}) collective-permute-start(bf16[576,256]{1,0:T(8,128)(2,1)} %bitcast.9), channel_id=1, source_target_pairs={{0,4},{4,8},{8,12},{12,16},{16,20},{20,24},{24,28},{28,32},{32,36}... | collective-permute-start | bytes 884744 | tf_op jit(solution)/shard_map/ppermute | solution.py:24
  4.7 3.5 %collective-permute-start = (bf16[576,256]{1,0:T(8,128)(2,1)}, bf16[576,256]{1,0:T(8,128)(2,1)S(1)}, u32[]{:S(2)}, u32[]{:S(2)}) collective-permute-start(bf16[576,256]{1,0:T(8,128)(2,1)} %bitcast.10), channel_id=1, source_target_pairs={{0,8},{4,12},{8,16},{12,20},{16,24},{20,28},{24,32},{28,36},{32,40... | collective-permute-start | bytes 884744 | tf_op jit(solution)/shard_map/ppermute | solution.py:24
  9.7 8.4 %prepare.1 = (bf16[576,4096]{1,0:T(8,128)(2,1)}, bf16[512,4096]{1,0:T(8,128)(2,1)}, bf16[128,4096]{1,0:T(8,128)(2,1)}, bf16[128,4096]{1,0:T(8,128)(2,1)}) custom-call(bf16[256,3072]{1,0:T(8,128)(2,1)} %query_ref.1, bf16[256,2048]{1,0:T(8,128)(2,1)} %dout_ref.1, bf16[16,128,512]{2,1,0:T(8,128)(2,1)} %refs_2_.1, bf16[16,128,512]{2,1,0:T(8,128)(2,1)} %refs_3_.1), custom_call_target="tpu_custom_call" | custom-call | flops 1073741824 | bytes 16777216 | tf_op jit(solution)/shard_map/prepare/pallas_call | solution.py:75
  20.0 17.3 %score.2 = (bf16[768,4096]{1,0:T(8,128)(2,1)}, bf16[768,4096]{1,0:T(8,128)(2,1)}, bf16[512,4096]{1,0:T(8,128)(2,1)}, bf16[576,4096]{1,0:T(8,128)(2,1)}, bf16[512...) custom-call(s32[3]{0:T(128)} %pad_add_fusion.refs_0_.place_ref, ...), custom_call_target="tpu_custom_call" | custom-call | flops 13690208256 | bytes 25165824 | tf_op jit(solution)/shard_map/score/pallas_call | solution.py:175
  37.3 3.0 %collective-permute-start.2 = (bf16[512,512]{1,0:T(8,128)(2,1)}, bf16[512,512]{1,0:T(8,128)(2,1)S(1)}, u32[]{:S(2)}, u32[]{:S(2)}) collective-permute-start(bf16[512,512]{1,0:T(8,128)(2,1)} %get-tuple-element.70), channel_id=1, source_target_pairs={{0,32},{4,36},{8,40},{12,44},{16,48},{20,52},{24,56},{28,60},{32,6... | collective-permute-start | bytes 1572872 | tf_op jit(solution)/shard_map/ppermute | solution.py:527
  43.3 17.3 %score.3 = (bf16[768,4096]{1,0:T(8,128)(2,1)}, bf16[768,4096]{1,0:T(8,128)(2,1)}, bf16[512,4096]{1,0:T(8,128)(2,1)}, bf16[576,4096]{1,0:T(8,128)(2,1)}, bf16[512...) custom-call(s32[3]{0:T(128)} %pad_add_fusion.refs_0_.place_ref, ...), custom_call_target="tpu_custom_call", output_to_operand_aliasing={{0}: (10, {}), {1}: (11, {}), {2}: (12, {}), {3}: (13, {})} | custom-call | flops 13690208256 | bytes 25165824 | tf_op jit(solution)/shard_map/score/pallas_call | solution.py:175
  61.1 2.3 %collective-permute-start.9 = (bf16[512,512]{1,0:T(8,128)(2,1)}, bf16[512,512]{1,0:T(8,128)(2,1)S(1)}, u32[]{:S(2)}, u32[]{:S(2)}) collective-permute-start(bf16[512,512]{1,0:T(8,128)(2,1)} %get-tuple-element.80), channel_id=1, source_target_pairs={{0,24},{4,28},{8,0},{12,4},{16,8},{20,12},{24,16},{28,20},{32,56},... | collective-permute-start | bytes 1572872 | tf_op jit(solution)/shard_map/ppermute | solution.py:527
  67.1 13.6 %key_gradient.1 = (f32[576,768]{1,0:T(8,128)}, f32[8,128]{1,0:T(8,128)}) custom-call(bf16[576,4096]{1,0:T(8,128)(2,1)} %get-tuple-element.59.refs_4_.refs_0_, bf16[512,4096]{1,0:T(8,128)(2,1)} %get-tuple-element.60.refs_5_.refs_1_, bf16[768,4096]{1,0:T(8,128)(2,1)} %get-tuple-element.82.refs_2_, bf16[768,4096]{1,0:T(8,128)(2,1)} %get-tuple-element.83.refs_3_, ...), custom_call_target="tpu_custom_call" | custom-call | flops 13690208256 | bytes 25165824 | tf_op jit(solution)/shard_map/key_gradient/pallas_call | solution.py:237
  80.7 5.8 %collective-permute-done.10.refs_4_ = bf16[512,512]{1,0:T(8,128)(2,1)S(1)} collective-permute-done((bf16[512,512]{1,0:T(8,128)(2,1)}, bf16[512,512]{1,0:T(8,128)(2,1)S(1)}, u32[]{:S(2)}, u32[]{:S(2)}) %collective-permute-start.10) | collective-permute-done | bytes 524320 | tf_op jit(solution)/shard_map/ppermute | solution.py:527
  88.0 1.9 %copy-done.3 = f32[576,768]{1,0:T(8,128)S(1)} copy-done((f32[576,768]{1,0:T(8,128)S(1)}, f32[576,768]{1,0:T(8,128)}, u32[]{:S(2)}) %copy-start.3) | copy-done | bytes 1769496
  90.0 2.3 %collective-permute-start.14 = (f32[288,768]{1,0:T(8,128)S(1)}, f32[288,768]{1,0:T(8,128)S(1)}, u32[]{:S(2)}, u32[]{:S(2)}) collective-permute-start(f32[288,768]{1,0:T(8,128)S(1)} %get-tuple-element.93), channel_id=1, source_target_pairs={{0,1},{1,0},{2,3},{3,2},{4,5},{5,4},{6,7},{7,6},{8,9},{9,8},{10,11... | collective-permute-start | bytes 2654216 | tf_op jit(solution)/shard_map/ppermute | solution.py:539
  92.4 2.1 %collective-permute-done.14.refs_1_ = f32[288,768]{1,0:T(8,128)S(1)} collective-permute-done((f32[288,768]{1,0:T(8,128)S(1)}, f32[288,768]{1,0:T(8,128)S(1)}, u32[]{:S(2)}, u32[]{:S(2)}) %collective-permute-start.14) | collective-permute-done | bytes 884768 | tf_op jit(solution)/shard_map/ppermute | solution.py:539
  97.2 2.8 %collective-permute-start.5 = (bf16[128,512]{1,0:T(8,128)(2,1)S(1)}, bf16[128,512]{1,0:T(8,128)(2,1)S(1)}, u32[]{:S(2)}, u32[]{:S(2)}) collective-permute-start(bf16[128,512]{1,0:T(8,128)(2,1)S(1)} %get-tuple-element.75), channel_id=1, source_target_pairs={{0,8},{4,12},{8,16},{12,20},{16,24},{20,28},{24,0},{28,4},{32,40},... | collective-permute-start | bytes 393224 | tf_op jit(solution)/shard_map/ppermute | solution.py:527
  99.9 1.8 %collective-permute-start.6 = (bf16[128,512]{1,0:T(8,128)(2,1)S(1)}, bf16[128,512]{1,0:T(8,128)(2,1)S(1)}, u32[]{:S(2)}, u32[]{:S(2)}) collective-permute-start(bf16[128,512]{1,0:T(8,128)(2,1)S(1)} %get-tuple-element.76), channel_id=1, source_target_pairs={{0,24},{4,28},{8,0},{12,4},{16,8},{20,12},{24,16},{28,20},{32,56},... | collective-permute-start | bytes 393224 | tf_op jit(solution)/shard_map/ppermute | solution.py:527
  101.7 2.0 %collective-permute-start.7 = (bf16[128,512]{1,0:T(8,128)(2,1)S(1)}, bf16[128,512]{1,0:T(8,128)(2,1)S(1)}, u32[]{:S(2)}, u32[]{:S(2)}) collective-permute-start(bf16[128,512]{1,0:T(8,128)(2,1)S(1)} %get-tuple-element.77), channel_id=1, source_target_pairs={{0,16},{4,20},{8,24},{12,28},{16,0},{20,4},{24,8},{28,12},{32,48},... | collective-permute-start | bytes 393224 | tf_op jit(solution)/shard_map/ppermute | solution.py:527
  104.6 3.9 %collective-permute-start.11 = (bf16[128,512]{1,0:T(8,128)(2,1)S(1)}, bf16[128,512]{1,0:T(8,128)(2,1)S(1)}, u32[]{:S(2)}, u32[]{:S(2)}) collective-permute-start(bf16[128,512]{1,0:T(8,128)(2,1)S(1)} %get-tuple-element.87), channel_id=1, source_target_pairs={{0,32},{4,36},{8,40},{12,44},{16,48},{20,52},{24,56},{28,60},{32,6... | collective-permute-start | bytes 393224 | tf_op jit(solution)/shard_map/ppermute | solution.py:527
  108.9 2.0 %collective-permute-start.13 = (bf16[128,512]{1,0:T(8,128)(2,1)S(1)}, bf16[128,512]{1,0:T(8,128)(2,1)S(1)}, u32[]{:S(2)}, u32[]{:S(2)}) collective-permute-start(bf16[128,512]{1,0:T(8,128)(2,1)S(1)} %get-tuple-element.89), channel_id=1, source_target_pairs={{0,64},{4,68},{8,72},{12,76},{16,80},{20,84},{24,88},{28,92},{32,9... | collective-permute-start | bytes 393224 | tf_op jit(solution)/shard_map/ppermute | solution.py:527
  111.0 2.7 %collective-permute-start.24 = (bf16[288,256]{1,0:T(8,128)(2,1)S(1)}, bf16[288,256]{1,0:T(8,128)(2,1)S(1)}, u32[]{:S(2)}, u32[]{:S(2)}) collective-permute-start(bf16[288,256]{1,0:T(8,128)(2,1)S(1)} %merge.1.refs_0_), channel_id=1, source_target_pairs={{0,2},{2,0},{1,3},{3,1},{4,6},{6,4},{5,7},{7,5},{8,10},{10,8},{9,1... | collective-permute-start | bytes 442376 | tf_op jit(solution)/shard_map/ppermute | solution.py:543
  113.7 1.8 %collective-permute-done.13.refs_7_ = bf16[128,512]{1,0:T(8,128)(2,1)S(1)} collective-permute-done((bf16[128,512]{1,0:T(8,128)(2,1)S(1)}, bf16[128,512]{1,0:T(8,128)(2,1)S(1)}, u32[]{:S(2)}, u32[]{:S(2)}) %collective-permute-start.13) | collective-permute-done | bytes 131104 | tf_op jit(solution)/shard_map/ppermute | solution.py:527
  117.4 3.7 %collective-permute-start.25 = (f32[288,256]{1,0:T(8,128)S(1)}, f32[288,256]{1,0:T(8,128)S(1)}, u32[]{:S(2)}, u32[]{:S(2)}) collective-permute-start(f32[288,256]{1,0:T(8,128)S(1)} %get-tuple-element.100.refs_1_), channel_id=1, source_target_pairs={{0,1},{1,0},{2,3},{3,2},{4,5},{5,4},{6,7},{7,6},{8,9},{9,8},{10,11... | collective-permute-start | bytes 884744 | tf_op jit(solution)/shard_map/ppermute | solution.py:539
  121.1 1.8 %collective-permute-done.15.other_ref = bf16[256,512]{1,0:T(8,128)(2,1)S(1)} collective-permute-done((bf16[256,512]{1,0:T(8,128)(2,1)S(1)}, bf16[256,512]{1,0:T(8,128)(2,1)S(1)}, u32[]{:S(2)}, u32[]{:S(2)}) %collective-permute-start.15) | collective-permute-done | bytes 262176 | tf_op jit(solution)/shard_map/ppermute | solution.py:527
  123.1 4.6 %collective-permute-start.17 = (bf16[128,512]{1,0:T(8,128)(2,1)S(1)}, bf16[128,512]{1,0:T(8,128)(2,1)S(1)}, u32[]{:S(2)}, u32[]{:S(2)}) collective-permute-start(bf16[128,512]{1,0:T(8,128)(2,1)S(1)} %get-tuple-element.95.refs_0_), channel_id=1, source_target_pairs={{0,24},{4,28},{8,0},{12,4},{16,8},{20,12},{24,16},{28,20},{32,56},... | collective-permute-start | bytes 393224 | tf_op jit(solution)/shard_map/ppermute | solution.py:527
  128.2 1.8 %collective-permute-start.21 = (bf16[128,512]{1,0:T(8,128)(2,1)S(1)}, bf16[128,512]{1,0:T(8,128)(2,1)S(1)}, u32[]{:S(2)}, u32[]{:S(2)}) collective-permute-start(bf16[128,512]{1,0:T(8,128)(2,1)S(1)} %get-tuple-element.96.refs_4_), channel_id=1, source_target_pairs={{0,64},{4,68},{8,72},{12,76},{16,80},{20,84},{24,88},{28,92},{32,9... | collective-permute-start | bytes 393224 | tf_op jit(solution)/shard_map/ppermute | solution.py:527
  135.3 2.2 %collective-permute-done.19.refs_5_ = bf16[128,512]{1,0:T(8,128)(2,1)S(1)} collective-permute-done((bf16[128,512]{1,0:T(8,128)(2,1)S(1)}, bf16[128,512]{1,0:T(8,128)(2,1)S(1)}, u32[]{:S(2)}, u32[]{:S(2)}) %collective-permute-start.19) | collective-permute-done | bytes 131104 | tf_op jit(solution)/shard_map/ppermute | solution.py:527
  139.3 2.1 %collective-permute-start.28 = (bf16[512,512]{1,0:T(8,128)(2,1)S(1)}, bf16[512,512]{1,0:T(8,128)(2,1)S(1)}, u32[]{:S(2)}, u32[]{:S(2)}) collective-permute-start(bf16[512,512]{1,0:T(8,128)(2,1)S(1)} %get-tuple-element.106.refs_0_), channel_id=1, source_target_pairs={{0,16},{4,20},{8,24},{12,28},{16,0},{20,4},{24,8},{28,12},{32,48},... | collective-permute-start | bytes 1572872 | tf_op jit(solution)/shard_map/ppermute | solution.py:527
  141.4 1.9 %collective-permute-start.27 = (bf16[512,512]{1,0:T(8,128)(2,1)S(1)}, bf16[512,512]{1,0:T(8,128)(2,1)S(1)}, u32[]{:S(2)}, u32[]{:S(2)}) collective-permute-start(bf16[512,512]{1,0:T(8,128)(2,1)S(1)} %get-tuple-element.106.refs_0_), channel_id=1, source_target_pairs={{0,24},{4,28},{8,0},{12,4},{16,8},{20,12},{24,16},{28,20},{32,56},... | collective-permute-start | bytes 1572872 | tf_op jit(solution)/shard_map/ppermute | solution.py:527
  143.3 6.9 %collective-permute-done.31.refs_3_ = bf16[512,512]{1,0:T(8,128)(2,1)S(1)} collective-permute-done((bf16[512,512]{1,0:T(8,128)(2,1)S(1)}, bf16[512,512]{1,0:T(8,128)(2,1)S(1)}, u32[]{:S(2)}, u32[]{:S(2)}) %collective-permute-start.31) | collective-permute-done | bytes 524320 | tf_op jit(solution)/shard_map/ppermute | solution.py:527
  151.8 4.0 %project.1 = (bf16[256,2048]{1,0:T(8,128)(2,1)}, bf16[256,3072]{1,0:T(8,128)(2,1)}, f32[8,128]{1,0:T(8,128)S(1)}) custom-call(bf16[512,4096]{1,0:T(8,128)(2,1)S(1)} %copy-done.2, bf16[576,4096]{1,0:T(8,128)(2,1)S(1)} %bitcast.7, bf16[16,128,512]{2,1,0:T(8,128)(2,1)S(1)} %copy-done, bf16[16,128,512]{2,1,0:T(8,128)(2,1)S(1)} %copy-done.1, ...), custom_call_target="tpu_custom_call" | custom-call | flops 1048576 | bytes 1048576 | tf_op jit(solution)/shard_map/project/pallas_call | solution.py:346
  155.8 5.0 %collective-permute-done.30.refs_2_ = bf16[512,512]{1,0:T(8,128)(2,1)S(1)} collective-permute-done((bf16[512,512]{1,0:T(8,128)(2,1)S(1)}, bf16[512,512]{1,0:T(8,128)(2,1)S(1)}, u32[]{:S(2)}, u32[]{:S(2)}) %collective-permute-start.30) | collective-permute-done | bytes 524320 | tf_op jit(solution)/shard_map/ppermute | solution.py:527
  160.9 3.5 %collective-permute-done.29.refs_1_ = bf16[512,512]{1,0:T(8,128)(2,1)S(1)} collective-permute-done((bf16[512,512]{1,0:T(8,128)(2,1)S(1)}, bf16[512,512]{1,0:T(8,128)(2,1)S(1)}, u32[]{:S(2)}, u32[]{:S(2)}) %collective-permute-start.29) | collective-permute-done | bytes 524320 | tf_op jit(solution)/shard_map/ppermute | solution.py:527
  164.3 2.7 %widen.2 = (f32[16,128,512]{2,1,0:T(8,128)}, f32[16,128,512]{2,1,0:T(8,128)}) custom-call(s32[3]{0:T(128)S(1)} %copy-done.6, bf16[512,512]{1,0:T(8,128)(2,1)S(1)} %get-tuple-element.108.refs_0_, bf16[512,512]{1,0:T(8,128)(2,1)S(1)} %collective-permute-done.29.refs_1_, bf16[512,512]{1,0:T(8,128)(2,1)S(1)} %collective-permute-done.30.refs_2_, ...), custom_call_target="tpu_custom_call" | custom-call | flops 1048576 | bytes 1048576 | tf_op jit(solution)/shard_map/widen/pallas_call | solution.py:502
  167.1 2.7 %widen.3 = (f32[16,128,512]{2,1,0:T(8,128)}, f32[16,128,512]{2,1,0:T(8,128)}) custom-call(s32[3]{0:T(128)S(1)} %copy-done.6, bf16[512,512]{1,0:T(8,128)(2,1)S(1)} %get-tuple-element.106.refs_0_, bf16[512,512]{1,0:T(8,128)(2,1)S(1)} %collective-permute-done.26.refs_1_, ...), custom_call_target="tpu_custom_call", output_to_operand_aliasing={{0}: (6, {}), {1}: (7, {})} | custom-call | flops 1048576 | bytes 1048576 | tf_op jit(solution)/shard_map/widen/pallas_call | solution.py:502
  (80 shorter events, 27.2 us)
Async XLA Ops:
  0.6 18.1 %collective-permute-start.1 = (bf16[576,256]{1,0:T(8,128)(2,1)}, bf16[576,256]{1,0:T(8,128)(2,1)S(1)}, u32[]{:S(2)}, u32[]{:S(2)}) collective-permute-start(bf16[576,256]{1,0:T(8,128)(2,1)} %bitcast.9), channel_id=1, source_target_pairs={{0,4},{4,8},{8,12},{12,16},{16,20},{20,24},{24,28},{28,32},{32,36}... | collective-permute-start | bytes 884744 | tf_op jit(solution)/shard_map/ppermute | solution.py:24
  4.7 14.6 %collective-permute-start = (bf16[576,256]{1,0:T(8,128)(2,1)}, bf16[576,256]{1,0:T(8,128)(2,1)S(1)}, u32[]{:S(2)}, u32[]{:S(2)}) collective-permute-start(bf16[576,256]{1,0:T(8,128)(2,1)} %bitcast.10), channel_id=1, source_target_pairs={{0,8},{4,12},{8,16},{12,20},{16,24},{20,28},{24,32},{28,36},{32,40... | collective-permute-start | bytes 884744 | tf_op jit(solution)/shard_map/ppermute | solution.py:24
  37.3 26.1 %collective-permute-start.2 = (bf16[512,512]{1,0:T(8,128)(2,1)}, bf16[512,512]{1,0:T(8,128)(2,1)S(1)}, u32[]{:S(2)}, u32[]{:S(2)}) collective-permute-start(bf16[512,512]{1,0:T(8,128)(2,1)} %get-tuple-element.70), channel_id=1, source_target_pairs={{0,32},{4,36},{8,40},{12,44},{16,48},{20,52},{24,56},{28,60},{32,6... | collective-permute-start | bytes 1572872 | tf_op jit(solution)/shard_map/ppermute | solution.py:527
  40.3 24.2 %collective-permute-start.3 = (bf16[512,512]{1,0:T(8,128)(2,1)}, bf16[512,512]{1,0:T(8,128)(2,1)S(1)}, u32[]{:S(2)}, u32[]{:S(2)}) collective-permute-start(bf16[512,512]{1,0:T(8,128)(2,1)} %get-tuple-element.71), channel_id=1, source_target_pairs={{0,96},{4,100},{8,104},{12,108},{16,112},{20,116},{24,120},{28,124... | collective-permute-start | bytes 1572872 | tf_op jit(solution)/shard_map/ppermute | solution.py:527
  42.0 22.9 %collective-permute-start.4 = (bf16[512,512]{1,0:T(8,128)(2,1)}, bf16[512,512]{1,0:T(8,128)(2,1)S(1)}, u32[]{:S(2)}, u32[]{:S(2)}) collective-permute-start(bf16[512,512]{1,0:T(8,128)(2,1)} %get-tuple-element.72), channel_id=1, source_target_pairs={{0,64},{4,68},{8,72},{12,76},{16,80},{20,84},{24,88},{28,92},{32,9... | collective-permute-start | bytes 1572872 | tf_op jit(solution)/shard_map/ppermute | solution.py:527
  60.7 20.0 %collective-permute-start.8 = (bf16[512,512]{1,0:T(8,128)(2,1)}, bf16[512,512]{1,0:T(8,128)(2,1)S(1)}, u32[]{:S(2)}, u32[]{:S(2)}) collective-permute-start(bf16[512,512]{1,0:T(8,128)(2,1)} %get-tuple-element.79), channel_id=1, source_target_pairs={{0,8},{4,12},{8,16},{12,20},{16,24},{20,28},{24,0},{28,4},{32,40},... | collective-permute-start | bytes 1572872 | tf_op jit(solution)/shard_map/ppermute | solution.py:527
  61.1 19.6 %collective-permute-start.9 = (bf16[512,512]{1,0:T(8,128)(2,1)}, bf16[512,512]{1,0:T(8,128)(2,1)S(1)}, u32[]{:S(2)}, u32[]{:S(2)}) collective-permute-start(bf16[512,512]{1,0:T(8,128)(2,1)} %get-tuple-element.80), channel_id=1, source_target_pairs={{0,24},{4,28},{8,0},{12,4},{16,8},{20,12},{24,16},{28,20},{32,56},... | collective-permute-start | bytes 1572872 | tf_op jit(solution)/shard_map/ppermute | solution.py:527
  63.4 23.1 %collective-permute-start.10 = (bf16[512,512]{1,0:T(8,128)(2,1)}, bf16[512,512]{1,0:T(8,128)(2,1)S(1)}, u32[]{:S(2)}, u32[]{:S(2)}) collective-permute-start(bf16[512,512]{1,0:T(8,128)(2,1)} %get-tuple-element.81), channel_id=1, source_target_pairs={{0,16},{4,20},{8,24},{12,28},{16,0},{20,4},{24,8},{28,12},{32,48},... | collective-permute-start | bytes 1572872 | tf_op jit(solution)/shard_map/ppermute | solution.py:527
  90.0 4.4 %collective-permute-start.14 = (f32[288,768]{1,0:T(8,128)S(1)}, f32[288,768]{1,0:T(8,128)S(1)}, u32[]{:S(2)}, u32[]{:S(2)}) collective-permute-start(f32[288,768]{1,0:T(8,128)S(1)} %get-tuple-element.93), channel_id=1, source_target_pairs={{0,1},{1,0},{2,3},{3,2},{4,5},{5,4},{6,7},{7,6},{8,9},{9,8},{10,11... | collective-permute-start | bytes 2654216 | tf_op jit(solution)/shard_map/ppermute | solution.py:539
  94.6 13.9 %collective-permute-start.22 = (bf16[288,256]{1,0:T(8,128)(2,1)S(1)}, bf16[288,256]{1,0:T(8,128)(2,1)S(1)}, u32[]{:S(2)}, u32[]{:S(2)}) collective-permute-start(bf16[288,256]{1,0:T(8,128)(2,1)S(1)} %get-tuple-element.98), channel_id=1, source_target_pairs={{8,0},{12,4},{16,8},{20,12},{24,16},{28,20},{32,24},{36,28},{40,32... | collective-permute-start | bytes 442376 | tf_op jit(solution)/shard_map/ppermute | solution.py:24
  95.9 13.1 %collective-permute-start.23 = (bf16[288,256]{1,0:T(8,128)(2,1)S(1)}, bf16[288,256]{1,0:T(8,128)(2,1)S(1)}, u32[]{:S(2)}, u32[]{:S(2)}) collective-permute-start(bf16[288,256]{1,0:T(8,128)(2,1)S(1)} %get-tuple-element.99), channel_id=1, source_target_pairs={{4,0},{8,4},{12,8},{16,12},{20,16},{24,20},{28,24},{32,28},{36,32}... | collective-permute-start | bytes 442376 | tf_op jit(solution)/shard_map/ppermute | solution.py:24
  97.2 7.4 %collective-permute-start.5 = (bf16[128,512]{1,0:T(8,128)(2,1)S(1)}, bf16[128,512]{1,0:T(8,128)(2,1)S(1)}, u32[]{:S(2)}, u32[]{:S(2)}) collective-permute-start(bf16[128,512]{1,0:T(8,128)(2,1)S(1)} %get-tuple-element.75), channel_id=1, source_target_pairs={{0,8},{4,12},{8,16},{12,20},{16,24},{20,28},{24,0},{28,4},{32,40},... | collective-permute-start | bytes 393224 | tf_op jit(solution)/shard_map/ppermute | solution.py:527
  99.9 11.0 %collective-permute-start.6 = (bf16[128,512]{1,0:T(8,128)(2,1)S(1)}, bf16[128,512]{1,0:T(8,128)(2,1)S(1)}, u32[]{:S(2)}, u32[]{:S(2)}) collective-permute-start(bf16[128,512]{1,0:T(8,128)(2,1)S(1)} %get-tuple-element.76), channel_id=1, source_target_pairs={{0,24},{4,28},{8,0},{12,4},{16,8},{20,12},{24,16},{28,20},{32,56},... | collective-permute-start | bytes 393224 | tf_op jit(solution)/shard_map/ppermute | solution.py:527
  101.7 11.9 %collective-permute-start.7 = (bf16[128,512]{1,0:T(8,128)(2,1)S(1)}, bf16[128,512]{1,0:T(8,128)(2,1)S(1)}, u32[]{:S(2)}, u32[]{:S(2)}) collective-permute-start(bf16[128,512]{1,0:T(8,128)(2,1)S(1)} %get-tuple-element.77), channel_id=1, source_target_pairs={{0,16},{4,20},{8,24},{12,28},{16,0},{20,4},{24,8},{28,12},{32,48},... | collective-permute-start | bytes 393224 | tf_op jit(solution)/shard_map/ppermute | solution.py:527
  104.6 9.1 %collective-permute-start.11 = (bf16[128,512]{1,0:T(8,128)(2,1)S(1)}, bf16[128,512]{1,0:T(8,128)(2,1)S(1)}, u32[]{:S(2)}, u32[]{:S(2)}) collective-permute-start(bf16[128,512]{1,0:T(8,128)(2,1)S(1)} %get-tuple-element.87), channel_id=1, source_target_pairs={{0,32},{4,36},{8,40},{12,44},{16,48},{20,52},{24,56},{28,60},{32,6... | collective-permute-start | bytes 393224 | tf_op jit(solution)/shard_map/ppermute | solution.py:527
  108.5 5.2 %collective-permute-start.12 = (bf16[128,512]{1,0:T(8,128)(2,1)S(1)}, bf16[128,512]{1,0:T(8,128)(2,1)S(1)}, u32[]{:S(2)}, u32[]{:S(2)}) collective-permute-start(bf16[128,512]{1,0:T(8,128)(2,1)S(1)} %get-tuple-element.88), channel_id=1, source_target_pairs={{0,96},{4,100},{8,104},{12,108},{16,112},{20,116},{24,120},{28,124... | collective-permute-start | bytes 393224 | tf_op jit(solution)/shard_map/ppermute | solution.py:527
  108.9 6.5 %collective-permute-start.13 = (bf16[128,512]{1,0:T(8,128)(2,1)S(1)}, bf16[128,512]{1,0:T(8,128)(2,1)S(1)}, u32[]{:S(2)}, u32[]{:S(2)}) collective-permute-start(bf16[128,512]{1,0:T(8,128)(2,1)S(1)} %get-tuple-element.89), channel_id=1, source_target_pairs={{0,64},{4,68},{8,72},{12,76},{16,80},{20,84},{24,88},{28,92},{32,9... | collective-permute-start | bytes 393224 | tf_op jit(solution)/shard_map/ppermute | solution.py:527
  111.0 5.9 %collective-permute-start.24 = (bf16[288,256]{1,0:T(8,128)(2,1)S(1)}, bf16[288,256]{1,0:T(8,128)(2,1)S(1)}, u32[]{:S(2)}, u32[]{:S(2)}) collective-permute-start(bf16[288,256]{1,0:T(8,128)(2,1)S(1)} %merge.1.refs_0_), channel_id=1, source_target_pairs={{0,2},{2,0},{1,3},{3,1},{4,6},{6,4},{5,7},{7,5},{8,10},{10,8},{9,1... | collective-permute-start | bytes 442376 | tf_op jit(solution)/shard_map/ppermute | solution.py:543
  115.6 7.4 %collective-permute-start.15 = (bf16[256,512]{1,0:T(8,128)(2,1)S(1)}, bf16[256,512]{1,0:T(8,128)(2,1)S(1)}, u32[]{:S(2)}, u32[]{:S(2)}) collective-permute-start(bf16[256,512]{1,0:T(8,128)(2,1)S(1)} %totals.1.mine_ref), channel_id=1, source_target_pairs={{0,4},{4,0},{8,12},{12,8},{16,20},{20,16},{24,28},{28,24},{32,36},... | collective-permute-start | bytes 786440 | tf_op jit(solution)/shard_map/ppermute | solution.py:527
  117.4 14.0 %collective-permute-start.25 = (f32[288,256]{1,0:T(8,128)S(1)}, f32[288,256]{1,0:T(8,128)S(1)}, u32[]{:S(2)}, u32[]{:S(2)}) collective-permute-start(f32[288,256]{1,0:T(8,128)S(1)} %get-tuple-element.100.refs_1_), channel_id=1, source_target_pairs={{0,1},{1,0},{2,3},{3,2},{4,5},{5,4},{6,7},{7,6},{8,9},{9,8},{10,11... | collective-permute-start | bytes 884744 | tf_op jit(solution)/shard_map/ppermute | solution.py:539
  123.0 7.0 %collective-permute-start.18 = (bf16[128,512]{1,0:T(8,128)(2,1)S(1)}, bf16[128,512]{1,0:T(8,128)(2,1)S(1)}, u32[]{:S(2)}, u32[]{:S(2)}) collective-permute-start(bf16[128,512]{1,0:T(8,128)(2,1)S(1)} %get-tuple-element.95.refs_0_), channel_id=1, source_target_pairs={{0,16},{4,20},{8,24},{12,28},{16,0},{20,4},{24,8},{28,12},{32,48},... | collective-permute-start | bytes 393224 | tf_op jit(solution)/shard_map/ppermute | solution.py:527
  123.1 10.1 %collective-permute-start.17 = (bf16[128,512]{1,0:T(8,128)(2,1)S(1)}, bf16[128,512]{1,0:T(8,128)(2,1)S(1)}, u32[]{:S(2)}, u32[]{:S(2)}) collective-permute-start(bf16[128,512]{1,0:T(8,128)(2,1)S(1)} %get-tuple-element.95.refs_0_), channel_id=1, source_target_pairs={{0,24},{4,28},{8,0},{12,4},{16,8},{20,12},{24,16},{28,20},{32,56},... | collective-permute-start | bytes 393224 | tf_op jit(solution)/shard_map/ppermute | solution.py:527
  127.7 5.5 %collective-permute-start.16 = (bf16[128,512]{1,0:T(8,128)(2,1)S(1)}, bf16[128,512]{1,0:T(8,128)(2,1)S(1)}, u32[]{:S(2)}, u32[]{:S(2)}) collective-permute-start(bf16[128,512]{1,0:T(8,128)(2,1)S(1)} %get-tuple-element.95.refs_0_), channel_id=1, source_target_pairs={{0,8},{4,12},{8,16},{12,20},{16,24},{20,28},{24,0},{28,4},{32,40},... | collective-permute-start | bytes 393224 | tf_op jit(solution)/shard_map/ppermute | solution.py:527
  128.2 5.3 %collective-permute-start.21 = (bf16[128,512]{1,0:T(8,128)(2,1)S(1)}, bf16[128,512]{1,0:T(8,128)(2,1)S(1)}, u32[]{:S(2)}, u32[]{:S(2)}) collective-permute-start(bf16[128,512]{1,0:T(8,128)(2,1)S(1)} %get-tuple-element.96.refs_4_), channel_id=1, source_target_pairs={{0,64},{4,68},{8,72},{12,76},{16,80},{20,84},{24,88},{28,92},{32,9... | collective-permute-start | bytes 393224 | tf_op jit(solution)/shard_map/ppermute | solution.py:527
  130.1 5.3 %collective-permute-start.20 = (bf16[128,512]{1,0:T(8,128)(2,1)S(1)}, bf16[128,512]{1,0:T(8,128)(2,1)S(1)}, u32[]{:S(2)}, u32[]{:S(2)}) collective-permute-start(bf16[128,512]{1,0:T(8,128)(2,1)S(1)} %get-tuple-element.96.refs_4_), channel_id=1, source_target_pairs={{0,96},{4,100},{8,104},{12,108},{16,112},{20,116},{24,120},{28,124... | collective-permute-start | bytes 393224 | tf_op jit(solution)/shard_map/ppermute | solution.py:527
  131.4 6.1 %collective-permute-start.19 = (bf16[128,512]{1,0:T(8,128)(2,1)S(1)}, bf16[128,512]{1,0:T(8,128)(2,1)S(1)}, u32[]{:S(2)}, u32[]{:S(2)}) collective-permute-start(bf16[128,512]{1,0:T(8,128)(2,1)S(1)} %get-tuple-element.96.refs_4_), channel_id=1, source_target_pairs={{0,32},{4,36},{8,40},{12,44},{16,48},{20,52},{24,56},{28,60},{32,6... | collective-permute-start | bytes 393224 | tf_op jit(solution)/shard_map/ppermute | solution.py:527
  137.6 12.6 %collective-permute-start.31 = (bf16[512,512]{1,0:T(8,128)(2,1)S(1)}, bf16[512,512]{1,0:T(8,128)(2,1)S(1)}, u32[]{:S(2)}, u32[]{:S(2)}) collective-permute-start(bf16[512,512]{1,0:T(8,128)(2,1)S(1)} %get-tuple-element.108.refs_0_), channel_id=1, source_target_pairs={{0,64},{4,68},{8,72},{12,76},{16,80},{20,84},{24,88},{28,92},{32,9... | collective-permute-start | bytes 1572872 | tf_op jit(solution)/shard_map/ppermute | solution.py:527
  137.7 23.1 %collective-permute-start.30 = (bf16[512,512]{1,0:T(8,128)(2,1)S(1)}, bf16[512,512]{1,0:T(8,128)(2,1)S(1)}, u32[]{:S(2)}, u32[]{:S(2)}) collective-permute-start(bf16[512,512]{1,0:T(8,128)(2,1)S(1)} %get-tuple-element.108.refs_0_), channel_id=1, source_target_pairs={{0,96},{4,100},{8,104},{12,108},{16,112},{20,116},{24,120},{28,124... | collective-permute-start | bytes 1572872 | tf_op jit(solution)/shard_map/ppermute | solution.py:527
  138.7 25.6 %collective-permute-start.29 = (bf16[512,512]{1,0:T(8,128)(2,1)S(1)}, bf16[512,512]{1,0:T(8,128)(2,1)S(1)}, u32[]{:S(2)}, u32[]{:S(2)}) collective-permute-start(bf16[512,512]{1,0:T(8,128)(2,1)S(1)} %get-tuple-element.108.refs_0_), channel_id=1, source_target_pairs={{0,32},{4,36},{8,40},{12,44},{16,48},{20,52},{24,56},{28,60},{32,6... | collective-permute-start | bytes 1572872 | tf_op jit(solution)/shard_map/ppermute | solution.py:527
  139.3 27.7 %collective-permute-start.28 = (bf16[512,512]{1,0:T(8,128)(2,1)S(1)}, bf16[512,512]{1,0:T(8,128)(2,1)S(1)}, u32[]{:S(2)}, u32[]{:S(2)}) collective-permute-start(bf16[512,512]{1,0:T(8,128)(2,1)S(1)} %get-tuple-element.106.refs_0_), channel_id=1, source_target_pairs={{0,16},{4,20},{8,24},{12,28},{16,0},{20,4},{24,8},{28,12},{32,48},... | collective-permute-start | bytes 1572872 | tf_op jit(solution)/shard_map/ppermute | solution.py:527
  141.4 25.6 %collective-permute-start.27 = (bf16[512,512]{1,0:T(8,128)(2,1)S(1)}, bf16[512,512]{1,0:T(8,128)(2,1)S(1)}, u32[]{:S(2)}, u32[]{:S(2)}) collective-permute-start(bf16[512,512]{1,0:T(8,128)(2,1)S(1)} %get-tuple-element.106.refs_0_), channel_id=1, source_target_pairs={{0,24},{4,28},{8,0},{12,4},{16,8},{20,12},{24,16},{28,20},{32,56},... | collective-permute-start | bytes 1572872 | tf_op jit(solution)/shard_map/ppermute | solution.py:527
  150.2 16.8 %collective-permute-start.26 = (bf16[512,512]{1,0:T(8,128)(2,1)S(1)}, bf16[512,512]{1,0:T(8,128)(2,1)S(1)}, u32[]{:S(2)}, u32[]{:S(2)}) collective-permute-start(bf16[512,512]{1,0:T(8,128)(2,1)S(1)} %get-tuple-element.106.refs_0_), channel_id=1, source_target_pairs={{0,8},{4,12},{8,16},{12,20},{16,24},{20,28},{24,0},{28,4},{32,40},... | collective-permute-start | bytes 1572872 | tf_op jit(solution)/shard_map/ppermute | solution.py:527
  (14 other events, 429.4 us)

commit v5 on v4

--- a/solution.py
+++ b/solution.py
@@ -219,15 +219,20 @@
     )(place, block_mask, segments, blocks, qfull, dlo, dout_t, nope_t, *carried)
 
 
-def key_kernel(qfull_ref, dlo_ref, probs_ref, dscore_ref, _, total_ref):
+def key_kernel(qfull_ref, dlo_ref, probs_ref, dscore_ref, _, low_ref, total_ref):
     rank = dlo_ref.shape[0]
-
-    @pl.when(pl.program_id(0) == 0)
+    step = pl.program_id(0)
+
+    @pl.when(step == 0)
     def _():
         total_ref[...] = jnp.zeros_like(total_ref)
 
     total_ref[:rank] += dot_nt(qfull_ref[:rank], dscore_ref[...]) + dot_nt(dlo_ref[...], probs_ref[...])
     total_ref[rank:] += dot_nt(qfull_ref[rank:], dscore_ref[...])
+
+    @pl.when(step == pl.num_programs(0) - 1)
+    def _():
+        low_ref[...] = total_ref[...].astype(low_ref.dtype)
 
 
 def key_gradient(qfull, dlo, probs, dscore, toks, after):
@@ -235,12 +240,13 @@
     heads = qfull.shape[1] // toks
     heads_of = lambda rows: pl.BlockSpec((rows, GROUP * toks), lambda s: (0, s))
     return pl.pallas_call(
-        with_token(key_kernel),
+        with_token(key_kernel, 1),
         grid=(heads // GROUP,),
         in_specs=[heads_of(lat), heads_of(rank), heads_of(span), heads_of(span)]
         + [pl.BlockSpec(memory_space=pl.ANY)],
         out_specs=[pl.BlockSpec((lat, span), lambda s: (0, 0)), TOKEN_BLOCK],
-        out_shape=[jax.ShapeDtypeStruct((lat, span), jnp.float32), TOKEN],
+        out_shape=[jax.ShapeDtypeStruct((lat, span), jnp.bfloat16), TOKEN],
+        scratch_shapes=[pltpu.VMEM((lat, span), jnp.float32)],
         compiler_params=pltpu.CompilerParams(vmem_limit_bytes=LARGE),
         cost_estimate=pl.CostEstimate(
             flops=4 * heads * toks * span * (rank + lat), bytes_accessed=24 * MIB, transcendentals=0
@@ -253,7 +259,8 @@
     toks = own_ref.shape[1]
     for part, part_ref in enumerate(part_refs + (own_ref,)):
         span = slice(part * toks, (part + 1) * toks)
-        part_ref[...] = (keep_ref[:, span] + got_ref[:, span]).astype(part_ref.dtype)
+        total = keep_ref[:, span].astype(jnp.float32) + got_ref[:, span].astype(jnp.float32)
+        part_ref[...] = total.astype(part_ref.dtype)
 
 
 def split(keep, got, toks):
@@ -400,7 +407,7 @@
         cut_kernel,
         in_specs=[pl.BlockSpec(memory_space=pltpu.SMEM), whole, pl.BlockSpec(memory_space=pl.ANY)],
         out_specs=[whole] * 2,
-        out_shape=[jax.ShapeDtypeStruct((rows // 2, cols), jnp.float32)] * 2,
+        out_shape=[jax.ShapeDtypeStruct((rows // 2, cols), total.dtype)] * 2,
         compiler_params=pltpu.CompilerParams(vmem_limit_bytes=12 * MIB),
         cost_estimate=BRIEF,
         name="cut",

time: 170 us -> 169 us (level)
  no operation moved by 1% of the time
where the time goes in v5:
time: 169 us
  Pallas kernels  69.4 us (41%)
  starting transfers between devices  57.9 us (34%)
  waiting for transfers between devices  34.3 us (20%)
  local copies, waits for them, and re-layouts  5.65 us (3%)
    ppermute x25, starting transfers between devices, moved(): return lax.ppermute(block, 'ctx', route)  39 us
    pallas_call x2, Pallas kernels, score(): pl.pallas_call(with_token(functools.partial(score_kernel, inv_root, which...  34.7 us
    ppermute x25, waiting for transfers between devices, moved(): return lax.ppermute(block, 'ctx', route)  31.6 us
    pallas_call x1, Pallas kernels, key_gradient(): pl.pallas_call(with_token(key_kernel, 1), grid=(heads // GROUP,), in_spec...  13.3 us
    ppermute x4, starting transfers between devices, shifted(): return lax.ppermute(block, axis, route)  10.2 us
    pallas_call x1, Pallas kernels, prepare(): pl.pallas_call(prepare_kernel, grid=(heads // GROUP,), in_specs=[pl.Block...  8.33 us
    ppermute x2, starting transfers between devices, swap_core(): return lax.ppermute(block, 'head', [(0, 1), (1, 0), (2, 3), (3, 2)])  6.03 us
    pallas_call x2, Pallas kernels, widen(): pl.pallas_call(functools.partial(widen_kernel, chunk), in_specs=[pl.Block...  5.41 us
  transfers between devices with their start and end apart: 32, of which 15 were waited for; matrix products, arithmetic and copies ran while one was open for 1% of the time, Pallas kernels for 29%

profile of v5, /device:TPU:1, one launch (start us, length us, event | category | flops | bytes accessed | tf_op | source)
XLA Modules:
  0.0 168.9 jit_solution(5333438032961519136)
XLA Ops:
  0.6 4.0 %collective-permute-start.1 = (bf16[576,256]{1,0:T(8,128)(2,1)}, bf16[576,256]{1,0:T(8,128)(2,1)S(1)}, u32[]{:S(2)}, u32[]{:S(2)}) collective-permute-start(bf16[576,256]{1,0:T(8,128)(2,1)} %bitcast.9), channel_id=1, source_target_pairs={{0,4},{4,8},{8,12},{12,16},{16,20},{20,24},{24,28},{28,32},{32,36}... | collective-permute-start | bytes 884744 | tf_op jit(solution)/shard_map/ppermute | solution.py:24
  4.7 3.5 %collective-permute-start = (bf16[576,256]{1,0:T(8,128)(2,1)}, bf16[576,256]{1,0:T(8,128)(2,1)S(1)}, u32[]{:S(2)}, u32[]{:S(2)}) collective-permute-start(bf16[576,256]{1,0:T(8,128)(2,1)} %bitcast.10), channel_id=1, source_target_pairs={{0,8},{4,12},{8,16},{12,20},{16,24},{20,28},{24,32},{28,36},{32,40... | collective-permute-start | bytes 884744 | tf_op jit(solution)/shard_map/ppermute | solution.py:24
  9.7 8.3 %prepare.1 = (bf16[576,4096]{1,0:T(8,128)(2,1)}, bf16[512,4096]{1,0:T(8,128)(2,1)}, bf16[128,4096]{1,0:T(8,128)(2,1)}, bf16[128,4096]{1,0:T(8,128)(2,1)}) custom-call(bf16[256,3072]{1,0:T(8,128)(2,1)} %query_ref.1, bf16[256,2048]{1,0:T(8,128)(2,1)} %dout_ref.1, bf16[16,128,512]{2,1,0:T(8,128)(2,1)} %refs_2_.1, bf16[16,128,512]{2,1,0:T(8,128)(2,1)} %refs_3_.1), custom_call_target="tpu_custom_call" | custom-call | flops 1073741824 | bytes 16777216 | tf_op jit(solution)/shard_map/prepare/pallas_call | solution.py:75
  20.0 17.4 %score.2 = (bf16[768,4096]{1,0:T(8,128)(2,1)}, bf16[768,4096]{1,0:T(8,128)(2,1)}, bf16[512,4096]{1,0:T(8,128)(2,1)}, bf16[576,4096]{1,0:T(8,128)(2,1)}, bf16[512...) custom-call(s32[3]{0:T(128)} %pad_add_fusion.refs_0_.place_ref, ...), custom_call_target="tpu_custom_call" | custom-call | flops 13690208256 | bytes 25165824 | tf_op jit(solution)/shard_map/score/pallas_call | solution.py:175
  37.4 3.0 %collective-permute-start.2 = (bf16[512,512]{1,0:T(8,128)(2,1)}, bf16[512,512]{1,0:T(8,128)(2,1)S(1)}, u32[]{:S(2)}, u32[]{:S(2)}) collective-permute-start(bf16[512,512]{1,0:T(8,128)(2,1)} %get-tuple-element.70), channel_id=1, source_target_pairs={{0,32},{4,36},{8,40},{12,44},{16,48},{20,52},{24,56},{28,60},{32,6... | collective-permute-start | bytes 1572872 | tf_op jit(solution)/shard_map/ppermute | solution.py:534
  40.4 1.7 %collective-permute-start.3 = (bf16[512,512]{1,0:T(8,128)(2,1)}, bf16[512,512]{1,0:T(8,128)(2,1)S(1)}, u32[]{:S(2)}, u32[]{:S(2)}) collective-permute-start(bf16[512,512]{1,0:T(8,128)(2,1)} %get-tuple-element.71), channel_id=1, source_target_pairs={{0,96},{4,100},{8,104},{12,108},{16,112},{20,116},{24,120},{28,124... | collective-permute-start | bytes 1572872 | tf_op jit(solution)/shard_map/ppermute | solution.py:534
  43.4 17.3 %score.3 = (bf16[768,4096]{1,0:T(8,128)(2,1)}, bf16[768,4096]{1,0:T(8,128)(2,1)}, bf16[512,4096]{1,0:T(8,128)(2,1)}, bf16[576,4096]{1,0:T(8,128)(2,1)}, bf16[512...) custom-call(s32[3]{0:T(128)} %pad_add_fusion.refs_0_.place_ref, ...), custom_call_target="tpu_custom_call", output_to_operand_aliasing={{0}: (10, {}), {1}: (11, {}), {2}: (12, {}), {3}: (13, {})} | custom-call | flops 13690208256 | bytes 25165824 | tf_op jit(solution)/shard_map/score/pallas_call | solution.py:175
  61.2 2.3 %collective-permute-start.9 = (bf16[512,512]{1,0:T(8,128)(2,1)}, bf16[512,512]{1,0:T(8,128)(2,1)S(1)}, u32[]{:S(2)}, u32[]{:S(2)}) collective-permute-start(bf16[512,512]{1,0:T(8,128)(2,1)} %get-tuple-element.80), channel_id=1, source_target_pairs={{0,24},{4,28},{8,0},{12,4},{16,8},{20,12},{24,16},{28,20},{32,56},... | collective-permute-start | bytes 1572872 | tf_op jit(solution)/shard_map/ppermute | solution.py:534
  67.2 13.3 %key_gradient.1 = (bf16[576,768]{1,0:T(8,128)(2,1)}, f32[8,128]{1,0:T(8,128)}) custom-call(bf16[576,4096]{1,0:T(8,128)(2,1)} %get-tuple-element.59.refs_4_.refs_0_, bf16[512,4096]{1,0:T(8,128)(2,1)} %get-tuple-element.60.refs_5_.refs_1_, bf16[768,4096]{1,0:T(8,128)(2,1)} %get-tuple-element.82.refs_2_, bf16[768,4096]{1,0:T(8,128)(2,1)} %get-tuple-element.83.refs_3_, ...), custom_call_target="tpu_custom_call" | custom-call | flops 13690208256 | bytes 25165824 | tf_op jit(solution)/shard_map/key_gradient/pallas_call | solution.py:242
  80.5 6.0 %collective-permute-done.10.refs_4_ = bf16[512,512]{1,0:T(8,128)(2,1)S(1)} collective-permute-done((bf16[512,512]{1,0:T(8,128)(2,1)}, bf16[512,512]{1,0:T(8,128)(2,1)S(1)}, u32[]{:S(2)}, u32[]{:S(2)}) %collective-permute-start.10) | collective-permute-done | bytes 524320 | tf_op jit(solution)/shard_map/ppermute | solution.py:534
  89.7 2.3 %collective-permute-start.14 = (bf16[288,768]{1,0:T(8,128)(2,1)S(1)}, bf16[288,768]{1,0:T(8,128)(2,1)S(1)}, u32[]{:S(2)}, u32[]{:S(2)}) collective-permute-start(bf16[288,768]{1,0:T(8,128)(2,1)S(1)} %get-tuple-element.93), channel_id=1, source_target_pairs={{0,1},{1,0},{2,3},{3,2},{4,5},{5,4},{6,7},{7,6},{8,9},{9,8},{10,11... | collective-permute-start | bytes 1327112 | tf_op jit(solution)/shard_map/ppermute | solution.py:546
  96.1 2.8 %collective-permute-start.5 = (bf16[128,512]{1,0:T(8,128)(2,1)S(1)}, bf16[128,512]{1,0:T(8,128)(2,1)S(1)}, u32[]{:S(2)}, u32[]{:S(2)}) collective-permute-start(bf16[128,512]{1,0:T(8,128)(2,1)S(1)} %get-tuple-element.75), channel_id=1, source_target_pairs={{0,8},{4,12},{8,16},{12,20},{16,24},{20,28},{24,0},{28,4},{32,40},... | collective-permute-start | bytes 393224 | tf_op jit(solution)/shard_map/ppermute | solution.py:534
  98.9 1.8 %collective-permute-start.6 = (bf16[128,512]{1,0:T(8,128)(2,1)S(1)}, bf16[128,512]{1,0:T(8,128)(2,1)S(1)}, u32[]{:S(2)}, u32[]{:S(2)}) collective-permute-start(bf16[128,512]{1,0:T(8,128)(2,1)S(1)} %get-tuple-element.76), channel_id=1, source_target_pairs={{0,24},{4,28},{8,0},{12,4},{16,8},{20,12},{24,16},{28,20},{32,56},... | collective-permute-start | bytes 393224 | tf_op jit(solution)/shard_map/ppermute | solution.py:534
  100.7 2.0 %collective-permute-start.7 = (bf16[128,512]{1,0:T(8,128)(2,1)S(1)}, bf16[128,512]{1,0:T(8,128)(2,1)S(1)}, u32[]{:S(2)}, u32[]{:S(2)}) collective-permute-start(bf16[128,512]{1,0:T(8,128)(2,1)S(1)} %get-tuple-element.77), channel_id=1, source_target_pairs={{0,16},{4,20},{8,24},{12,28},{16,0},{20,4},{24,8},{28,12},{32,48},... | collective-permute-start | bytes 393224 | tf_op jit(solution)/shard_map/ppermute | solution.py:534
  103.6 3.9 %collective-permute-start.11 = (bf16[128,512]{1,0:T(8,128)(2,1)S(1)}, bf16[128,512]{1,0:T(8,128)(2,1)S(1)}, u32[]{:S(2)}, u32[]{:S(2)}) collective-permute-start(bf16[128,512]{1,0:T(8,128)(2,1)S(1)} %get-tuple-element.87), channel_id=1, source_target_pairs={{0,32},{4,36},{8,40},{12,44},{16,48},{20,52},{24,56},{28,60},{32,6... | collective-permute-start | bytes 393224 | tf_op jit(solution)/shard_map/ppermute | solution.py:534
  107.9 2.0 %collective-permute-start.13 = (bf16[128,512]{1,0:T(8,128)(2,1)S(1)}, bf16[128,512]{1,0:T(8,128)(2,1)S(1)}, u32[]{:S(2)}, u32[]{:S(2)}) collective-permute-start(bf16[128,512]{1,0:T(8,128)(2,1)S(1)} %get-tuple-element.89), channel_id=1, source_target_pairs={{0,64},{4,68},{8,72},{12,76},{16,80},{20,84},{24,88},{28,92},{32,9... | collective-permute-start | bytes 393224 | tf_op jit(solution)/shard_map/ppermute | solution.py:534
  110.0 2.7 %collective-permute-start.24 = (bf16[288,256]{1,0:T(8,128)(2,1)S(1)}, bf16[288,256]{1,0:T(8,128)(2,1)S(1)}, u32[]{:S(2)}, u32[]{:S(2)}) collective-permute-start(bf16[288,256]{1,0:T(8,128)(2,1)S(1)} %merge.1.refs_0_), channel_id=1, source_target_pairs={{0,2},{2,0},{1,3},{3,1},{4,6},{6,4},{5,7},{7,5},{8,10},{10,8},{9,1... | collective-permute-start | bytes 442376 | tf_op jit(solution)/shard_map/ppermute | solution.py:550
  112.7 1.8 %collective-permute-done.13.refs_7_ = bf16[128,512]{1,0:T(8,128)(2,1)S(1)} collective-permute-done((bf16[128,512]{1,0:T(8,128)(2,1)S(1)}, bf16[128,512]{1,0:T(8,128)(2,1)S(1)}, u32[]{:S(2)}, u32[]{:S(2)}) %collective-permute-start.13) | collective-permute-done | bytes 131104 | tf_op jit(solution)/shard_map/ppermute | solution.py:534
  116.4 3.7 %collective-permute-start.25 = (f32[288,256]{1,0:T(8,128)S(1)}, f32[288,256]{1,0:T(8,128)S(1)}, u32[]{:S(2)}, u32[]{:S(2)}) collective-permute-start(f32[288,256]{1,0:T(8,128)S(1)} %get-tuple-element.100.refs_1_), channel_id=1, source_target_pairs={{0,1},{1,0},{2,3},{3,2},{4,5},{5,4},{6,7},{7,6},{8,9},{9,8},{10,11... | collective-permute-start | bytes 884744 | tf_op jit(solution)/shard_map/ppermute | solution.py:546
  120.1 1.8 %collective-permute-done.15.other_ref = bf16[256,512]{1,0:T(8,128)(2,1)S(1)} collective-permute-done((bf16[256,512]{1,0:T(8,128)(2,1)S(1)}, bf16[256,512]{1,0:T(8,128)(2,1)S(1)}, u32[]{:S(2)}, u32[]{:S(2)}) %collective-permute-start.15) | collective-permute-done | bytes 262176 | tf_op jit(solution)/shard_map/ppermute | solution.py:534
  122.1 4.6 %collective-permute-start.17 = (bf16[128,512]{1,0:T(8,128)(2,1)S(1)}, bf16[128,512]{1,0:T(8,128)(2,1)S(1)}, u32[]{:S(2)}, u32[]{:S(2)}) collective-permute-start(bf16[128,512]{1,0:T(8,128)(2,1)S(1)} %get-tuple-element.95.refs_0_), channel_id=1, source_target_pairs={{0,24},{4,28},{8,0},{12,4},{16,8},{20,12},{24,16},{28,20},{32,56},... | collective-permute-start | bytes 393224 | tf_op jit(solution)/shard_map/ppermute | solution.py:534
  127.2 1.9 %collective-permute-start.21 = (bf16[128,512]{1,0:T(8,128)(2,1)S(1)}, bf16[128,512]{1,0:T(8,128)(2,1)S(1)}, u32[]{:S(2)}, u32[]{:S(2)}) collective-permute-start(bf16[128,512]{1,0:T(8,128)(2,1)S(1)} %get-tuple-element.96.refs_4_), channel_id=1, source_target_pairs={{0,64},{4,68},{8,72},{12,76},{16,80},{20,84},{24,88},{28,92},{32,9... | collective-permute-start | bytes 393224 | tf_op jit(solution)/shard_map/ppermute | solution.py:534
  132.5 1.8 %collective-permute-done.20.refs_6_ = bf16[128,512]{1,0:T(8,128)(2,1)S(1)} collective-permute-done((bf16[128,512]{1,0:T(8,128)(2,1)S(1)}, bf16[128,512]{1,0:T(8,128)(2,1)S(1)}, u32[]{:S(2)}, u32[]{:S(2)}) %collective-permute-start.20) | collective-permute-done | bytes 131104 | tf_op jit(solution)/shard_map/ppermute | solution.py:534
  134.3 2.2 %collective-permute-done.19.refs_5_ = bf16[128,512]{1,0:T(8,128)(2,1)S(1)} collective-permute-done((bf16[128,512]{1,0:T(8,128)(2,1)S(1)}, bf16[128,512]{1,0:T(8,128)(2,1)S(1)}, u32[]{:S(2)}, u32[]{:S(2)}) %collective-permute-start.19) | collective-permute-done | bytes 131104 | tf_op jit(solution)/shard_map/ppermute | solution.py:534
  138.3 2.2 %collective-permute-start.28 = (bf16[512,512]{1,0:T(8,128)(2,1)S(1)}, bf16[512,512]{1,0:T(8,128)(2,1)S(1)}, u32[]{:S(2)}, u32[]{:S(2)}) collective-permute-start(bf16[512,512]{1,0:T(8,128)(2,1)S(1)} %get-tuple-element.106.refs_0_), channel_id=1, source_target_pairs={{0,16},{4,20},{8,24},{12,28},{16,0},{20,4},{24,8},{28,12},{32,48},... | collective-permute-start | bytes 1572872 | tf_op jit(solution)/shard_map/ppermute | solution.py:534
  140.4 1.9 %collective-permute-start.27 = (bf16[512,512]{1,0:T(8,128)(2,1)S(1)}, bf16[512,512]{1,0:T(8,128)(2,1)S(1)}, u32[]{:S(2)}, u32[]{:S(2)}) collective-permute-start(bf16[512,512]{1,0:T(8,128)(2,1)S(1)} %get-tuple-element.106.refs_0_), channel_id=1, source_target_pairs={{0,24},{4,28},{8,0},{12,4},{16,8},{20,12},{24,16},{28,20},{32,56},... | collective-permute-start | bytes 1572872 | tf_op jit(solution)/shard_map/ppermute | solution.py:534
  142.3 6.9 %collective-permute-done.31.refs_3_ = bf16[512,512]{1,0:T(8,128)(2,1)S(1)} collective-permute-done((bf16[512,512]{1,0:T(8,128)(2,1)S(1)}, bf16[512,512]{1,0:T(8,128)(2,1)S(1)}, u32[]{:S(2)}, u32[]{:S(2)}) %collective-permute-start.31) | collective-permute-done | bytes 524320 | tf_op jit(solution)/shard_map/ppermute | solution.py:534
  150.7 4.0 %project.1 = (bf16[256,2048]{1,0:T(8,128)(2,1)}, bf16[256,3072]{1,0:T(8,128)(2,1)}, f32[8,128]{1,0:T(8,128)S(1)}) custom-call(bf16[512,4096]{1,0:T(8,128)(2,1)S(1)} %copy-done.2, bf16[576,4096]{1,0:T(8,128)(2,1)S(1)} %bitcast.7, bf16[16,128,512]{2,1,0:T(8,128)(2,1)S(1)} %copy-done, bf16[16,128,512]{2,1,0:T(8,128)(2,1)S(1)} %copy-done.1, ...), custom_call_target="tpu_custom_call" | custom-call | flops 1048576 | bytes 1048576 | tf_op jit(solution)/shard_map/project/pallas_call | solution.py:353
  154.8 5.1 %collective-permute-done.30.refs_2_ = bf16[512,512]{1,0:T(8,128)(2,1)S(1)} collective-permute-done((bf16[512,512]{1,0:T(8,128)(2,1)S(1)}, bf16[512,512]{1,0:T(8,128)(2,1)S(1)}, u32[]{:S(2)}, u32[]{:S(2)}) %collective-permute-start.30) | collective-permute-done | bytes 524320 | tf_op jit(solution)/shard_map/ppermute | solution.py:534
  159.8 3.5 %collective-permute-done.29.refs_1_ = bf16[512,512]{1,0:T(8,128)(2,1)S(1)} collective-permute-done((bf16[512,512]{1,0:T(8,128)(2,1)S(1)}, bf16[512,512]{1,0:T(8,128)(2,1)S(1)}, u32[]{:S(2)}, u32[]{:S(2)}) %collective-permute-start.29) | collective-permute-done | bytes 524320 | tf_op jit(solution)/shard_map/ppermute | solution.py:534
  163.3 2.7 %widen.2 = (f32[16,128,512]{2,1,0:T(8,128)}, f32[16,128,512]{2,1,0:T(8,128)}) custom-call(s32[3]{0:T(128)S(1)} %copy-done.6, bf16[512,512]{1,0:T(8,128)(2,1)S(1)} %get-tuple-element.108.refs_0_, bf16[512,512]{1,0:T(8,128)(2,1)S(1)} %collective-permute-done.29.refs_1_, bf16[512,512]{1,0:T(8,128)(2,1)S(1)} %collective-permute-done.30.refs_2_, ...), custom_call_target="tpu_custom_call" | custom-call | flops 1048576 | bytes 1048576 | tf_op jit(solution)/shard_map/widen/pallas_call | solution.py:509
  166.0 2.7 %widen.3 = (f32[16,128,512]{2,1,0:T(8,128)}, f32[16,128,512]{2,1,0:T(8,128)}) custom-call(s32[3]{0:T(128)S(1)} %copy-done.6, bf16[512,512]{1,0:T(8,128)(2,1)S(1)} %get-tuple-element.106.refs_0_, bf16[512,512]{1,0:T(8,128)(2,1)S(1)} %collective-permute-done.26.refs_1_, ...), custom_call_target="tpu_custom_call", output_to_operand_aliasing={{0}: (6, {}), {1}: (7, {})} | custom-call | flops 1048576 | bytes 1048576 | tf_op jit(solution)/shard_map/widen/pallas_call | solution.py:509
  (80 shorter events, 26.6 us)
Async XLA Ops:
  0.6 18.0 %collective-permute-start.1 = (bf16[576,256]{1,0:T(8,128)(2,1)}, bf16[576,256]{1,0:T(8,128)(2,1)S(1)}, u32[]{:S(2)}, u32[]{:S(2)}) collective-permute-start(bf16[576,256]{1,0:T(8,128)(2,1)} %bitcast.9), channel_id=1, source_target_pairs={{0,4},{4,8},{8,12},{12,16},{16,20},{20,24},{24,28},{28,32},{32,36}... | collective-permute-start | bytes 884744 | tf_op jit(solution)/shard_map/ppermute | solution.py:24
  4.7 14.6 %collective-permute-start = (bf16[576,256]{1,0:T(8,128)(2,1)}, bf16[576,256]{1,0:T(8,128)(2,1)S(1)}, u32[]{:S(2)}, u32[]{:S(2)}) collective-permute-start(bf16[576,256]{1,0:T(8,128)(2,1)} %bitcast.10), channel_id=1, source_target_pairs={{0,8},{4,12},{8,16},{12,20},{16,24},{20,28},{24,32},{28,36},{32,40... | collective-permute-start | bytes 884744 | tf_op jit(solution)/shard_map/ppermute | solution.py:24
  37.4 26.1 %collective-permute-start.2 = (bf16[512,512]{1,0:T(8,128)(2,1)}, bf16[512,512]{1,0:T(8,128)(2,1)S(1)}, u32[]{:S(2)}, u32[]{:S(2)}) collective-permute-start(bf16[512,512]{1,0:T(8,128)(2,1)} %get-tuple-element.70), channel_id=1, source_target_pairs={{0,32},{4,36},{8,40},{12,44},{16,48},{20,52},{24,56},{28,60},{32,6... | collective-permute-start | bytes 1572872 | tf_op jit(solution)/shard_map/ppermute | solution.py:534
  40.4 24.2 %collective-permute-start.3 = (bf16[512,512]{1,0:T(8,128)(2,1)}, bf16[512,512]{1,0:T(8,128)(2,1)S(1)}, u32[]{:S(2)}, u32[]{:S(2)}) collective-permute-start(bf16[512,512]{1,0:T(8,128)(2,1)} %get-tuple-element.71), channel_id=1, source_target_pairs={{0,96},{4,100},{8,104},{12,108},{16,112},{20,116},{24,120},{28,124... | collective-permute-start | bytes 1572872 | tf_op jit(solution)/shard_map/ppermute | solution.py:534
  42.1 23.0 %collective-permute-start.4 = (bf16[512,512]{1,0:T(8,128)(2,1)}, bf16[512,512]{1,0:T(8,128)(2,1)S(1)}, u32[]{:S(2)}, u32[]{:S(2)}) collective-permute-start(bf16[512,512]{1,0:T(8,128)(2,1)} %get-tuple-element.72), channel_id=1, source_target_pairs={{0,64},{4,68},{8,72},{12,76},{16,80},{20,84},{24,88},{28,92},{32,9... | collective-permute-start | bytes 1572872 | tf_op jit(solution)/shard_map/ppermute | solution.py:534
  60.8 19.7 %collective-permute-start.8 = (bf16[512,512]{1,0:T(8,128)(2,1)}, bf16[512,512]{1,0:T(8,128)(2,1)S(1)}, u32[]{:S(2)}, u32[]{:S(2)}) collective-permute-start(bf16[512,512]{1,0:T(8,128)(2,1)} %get-tuple-element.79), channel_id=1, source_target_pairs={{0,8},{4,12},{8,16},{12,20},{16,24},{20,28},{24,0},{28,4},{32,40},... | collective-permute-start | bytes 1572872 | tf_op jit(solution)/shard_map/ppermute | solution.py:534
  61.2 19.3 %collective-permute-start.9 = (bf16[512,512]{1,0:T(8,128)(2,1)}, bf16[512,512]{1,0:T(8,128)(2,1)S(1)}, u32[]{:S(2)}, u32[]{:S(2)}) collective-permute-start(bf16[512,512]{1,0:T(8,128)(2,1)} %get-tuple-element.80), channel_id=1, source_target_pairs={{0,24},{4,28},{8,0},{12,4},{16,8},{20,12},{24,16},{28,20},{32,56},... | collective-permute-start | bytes 1572872 | tf_op jit(solution)/shard_map/ppermute | solution.py:534
  63.5 23.0 %collective-permute-start.10 = (bf16[512,512]{1,0:T(8,128)(2,1)}, bf16[512,512]{1,0:T(8,128)(2,1)S(1)}, u32[]{:S(2)}, u32[]{:S(2)}) collective-permute-start(bf16[512,512]{1,0:T(8,128)(2,1)} %get-tuple-element.81), channel_id=1, source_target_pairs={{0,16},{4,20},{8,24},{12,28},{16,0},{20,4},{24,8},{28,12},{32,48},... | collective-permute-start | bytes 1572872 | tf_op jit(solution)/shard_map/ppermute | solution.py:534
  89.7 3.8 %collective-permute-start.14 = (bf16[288,768]{1,0:T(8,128)(2,1)S(1)}, bf16[288,768]{1,0:T(8,128)(2,1)S(1)}, u32[]{:S(2)}, u32[]{:S(2)}) collective-permute-start(bf16[288,768]{1,0:T(8,128)(2,1)S(1)} %get-tuple-element.93), channel_id=1, source_target_pairs={{0,1},{1,0},{2,3},{3,2},{4,5},{5,4},{6,7},{7,6},{8,9},{9,8},{10,11... | collective-permute-start | bytes 1327112 | tf_op jit(solution)/shard_map/ppermute | solution.py:546
  93.5 13.9 %collective-permute-start.22 = (bf16[288,256]{1,0:T(8,128)(2,1)S(1)}, bf16[288,256]{1,0:T(8,128)(2,1)S(1)}, u32[]{:S(2)}, u32[]{:S(2)}) collective-permute-start(bf16[288,256]{1,0:T(8,128)(2,1)S(1)} %get-tuple-element.98), channel_id=1, source_target_pairs={{8,0},{12,4},{16,8},{20,12},{24,16},{28,20},{32,24},{36,28},{40,32... | collective-permute-start | bytes 442376 | tf_op jit(solution)/shard_map/ppermute | solution.py:24
  94.8 13.1 %collective-permute-start.23 = (bf16[288,256]{1,0:T(8,128)(2,1)S(1)}, bf16[288,256]{1,0:T(8,128)(2,1)S(1)}, u32[]{:S(2)}, u32[]{:S(2)}) collective-permute-start(bf16[288,256]{1,0:T(8,128)(2,1)S(1)} %get-tuple-element.99), channel_id=1, source_target_pairs={{4,0},{8,4},{12,8},{16,12},{20,16},{24,20},{28,24},{32,28},{36,32}... | collective-permute-start | bytes 442376 | tf_op jit(solution)/shard_map/ppermute | solution.py:24
  96.1 7.4 %collective-permute-start.5 = (bf16[128,512]{1,0:T(8,128)(2,1)S(1)}, bf16[128,512]{1,0:T(8,128)(2,1)S(1)}, u32[]{:S(2)}, u32[]{:S(2)}) collective-permute-start(bf16[128,512]{1,0:T(8,128)(2,1)S(1)} %get-tuple-element.75), channel_id=1, source_target_pairs={{0,8},{4,12},{8,16},{12,20},{16,24},{20,28},{24,0},{28,4},{32,40},... | collective-permute-start | bytes 393224 | tf_op jit(solution)/shard_map/ppermute | solution.py:534
  98.9 11.0 %collective-permute-start.6 = (bf16[128,512]{1,0:T(8,128)(2,1)S(1)}, bf16[128,512]{1,0:T(8,128)(2,1)S(1)}, u32[]{:S(2)}, u32[]{:S(2)}) collective-permute-start(bf16[128,512]{1,0:T(8,128)(2,1)S(1)} %get-tuple-element.76), channel_id=1, source_target_pairs={{0,24},{4,28},{8,0},{12,4},{16,8},{20,12},{24,16},{28,20},{32,56},... | collective-permute-start | bytes 393224 | tf_op jit(solution)/shard_map/ppermute | solution.py:534
  100.7 11.9 %collective-permute-start.7 = (bf16[128,512]{1,0:T(8,128)(2,1)S(1)}, bf16[128,512]{1,0:T(8,128)(2,1)S(1)}, u32[]{:S(2)}, u32[]{:S(2)}) collective-permute-start(bf16[128,512]{1,0:T(8,128)(2,1)S(1)} %get-tuple-element.77), channel_id=1, source_target_pairs={{0,16},{4,20},{8,24},{12,28},{16,0},{20,4},{24,8},{28,12},{32,48},... | collective-permute-start | bytes 393224 | tf_op jit(solution)/shard_map/ppermute | solution.py:534
  103.6 9.1 %collective-permute-start.11 = (bf16[128,512]{1,0:T(8,128)(2,1)S(1)}, bf16[128,512]{1,0:T(8,128)(2,1)S(1)}, u32[]{:S(2)}, u32[]{:S(2)}) collective-permute-start(bf16[128,512]{1,0:T(8,128)(2,1)S(1)} %get-tuple-element.87), channel_id=1, source_target_pairs={{0,32},{4,36},{8,40},{12,44},{16,48},{20,52},{24,56},{28,60},{32,6... | collective-permute-start | bytes 393224 | tf_op jit(solution)/shard_map/ppermute | solution.py:534
  107.5 5.2 %collective-permute-start.12 = (bf16[128,512]{1,0:T(8,128)(2,1)S(1)}, bf16[128,512]{1,0:T(8,128)(2,1)S(1)}, u32[]{:S(2)}, u32[]{:S(2)}) collective-permute-start(bf16[128,512]{1,0:T(8,128)(2,1)S(1)} %get-tuple-element.88), channel_id=1, source_target_pairs={{0,96},{4,100},{8,104},{12,108},{16,112},{20,116},{24,120},{28,124... | collective-permute-start | bytes 393224 | tf_op jit(solution)/shard_map/ppermute | solution.py:534
  107.9 6.5 %collective-permute-start.13 = (bf16[128,512]{1,0:T(8,128)(2,1)S(1)}, bf16[128,512]{1,0:T(8,128)(2,1)S(1)}, u32[]{:S(2)}, u32[]{:S(2)}) collective-permute-start(bf16[128,512]{1,0:T(8,128)(2,1)S(1)} %get-tuple-element.89), channel_id=1, source_target_pairs={{0,64},{4,68},{8,72},{12,76},{16,80},{20,84},{24,88},{28,92},{32,9... | collective-permute-start | bytes 393224 | tf_op jit(solution)/shard_map/ppermute | solution.py:534
  110.0 5.9 %collective-permute-start.24 = (bf16[288,256]{1,0:T(8,128)(2,1)S(1)}, bf16[288,256]{1,0:T(8,128)(2,1)S(1)}, u32[]{:S(2)}, u32[]{:S(2)}) collective-permute-start(bf16[288,256]{1,0:T(8,128)(2,1)S(1)} %merge.1.refs_0_), channel_id=1, source_target_pairs={{0,2},{2,0},{1,3},{3,1},{4,6},{6,4},{5,7},{7,5},{8,10},{10,8},{9,1... | collective-permute-start | bytes 442376 | tf_op jit(solution)/shard_map/ppermute | solution.py:550
  114.6 7.3 %collective-permute-start.15 = (bf16[256,512]{1,0:T(8,128)(2,1)S(1)}, bf16[256,512]{1,0:T(8,128)(2,1)S(1)}, u32[]{:S(2)}, u32[]{:S(2)}) collective-permute-start(bf16[256,512]{1,0:T(8,128)(2,1)S(1)} %totals.1.mine_ref), channel_id=1, source_target_pairs={{0,4},{4,0},{8,12},{12,8},{16,20},{20,16},{24,28},{28,24},{32,36},... | collective-permute-start | bytes 786440 | tf_op jit(solution)/shard_map/ppermute | solution.py:534
  116.4 14.0 %collective-permute-start.25 = (f32[288,256]{1,0:T(8,128)S(1)}, f32[288,256]{1,0:T(8,128)S(1)}, u32[]{:S(2)}, u32[]{:S(2)}) collective-permute-start(f32[288,256]{1,0:T(8,128)S(1)} %get-tuple-element.100.refs_1_), channel_id=1, source_target_pairs={{0,1},{1,0},{2,3},{3,2},{4,5},{5,4},{6,7},{7,6},{8,9},{9,8},{10,11... | collective-permute-start | bytes 884744 | tf_op jit(solution)/shard_map/ppermute | solution.py:546
  122.0 7.1 %collective-permute-start.18 = (bf16[128,512]{1,0:T(8,128)(2,1)S(1)}, bf16[128,512]{1,0:T(8,128)(2,1)S(1)}, u32[]{:S(2)}, u32[]{:S(2)}) collective-permute-start(bf16[128,512]{1,0:T(8,128)(2,1)S(1)} %get-tuple-element.95.refs_0_), channel_id=1, source_target_pairs={{0,16},{4,20},{8,24},{12,28},{16,0},{20,4},{24,8},{28,12},{32,48},... | collective-permute-start | bytes 393224 | tf_op jit(solution)/shard_map/ppermute | solution.py:534
  122.1 10.1 %collective-permute-start.17 = (bf16[128,512]{1,0:T(8,128)(2,1)S(1)}, bf16[128,512]{1,0:T(8,128)(2,1)S(1)}, u32[]{:S(2)}, u32[]{:S(2)}) collective-permute-start(bf16[128,512]{1,0:T(8,128)(2,1)S(1)} %get-tuple-element.95.refs_0_), channel_id=1, source_target_pairs={{0,24},{4,28},{8,0},{12,4},{16,8},{20,12},{24,16},{28,20},{32,56},... | collective-permute-start | bytes 393224 | tf_op jit(solution)/shard_map/ppermute | solution.py:534
  126.7 5.5 %collective-permute-start.16 = (bf16[128,512]{1,0:T(8,128)(2,1)S(1)}, bf16[128,512]{1,0:T(8,128)(2,1)S(1)}, u32[]{:S(2)}, u32[]{:S(2)}) collective-permute-start(bf16[128,512]{1,0:T(8,128)(2,1)S(1)} %get-tuple-element.95.refs_0_), channel_id=1, source_target_pairs={{0,8},{4,12},{8,16},{12,20},{16,24},{20,28},{24,0},{28,4},{32,40},... | collective-permute-start | bytes 393224 | tf_op jit(solution)/shard_map/ppermute | solution.py:534
  127.2 5.3 %collective-permute-start.21 = (bf16[128,512]{1,0:T(8,128)(2,1)S(1)}, bf16[128,512]{1,0:T(8,128)(2,1)S(1)}, u32[]{:S(2)}, u32[]{:S(2)}) collective-permute-start(bf16[128,512]{1,0:T(8,128)(2,1)S(1)} %get-tuple-element.96.refs_4_), channel_id=1, source_target_pairs={{0,64},{4,68},{8,72},{12,76},{16,80},{20,84},{24,88},{28,92},{32,9... | collective-permute-start | bytes 393224 | tf_op jit(solution)/shard_map/ppermute | solution.py:534
  129.1 5.3 %collective-permute-start.20 = (bf16[128,512]{1,0:T(8,128)(2,1)S(1)}, bf16[128,512]{1,0:T(8,128)(2,1)S(1)}, u32[]{:S(2)}, u32[]{:S(2)}) collective-permute-start(bf16[128,512]{1,0:T(8,128)(2,1)S(1)} %get-tuple-element.96.refs_4_), channel_id=1, source_target_pairs={{0,96},{4,100},{8,104},{12,108},{16,112},{20,116},{24,120},{28,124... | collective-permute-start | bytes 393224 | tf_op jit(solution)/shard_map/ppermute | solution.py:534
  130.4 6.1 %collective-permute-start.19 = (bf16[128,512]{1,0:T(8,128)(2,1)S(1)}, bf16[128,512]{1,0:T(8,128)(2,1)S(1)}, u32[]{:S(2)}, u32[]{:S(2)}) collective-permute-start(bf16[128,512]{1,0:T(8,128)(2,1)S(1)} %get-tuple-element.96.refs_4_), channel_id=1, source_target_pairs={{0,32},{4,36},{8,40},{12,44},{16,48},{20,52},{24,56},{28,60},{32,6... | collective-permute-start | bytes 393224 | tf_op jit(solution)/shard_map/ppermute | solution.py:534
  136.6 12.6 %collective-permute-start.31 = (bf16[512,512]{1,0:T(8,128)(2,1)S(1)}, bf16[512,512]{1,0:T(8,128)(2,1)S(1)}, u32[]{:S(2)}, u32[]{:S(2)}) collective-permute-start(bf16[512,512]{1,0:T(8,128)(2,1)S(1)} %get-tuple-element.108.refs_0_), channel_id=1, source_target_pairs={{0,64},{4,68},{8,72},{12,76},{16,80},{20,84},{24,88},{28,92},{32,9... | collective-permute-start | bytes 1572872 | tf_op jit(solution)/shard_map/ppermute | solution.py:534
  136.7 23.1 %collective-permute-start.30 = (bf16[512,512]{1,0:T(8,128)(2,1)S(1)}, bf16[512,512]{1,0:T(8,128)(2,1)S(1)}, u32[]{:S(2)}, u32[]{:S(2)}) collective-permute-start(bf16[512,512]{1,0:T(8,128)(2,1)S(1)} %get-tuple-element.108.refs_0_), channel_id=1, source_target_pairs={{0,96},{4,100},{8,104},{12,108},{16,112},{20,116},{24,120},{28,124... | collective-permute-start | bytes 1572872 | tf_op jit(solution)/shard_map/ppermute | solution.py:534
  137.7 25.6 %collective-permute-start.29 = (bf16[512,512]{1,0:T(8,128)(2,1)S(1)}, bf16[512,512]{1,0:T(8,128)(2,1)S(1)}, u32[]{:S(2)}, u32[]{:S(2)}) collective-permute-start(bf16[512,512]{1,0:T(8,128)(2,1)S(1)} %get-tuple-element.108.refs_0_), channel_id=1, source_target_pairs={{0,32},{4,36},{8,40},{12,44},{16,48},{20,52},{24,56},{28,60},{32,6... | collective-permute-start | bytes 1572872 | tf_op jit(solution)/shard_map/ppermute | solution.py:534
  138.3 27.7 %collective-permute-start.28 = (bf16[512,512]{1,0:T(8,128)(2,1)S(1)}, bf16[512,512]{1,0:T(8,128)(2,1)S(1)}, u32[]{:S(2)}, u32[]{:S(2)}) collective-permute-start(bf16[512,512]{1,0:T(8,128)(2,1)S(1)} %get-tuple-element.106.refs_0_), channel_id=1, source_target_pairs={{0,16},{4,20},{8,24},{12,28},{16,0},{20,4},{24,8},{28,12},{32,48},... | collective-permute-start | bytes 1572872 | tf_op jit(solution)/shard_map/ppermute | solution.py:534
  140.4 25.6 %collective-permute-start.27 = (bf16[512,512]{1,0:T(8,128)(2,1)S(1)}, bf16[512,512]{1,0:T(8,128)(2,1)S(1)}, u32[]{:S(2)}, u32[]{:S(2)}) collective-permute-start(bf16[512,512]{1,0:T(8,128)(2,1)S(1)} %get-tuple-element.106.refs_0_), channel_id=1, source_target_pairs={{0,24},{4,28},{8,0},{12,4},{16,8},{20,12},{24,16},{28,20},{32,56},... | collective-permute-start | bytes 1572872 | tf_op jit(solution)/shard_map/ppermute | solution.py:534
  149.2 16.8 %collective-permute-start.26 = (bf16[512,512]{1,0:T(8,128)(2,1)S(1)}, bf16[512,512]{1,0:T(8,128)(2,1)S(1)}, u32[]{:S(2)}, u32[]{:S(2)}) collective-permute-start(bf16[512,512]{1,0:T(8,128)(2,1)S(1)} %get-tuple-element.106.refs_0_), channel_id=1, source_target_pairs={{0,8},{4,12},{8,16},{12,20},{16,24},{20,28},{24,0},{28,4},{32,40},... | collective-permute-start | bytes 1572872 | tf_op jit(solution)/shard_map/ppermute | solution.py:534
  (14 other events, 425.2 us)

commit v6 on v5

--- a/solution.py
+++ b/solution.py
@@ -25,13 +25,12 @@
 
 TOKEN = jax.ShapeDtypeStruct((8, 128), jnp.float32)
 WHOLE = pl.BlockSpec(memory_space=pltpu.VMEM)
-TOKEN_BLOCK = pl.BlockSpec((8, 128), lambda *_: (0, 0))
+TOKEN_BLOCK = pl.BlockSpec(memory_space=pltpu.HBM)
 
 
 def with_token(kernel, scratch=0):
     def wrapped(*refs):
         end = len(refs) - scratch
-        refs[end - 1][...] = jnp.zeros(TOKEN.shape, TOKEN.dtype)
         kernel(*refs[: end - 1], *refs[end:])
 
     return wrapped
@@ -116,11 +115,11 @@
             keys_t_ref[:, n * toks : (n + 1) * toks] = block_ref[...]
             keys_ref[n * toks : (n + 1) * toks] = block_ref[...].T
         position = place_ref[0]
-        seg_query = segments_ref[pl.ds(position, 1)].astype(jnp.float32)
+        seg_query = segments_ref[:, pl.ds(pl.multiple_of(position * toks, toks), toks)].astype(jnp.float32)
         for n in range(len(block_refs)):
             distance = len(block_refs) - 1 - n
             block = jnp.maximum(position - distance, 0)
-            seg_row = segments_ref[pl.ds(block, 1)].astype(jnp.float32)
+            seg_row = segments_ref[:, pl.ds(pl.multiple_of(block * toks, toks), toks)].astype(jnp.float32)
             seg_key = jnp.broadcast_to(seg_row, (toks, toks)).T
             granted = jnp.broadcast_to(mask_ref[position, block], (toks, toks)) == 1
             allowed = (seg_key == seg_query) | granted
@@ -386,7 +385,7 @@
         in_specs=[pl.BlockSpec(memory_space=pltpu.SMEM)]
         + [whole] * len(slabs)
         + [pl.BlockSpec(memory_space=pl.ANY)],
-        out_specs=[whole] * 5,
+        out_specs=[whole] * 4 + [TOKEN_BLOCK],
         out_shape=[jax.ShapeDtypeStruct((rows // 4, cols), jnp.bfloat16)] * 4 + [TOKEN],
         compiler_params=pltpu.CompilerParams(vmem_limit_bytes=16 * MIB),
         cost_estimate=BRIEF,
@@ -475,7 +474,7 @@
     return pl.pallas_call(
         with_token(stack_kernel),
         in_specs=[whole] * 2 * len(first) + [pl.BlockSpec(memory_space=pl.ANY)],
-        out_specs=[whole] * 3,
+        out_specs=[whole] * 2 + [TOKEN_BLOCK],
         out_shape=[jax.ShapeDtypeStruct((len(first) * rows, cols), first[0].dtype)] * 2 + [TOKEN],
         compiler_params=pltpu.CompilerParams(vmem_limit_bytes=16 * MIB),
         cost_estimate=BRIEF,
@@ -556,7 +555,7 @@
     width = query.shape[1] // heads
     inv_root = 1.0 / math.sqrt(width)
     position = lax.axis_index("ctx")
-    seg_rows = segments.reshape(-1, toks)
+    seg_rows = segments.reshape(1, -1)
     latent_t = latent.T
     blocks = [shifted(latent_t, "ctx", distance) for distance in (2, 1)] + [latent_t]
     qfull, dlo, dout_t, nope_t = prepare(query, d_out, w_uk, w_uv)

time: 169 us -> 169 us (level)
  transfers between devices with their start and end apart: 32 -> 32, of which waited for: 15 -> 15; matrix products, arithmetic and copies ran while one was open for 1% -> 0% of each run, Pallas kernels for 29% -> 29%
where the time goes in v6:
time: 169 us
  Pallas kernels  69.4 us (41%)
  starting transfers between devices  57.8 us (34%)
  waiting for transfers between devices  35.8 us (21%)
  local copies, waits for them, and re-layouts  4.27 us (3%)
    ppermute x25, starting transfers between devices, moved(): return lax.ppermute(block, 'ctx', route)  38.9 us
    pallas_call x2, Pallas kernels, score(): pl.pallas_call(with_token(functools.partial(score_kernel, inv_root, which...  34.7 us
    ppermute x25, waiting for transfers between devices, moved(): return lax.ppermute(block, 'ctx', route)  31.7 us
    pallas_call x1, Pallas kernels, key_gradient(): pl.pallas_call(with_token(key_kernel, 1), grid=(heads // GROUP,), in_spec...  13.3 us
    ppermute x4, starting transfers between devices, shifted(): return lax.ppermute(block, axis, route)  10.2 us
    pallas_call x1, Pallas kernels, prepare(): pl.pallas_call(prepare_kernel, grid=(heads // GROUP,), in_specs=[pl.Block...  8.34 us
    ppermute x2, starting transfers between devices, swap_core(): return lax.ppermute(block, 'head', [(0, 1), (1, 0), (2, 3), (3, 2)])  6.01 us
    pallas_call x2, Pallas kernels, widen(): pl.pallas_call(functools.partial(widen_kernel, chunk), in_specs=[pl.Block...  5.41 us
  transfers between devices with their start and end apart: 32, of which 15 were waited for; matrix products, arithmetic and copies ran while one was open for 0% of the time, Pallas kernels for 29%

profile of v6, /device:TPU:1, one launch (start us, length us, event | category | flops | bytes accessed | tf_op | source)
XLA Modules:
  0.0 169.0 jit_solution(12785060345993340184)
XLA Ops:
  0.6 4.0 %collective-permute-start.1 = (bf16[576,256]{1,0:T(8,128)(2,1)}, bf16[576,256]{1,0:T(8,128)(2,1)S(1)}, u32[]{:S(2)}, u32[]{:S(2)}) collective-permute-start(bf16[576,256]{1,0:T(8,128)(2,1)} %bitcast.10), channel_id=1, source_target_pairs={{0,4},{4,8},{8,12},{12,16},{16,20},{20,24},{24,28},{28,32},{32,36}... | collective-permute-start | bytes 884744 | tf_op jit(solution)/shard_map/ppermute | solution.py:24
  4.7 3.5 %collective-permute-start = (bf16[576,256]{1,0:T(8,128)(2,1)}, bf16[576,256]{1,0:T(8,128)(2,1)S(1)}, u32[]{:S(2)}, u32[]{:S(2)}) collective-permute-start(bf16[576,256]{1,0:T(8,128)(2,1)} %bitcast.11), channel_id=1, source_target_pairs={{0,8},{4,12},{8,16},{12,20},{16,24},{20,28},{24,32},{28,36},{32,40... | collective-permute-start | bytes 884744 | tf_op jit(solution)/shard_map/ppermute | solution.py:24
  8.3 8.3 %prepare.1 = (bf16[576,4096]{1,0:T(8,128)(2,1)}, bf16[512,4096]{1,0:T(8,128)(2,1)}, bf16[128,4096]{1,0:T(8,128)(2,1)}, bf16[128,4096]{1,0:T(8,128)(2,1)}) custom-call(bf16[256,3072]{1,0:T(8,128)(2,1)} %query_ref.1, bf16[256,2048]{1,0:T(8,128)(2,1)} %dout_ref.1, bf16[16,128,512]{2,1,0:T(8,128)(2,1)} %refs_2_.1, bf16[16,128,512]{2,1,0:T(8,128)(2,1)} %refs_3_.1), custom_call_target="tpu_custom_call" | custom-call | flops 1073741824 | bytes 16777216 | tf_op jit(solution)/shard_map/prepare/pallas_call | solution.py:74
  17.3 2.0 %collective-permute-done.refs_3__0_ = bf16[576,256]{1,0:T(8,128)(2,1)S(1)} collective-permute-done((bf16[576,256]{1,0:T(8,128)(2,1)}, bf16[576,256]{1,0:T(8,128)(2,1)S(1)}, u32[]{:S(2)}, u32[]{:S(2)}) %collective-permute-start) | collective-permute-done | bytes 294944 | tf_op jit(solution)/shard_map/ppermute | solution.py:24
  20.0 17.4 %score.2 = (bf16[768,4096]{1,0:T(8,128)(2,1)}, bf16[768,4096]{1,0:T(8,128)(2,1)}, bf16[512,4096]{1,0:T(8,128)(2,1)}, bf16[576,4096]{1,0:T(8,128)(2,1)}, bf16[512...) custom-call(s32[3]{0:T(128)} %pad_add_fusion.refs_0_.place_ref, ...), custom_call_target="tpu_custom_call" | custom-call | flops 13690208256 | bytes 25165824 | tf_op jit(solution)/shard_map/score/pallas_call | solution.py:174
  37.4 3.0 %collective-permute-start.2 = (bf16[512,512]{1,0:T(8,128)(2,1)}, bf16[512,512]{1,0:T(8,128)(2,1)S(1)}, u32[]{:S(2)}, u32[]{:S(2)}) collective-permute-start(bf16[512,512]{1,0:T(8,128)(2,1)} %get-tuple-element.70), channel_id=1, source_target_pairs={{0,32},{4,36},{8,40},{12,44},{16,48},{20,52},{24,56},{28,60},{32,6... | collective-permute-start | bytes 1572872 | tf_op jit(solution)/shard_map/ppermute | solution.py:533
  43.4 17.4 %score.3 = (bf16[768,4096]{1,0:T(8,128)(2,1)}, bf16[768,4096]{1,0:T(8,128)(2,1)}, bf16[512,4096]{1,0:T(8,128)(2,1)}, bf16[576,4096]{1,0:T(8,128)(2,1)}, bf16[512...) custom-call(s32[3]{0:T(128)} %pad_add_fusion.refs_0_.place_ref, ...), custom_call_target="tpu_custom_call", output_to_operand_aliasing={{0}: (10, {}), {1}: (11, {}), {2}: (12, {}), {3}: (13, {})} | custom-call | flops 13690208256 | bytes 25165824 | tf_op jit(solution)/shard_map/score/pallas_call | solution.py:174
  61.2 2.3 %collective-permute-start.9 = (bf16[512,512]{1,0:T(8,128)(2,1)}, bf16[512,512]{1,0:T(8,128)(2,1)S(1)}, u32[]{:S(2)}, u32[]{:S(2)}) collective-permute-start(bf16[512,512]{1,0:T(8,128)(2,1)} %get-tuple-element.80), channel_id=1, source_target_pairs={{0,24},{4,28},{8,0},{12,4},{16,8},{20,12},{24,16},{28,20},{32,56},... | collective-permute-start | bytes 1572872 | tf_op jit(solution)/shard_map/ppermute | solution.py:533
  67.2 13.3 %key_gradient.1 = (bf16[576,768]{1,0:T(8,128)(2,1)}, f32[8,128]{1,0:T(8,128)}) custom-call(bf16[576,4096]{1,0:T(8,128)(2,1)} %get-tuple-element.59.refs_4_.refs_0_, bf16[512,4096]{1,0:T(8,128)(2,1)} %get-tuple-element.60.refs_5_.refs_1_, bf16[768,4096]{1,0:T(8,128)(2,1)} %get-tuple-element.82.refs_2_, bf16[768,4096]{1,0:T(8,128)(2,1)} %get-tuple-element.83.refs_3_, ...), custom_call_target="tpu_custom_call" | custom-call | flops 13690208256 | bytes 25165824 | tf_op jit(solution)/shard_map/key_gradient/pallas_call | solution.py:241
  80.5 6.1 %collective-permute-done.10.refs_4_ = bf16[512,512]{1,0:T(8,128)(2,1)S(1)} collective-permute-done((bf16[512,512]{1,0:T(8,128)(2,1)}, bf16[512,512]{1,0:T(8,128)(2,1)S(1)}, u32[]{:S(2)}, u32[]{:S(2)}) %collective-permute-start.10) | collective-permute-done | bytes 524320 | tf_op jit(solution)/shard_map/ppermute | solution.py:533
  89.7 2.3 %collective-permute-start.14 = (bf16[288,768]{1,0:T(8,128)(2,1)S(1)}, bf16[288,768]{1,0:T(8,128)(2,1)S(1)}, u32[]{:S(2)}, u32[]{:S(2)}) collective-permute-start(bf16[288,768]{1,0:T(8,128)(2,1)S(1)} %get-tuple-element.93), channel_id=1, source_target_pairs={{0,1},{1,0},{2,3},{3,2},{4,5},{5,4},{6,7},{7,6},{8,9},{9,8},{10,11... | collective-permute-start | bytes 1327112 | tf_op jit(solution)/shard_map/ppermute | solution.py:545
  96.2 2.8 %collective-permute-start.5 = (bf16[128,512]{1,0:T(8,128)(2,1)S(1)}, bf16[128,512]{1,0:T(8,128)(2,1)S(1)}, u32[]{:S(2)}, u32[]{:S(2)}) collective-permute-start(bf16[128,512]{1,0:T(8,128)(2,1)S(1)} %get-tuple-element.75), channel_id=1, source_target_pairs={{0,8},{4,12},{8,16},{12,20},{16,24},{20,28},{24,0},{28,4},{32,40},... | collective-permute-start | bytes 393224 | tf_op jit(solution)/shard_map/ppermute | solution.py:533
  98.9 1.8 %collective-permute-start.6 = (bf16[128,512]{1,0:T(8,128)(2,1)S(1)}, bf16[128,512]{1,0:T(8,128)(2,1)S(1)}, u32[]{:S(2)}, u32[]{:S(2)}) collective-permute-start(bf16[128,512]{1,0:T(8,128)(2,1)S(1)} %get-tuple-element.76), channel_id=1, source_target_pairs={{0,24},{4,28},{8,0},{12,4},{16,8},{20,12},{24,16},{28,20},{32,56},... | collective-permute-start | bytes 393224 | tf_op jit(solution)/shard_map/ppermute | solution.py:533
  100.7 2.0 %collective-permute-start.7 = (bf16[128,512]{1,0:T(8,128)(2,1)S(1)}, bf16[128,512]{1,0:T(8,128)(2,1)S(1)}, u32[]{:S(2)}, u32[]{:S(2)}) collective-permute-start(bf16[128,512]{1,0:T(8,128)(2,1)S(1)} %get-tuple-element.77), channel_id=1, source_target_pairs={{0,16},{4,20},{8,24},{12,28},{16,0},{20,4},{24,8},{28,12},{32,48},... | collective-permute-start | bytes 393224 | tf_op jit(solution)/shard_map/ppermute | solution.py:533
  103.6 3.9 %collective-permute-start.11 = (bf16[128,512]{1,0:T(8,128)(2,1)S(1)}, bf16[128,512]{1,0:T(8,128)(2,1)S(1)}, u32[]{:S(2)}, u32[]{:S(2)}) collective-permute-start(bf16[128,512]{1,0:T(8,128)(2,1)S(1)} %get-tuple-element.87), channel_id=1, source_target_pairs={{0,32},{4,36},{8,40},{12,44},{16,48},{20,52},{24,56},{28,60},{32,6... | collective-permute-start | bytes 393224 | tf_op jit(solution)/shard_map/ppermute | solution.py:533
  107.9 2.0 %collective-permute-start.13 = (bf16[128,512]{1,0:T(8,128)(2,1)S(1)}, bf16[128,512]{1,0:T(8,128)(2,1)S(1)}, u32[]{:S(2)}, u32[]{:S(2)}) collective-permute-start(bf16[128,512]{1,0:T(8,128)(2,1)S(1)} %get-tuple-element.89), channel_id=1, source_target_pairs={{0,64},{4,68},{8,72},{12,76},{16,80},{20,84},{24,88},{28,92},{32,9... | collective-permute-start | bytes 393224 | tf_op jit(solution)/shard_map/ppermute | solution.py:533
  110.0 2.7 %collective-permute-start.24 = (bf16[288,256]{1,0:T(8,128)(2,1)S(1)}, bf16[288,256]{1,0:T(8,128)(2,1)S(1)}, u32[]{:S(2)}, u32[]{:S(2)}) collective-permute-start(bf16[288,256]{1,0:T(8,128)(2,1)S(1)} %merge.1.refs_0_), channel_id=1, source_target_pairs={{0,2},{2,0},{1,3},{3,1},{4,6},{6,4},{5,7},{7,5},{8,10},{10,8},{9,1... | collective-permute-start | bytes 442376 | tf_op jit(solution)/shard_map/ppermute | solution.py:549
  112.7 1.8 %collective-permute-done.13.refs_7_ = bf16[128,512]{1,0:T(8,128)(2,1)S(1)} collective-permute-done((bf16[128,512]{1,0:T(8,128)(2,1)S(1)}, bf16[128,512]{1,0:T(8,128)(2,1)S(1)}, u32[]{:S(2)}, u32[]{:S(2)}) %collective-permute-start.13) | collective-permute-done | bytes 131104 | tf_op jit(solution)/shard_map/ppermute | solution.py:533
  116.4 3.7 %collective-permute-start.25 = (f32[288,256]{1,0:T(8,128)S(1)}, f32[288,256]{1,0:T(8,128)S(1)}, u32[]{:S(2)}, u32[]{:S(2)}) collective-permute-start(f32[288,256]{1,0:T(8,128)S(1)} %get-tuple-element.100.refs_1_), channel_id=1, source_target_pairs={{0,1},{1,0},{2,3},{3,2},{4,5},{5,4},{6,7},{7,6},{8,9},{9,8},{10,11... | collective-permute-start | bytes 884744 | tf_op jit(solution)/shard_map/ppermute | solution.py:545
  120.2 1.8 %collective-permute-done.15.other_ref = bf16[256,512]{1,0:T(8,128)(2,1)S(1)} collective-permute-done((bf16[256,512]{1,0:T(8,128)(2,1)S(1)}, bf16[256,512]{1,0:T(8,128)(2,1)S(1)}, u32[]{:S(2)}, u32[]{:S(2)}) %collective-permute-start.15) | collective-permute-done | bytes 262176 | tf_op jit(solution)/shard_map/ppermute | solution.py:533
  122.1 4.6 %collective-permute-start.17 = (bf16[128,512]{1,0:T(8,128)(2,1)S(1)}, bf16[128,512]{1,0:T(8,128)(2,1)S(1)}, u32[]{:S(2)}, u32[]{:S(2)}) collective-permute-start(bf16[128,512]{1,0:T(8,128)(2,1)S(1)} %get-tuple-element.95.refs_0_), channel_id=1, source_target_pairs={{0,24},{4,28},{8,0},{12,4},{16,8},{20,12},{24,16},{28,20},{32,56},... | collective-permute-start | bytes 393224 | tf_op jit(solution)/shard_map/ppermute | solution.py:533
  127.2 1.8 %collective-permute-start.21 = (bf16[128,512]{1,0:T(8,128)(2,1)S(1)}, bf16[128,512]{1,0:T(8,128)(2,1)S(1)}, u32[]{:S(2)}, u32[]{:S(2)}) collective-permute-start(bf16[128,512]{1,0:T(8,128)(2,1)S(1)} %get-tuple-element.96.refs_4_), channel_id=1, source_target_pairs={{0,64},{4,68},{8,72},{12,76},{16,80},{20,84},{24,88},{28,92},{32,9... | collective-permute-start | bytes 393224 | tf_op jit(solution)/shard_map/ppermute | solution.py:533
  132.5 1.8 %collective-permute-done.20.refs_6_ = bf16[128,512]{1,0:T(8,128)(2,1)S(1)} collective-permute-done((bf16[128,512]{1,0:T(8,128)(2,1)S(1)}, bf16[128,512]{1,0:T(8,128)(2,1)S(1)}, u32[]{:S(2)}, u32[]{:S(2)}) %collective-permute-start.20) | collective-permute-done | bytes 131104 | tf_op jit(solution)/shard_map/ppermute | solution.py:533
  134.3 2.3 %collective-permute-done.19.refs_5_ = bf16[128,512]{1,0:T(8,128)(2,1)S(1)} collective-permute-done((bf16[128,512]{1,0:T(8,128)(2,1)S(1)}, bf16[128,512]{1,0:T(8,128)(2,1)S(1)}, u32[]{:S(2)}, u32[]{:S(2)}) %collective-permute-start.19) | collective-permute-done | bytes 131104 | tf_op jit(solution)/shard_map/ppermute | solution.py:533
  138.3 2.1 %collective-permute-start.28 = (bf16[512,512]{1,0:T(8,128)(2,1)S(1)}, bf16[512,512]{1,0:T(8,128)(2,1)S(1)}, u32[]{:S(2)}, u32[]{:S(2)}) collective-permute-start(bf16[512,512]{1,0:T(8,128)(2,1)S(1)} %get-tuple-element.106.refs_0_), channel_id=1, source_target_pairs={{0,16},{4,20},{8,24},{12,28},{16,0},{20,4},{24,8},{28,12},{32,48},... | collective-permute-start | bytes 1572872 | tf_op jit(solution)/shard_map/ppermute | solution.py:533
  140.4 1.9 %collective-permute-start.27 = (bf16[512,512]{1,0:T(8,128)(2,1)S(1)}, bf16[512,512]{1,0:T(8,128)(2,1)S(1)}, u32[]{:S(2)}, u32[]{:S(2)}) collective-permute-start(bf16[512,512]{1,0:T(8,128)(2,1)S(1)} %get-tuple-element.106.refs_0_), channel_id=1, source_target_pairs={{0,24},{4,28},{8,0},{12,4},{16,8},{20,12},{24,16},{28,20},{32,56},... | collective-permute-start | bytes 1572872 | tf_op jit(solution)/shard_map/ppermute | solution.py:533
  142.3 6.9 %collective-permute-done.31.refs_3_ = bf16[512,512]{1,0:T(8,128)(2,1)S(1)} collective-permute-done((bf16[512,512]{1,0:T(8,128)(2,1)S(1)}, bf16[512,512]{1,0:T(8,128)(2,1)S(1)}, u32[]{:S(2)}, u32[]{:S(2)}) %collective-permute-start.31) | collective-permute-done | bytes 524320 | tf_op jit(solution)/shard_map/ppermute | solution.py:533
  150.8 4.0 %project.1 = (bf16[256,2048]{1,0:T(8,128)(2,1)}, bf16[256,3072]{1,0:T(8,128)(2,1)}, f32[8,128]{1,0:T(8,128)S(1)}) custom-call(bf16[512,4096]{1,0:T(8,128)(2,1)S(1)} %copy-done.2, bf16[576,4096]{1,0:T(8,128)(2,1)S(1)} %bitcast.8, bf16[16,128,512]{2,1,0:T(8,128)(2,1)S(1)} %copy-done, bf16[16,128,512]{2,1,0:T(8,128)(2,1)S(1)} %copy-done.1, ...), custom_call_target="tpu_custom_call" | custom-call | flops 1048576 | bytes 1048576 | tf_op jit(solution)/shard_map/project/pallas_call | solution.py:352
  154.8 5.0 %collective-permute-done.30.refs_2_ = bf16[512,512]{1,0:T(8,128)(2,1)S(1)} collective-permute-done((bf16[512,512]{1,0:T(8,128)(2,1)S(1)}, bf16[512,512]{1,0:T(8,128)(2,1)S(1)}, u32[]{:S(2)}, u32[]{:S(2)}) %collective-permute-start.30) | collective-permute-done | bytes 524320 | tf_op jit(solution)/shard_map/ppermute | solution.py:533
  159.8 3.5 %collective-permute-done.29.refs_1_ = bf16[512,512]{1,0:T(8,128)(2,1)S(1)} collective-permute-done((bf16[512,512]{1,0:T(8,128)(2,1)S(1)}, bf16[512,512]{1,0:T(8,128)(2,1)S(1)}, u32[]{:S(2)}, u32[]{:S(2)}) %collective-permute-start.29) | collective-permute-done | bytes 524320 | tf_op jit(solution)/shard_map/ppermute | solution.py:533
  163.3 2.7 %widen.2 = (f32[16,128,512]{2,1,0:T(8,128)}, f32[16,128,512]{2,1,0:T(8,128)}) custom-call(s32[3]{0:T(128)S(1)} %copy-done.6, bf16[512,512]{1,0:T(8,128)(2,1)S(1)} %get-tuple-element.108.refs_0_, bf16[512,512]{1,0:T(8,128)(2,1)S(1)} %collective-permute-done.29.refs_1_, bf16[512,512]{1,0:T(8,128)(2,1)S(1)} %collective-permute-done.30.refs_2_, ...), custom_call_target="tpu_custom_call" | custom-call | flops 1048576 | bytes 1048576 | tf_op jit(solution)/shard_map/widen/pallas_call | solution.py:508
  166.1 2.7 %widen.3 = (f32[16,128,512]{2,1,0:T(8,128)}, f32[16,128,512]{2,1,0:T(8,128)}) custom-call(s32[3]{0:T(128)S(1)} %copy-done.6, bf16[512,512]{1,0:T(8,128)(2,1)S(1)} %get-tuple-element.106.refs_0_, bf16[512,512]{1,0:T(8,128)(2,1)S(1)} %collective-permute-done.26.refs_1_, ...), custom_call_target="tpu_custom_call", output_to_operand_aliasing={{0}: (6, {}), {1}: (7, {})} | custom-call | flops 1048576 | bytes 1048576 | tf_op jit(solution)/shard_map/widen/pallas_call | solution.py:508
  (79 shorter events, 26.3 us)
Async XLA Ops:
  0.6 16.6 %collective-permute-start.1 = (bf16[576,256]{1,0:T(8,128)(2,1)}, bf16[576,256]{1,0:T(8,128)(2,1)S(1)}, u32[]{:S(2)}, u32[]{:S(2)}) collective-permute-start(bf16[576,256]{1,0:T(8,128)(2,1)} %bitcast.10), channel_id=1, source_target_pairs={{0,4},{4,8},{8,12},{12,16},{16,20},{20,24},{24,28},{28,32},{32,36}... | collective-permute-start | bytes 884744 | tf_op jit(solution)/shard_map/ppermute | solution.py:24
  4.7 14.6 %collective-permute-start = (bf16[576,256]{1,0:T(8,128)(2,1)}, bf16[576,256]{1,0:T(8,128)(2,1)S(1)}, u32[]{:S(2)}, u32[]{:S(2)}) collective-permute-start(bf16[576,256]{1,0:T(8,128)(2,1)} %bitcast.11), channel_id=1, source_target_pairs={{0,8},{4,12},{8,16},{12,20},{16,24},{20,28},{24,32},{28,36},{32,40... | collective-permute-start | bytes 884744 | tf_op jit(solution)/shard_map/ppermute | solution.py:24
  37.4 26.1 %collective-permute-start.2 = (bf16[512,512]{1,0:T(8,128)(2,1)}, bf16[512,512]{1,0:T(8,128)(2,1)S(1)}, u32[]{:S(2)}, u32[]{:S(2)}) collective-permute-start(bf16[512,512]{1,0:T(8,128)(2,1)} %get-tuple-element.70), channel_id=1, source_target_pairs={{0,32},{4,36},{8,40},{12,44},{16,48},{20,52},{24,56},{28,60},{32,6... | collective-permute-start | bytes 1572872 | tf_op jit(solution)/shard_map/ppermute | solution.py:533
  40.4 24.2 %collective-permute-start.3 = (bf16[512,512]{1,0:T(8,128)(2,1)}, bf16[512,512]{1,0:T(8,128)(2,1)S(1)}, u32[]{:S(2)}, u32[]{:S(2)}) collective-permute-start(bf16[512,512]{1,0:T(8,128)(2,1)} %get-tuple-element.71), channel_id=1, source_target_pairs={{0,96},{4,100},{8,104},{12,108},{16,112},{20,116},{24,120},{28,124... | collective-permute-start | bytes 1572872 | tf_op jit(solution)/shard_map/ppermute | solution.py:533
  42.1 23.0 %collective-permute-start.4 = (bf16[512,512]{1,0:T(8,128)(2,1)}, bf16[512,512]{1,0:T(8,128)(2,1)S(1)}, u32[]{:S(2)}, u32[]{:S(2)}) collective-permute-start(bf16[512,512]{1,0:T(8,128)(2,1)} %get-tuple-element.72), channel_id=1, source_target_pairs={{0,64},{4,68},{8,72},{12,76},{16,80},{20,84},{24,88},{28,92},{32,9... | collective-permute-start | bytes 1572872 | tf_op jit(solution)/shard_map/ppermute | solution.py:533
  60.7 19.7 %collective-permute-start.8 = (bf16[512,512]{1,0:T(8,128)(2,1)}, bf16[512,512]{1,0:T(8,128)(2,1)S(1)}, u32[]{:S(2)}, u32[]{:S(2)}) collective-permute-start(bf16[512,512]{1,0:T(8,128)(2,1)} %get-tuple-element.79), channel_id=1, source_target_pairs={{0,8},{4,12},{8,16},{12,20},{16,24},{20,28},{24,0},{28,4},{32,40},... | collective-permute-start | bytes 1572872 | tf_op jit(solution)/shard_map/ppermute | solution.py:533
  61.2 19.3 %collective-permute-start.9 = (bf16[512,512]{1,0:T(8,128)(2,1)}, bf16[512,512]{1,0:T(8,128)(2,1)S(1)}, u32[]{:S(2)}, u32[]{:S(2)}) collective-permute-start(bf16[512,512]{1,0:T(8,128)(2,1)} %get-tuple-element.80), channel_id=1, source_target_pairs={{0,24},{4,28},{8,0},{12,4},{16,8},{20,12},{24,16},{28,20},{32,56},... | collective-permute-start | bytes 1572872 | tf_op jit(solution)/shard_map/ppermute | solution.py:533
  63.5 23.1 %collective-permute-start.10 = (bf16[512,512]{1,0:T(8,128)(2,1)}, bf16[512,512]{1,0:T(8,128)(2,1)S(1)}, u32[]{:S(2)}, u32[]{:S(2)}) collective-permute-start(bf16[512,512]{1,0:T(8,128)(2,1)} %get-tuple-element.81), channel_id=1, source_target_pairs={{0,16},{4,20},{8,24},{12,28},{16,0},{20,4},{24,8},{28,12},{32,48},... | collective-permute-start | bytes 1572872 | tf_op jit(solution)/shard_map/ppermute | solution.py:533
  89.7 3.7 %collective-permute-start.14 = (bf16[288,768]{1,0:T(8,128)(2,1)S(1)}, bf16[288,768]{1,0:T(8,128)(2,1)S(1)}, u32[]{:S(2)}, u32[]{:S(2)}) collective-permute-start(bf16[288,768]{1,0:T(8,128)(2,1)S(1)} %get-tuple-element.93), channel_id=1, source_target_pairs={{0,1},{1,0},{2,3},{3,2},{4,5},{5,4},{6,7},{7,6},{8,9},{9,8},{10,11... | collective-permute-start | bytes 1327112 | tf_op jit(solution)/shard_map/ppermute | solution.py:545
  93.6 13.9 %collective-permute-start.22 = (bf16[288,256]{1,0:T(8,128)(2,1)S(1)}, bf16[288,256]{1,0:T(8,128)(2,1)S(1)}, u32[]{:S(2)}, u32[]{:S(2)}) collective-permute-start(bf16[288,256]{1,0:T(8,128)(2,1)S(1)} %get-tuple-element.98), channel_id=1, source_target_pairs={{8,0},{12,4},{16,8},{20,12},{24,16},{28,20},{32,24},{36,28},{40,32... | collective-permute-start | bytes 442376 | tf_op jit(solution)/shard_map/ppermute | solution.py:24
  94.9 13.1 %collective-permute-start.23 = (bf16[288,256]{1,0:T(8,128)(2,1)S(1)}, bf16[288,256]{1,0:T(8,128)(2,1)S(1)}, u32[]{:S(2)}, u32[]{:S(2)}) collective-permute-start(bf16[288,256]{1,0:T(8,128)(2,1)S(1)} %get-tuple-element.99), channel_id=1, source_target_pairs={{4,0},{8,4},{12,8},{16,12},{20,16},{24,20},{28,24},{32,28},{36,32}... | collective-permute-start | bytes 442376 | tf_op jit(solution)/shard_map/ppermute | solution.py:24
  96.2 7.4 %collective-permute-start.5 = (bf16[128,512]{1,0:T(8,128)(2,1)S(1)}, bf16[128,512]{1,0:T(8,128)(2,1)S(1)}, u32[]{:S(2)}, u32[]{:S(2)}) collective-permute-start(bf16[128,512]{1,0:T(8,128)(2,1)S(1)} %get-tuple-element.75), channel_id=1, source_target_pairs={{0,8},{4,12},{8,16},{12,20},{16,24},{20,28},{24,0},{28,4},{32,40},... | collective-permute-start | bytes 393224 | tf_op jit(solution)/shard_map/ppermute | solution.py:533
  98.9 11.0 %collective-permute-start.6 = (bf16[128,512]{1,0:T(8,128)(2,1)S(1)}, bf16[128,512]{1,0:T(8,128)(2,1)S(1)}, u32[]{:S(2)}, u32[]{:S(2)}) collective-permute-start(bf16[128,512]{1,0:T(8,128)(2,1)S(1)} %get-tuple-element.76), channel_id=1, source_target_pairs={{0,24},{4,28},{8,0},{12,4},{16,8},{20,12},{24,16},{28,20},{32,56},... | collective-permute-start | bytes 393224 | tf_op jit(solution)/shard_map/ppermute | solution.py:533
  100.7 11.9 %collective-permute-start.7 = (bf16[128,512]{1,0:T(8,128)(2,1)S(1)}, bf16[128,512]{1,0:T(8,128)(2,1)S(1)}, u32[]{:S(2)}, u32[]{:S(2)}) collective-permute-start(bf16[128,512]{1,0:T(8,128)(2,1)S(1)} %get-tuple-element.77), channel_id=1, source_target_pairs={{0,16},{4,20},{8,24},{12,28},{16,0},{20,4},{24,8},{28,12},{32,48},... | collective-permute-start | bytes 393224 | tf_op jit(solution)/shard_map/ppermute | solution.py:533
  103.6 9.1 %collective-permute-start.11 = (bf16[128,512]{1,0:T(8,128)(2,1)S(1)}, bf16[128,512]{1,0:T(8,128)(2,1)S(1)}, u32[]{:S(2)}, u32[]{:S(2)}) collective-permute-start(bf16[128,512]{1,0:T(8,128)(2,1)S(1)} %get-tuple-element.87), channel_id=1, source_target_pairs={{0,32},{4,36},{8,40},{12,44},{16,48},{20,52},{24,56},{28,60},{32,6... | collective-permute-start | bytes 393224 | tf_op jit(solution)/shard_map/ppermute | solution.py:533
  107.5 5.2 %collective-permute-start.12 = (bf16[128,512]{1,0:T(8,128)(2,1)S(1)}, bf16[128,512]{1,0:T(8,128)(2,1)S(1)}, u32[]{:S(2)}, u32[]{:S(2)}) collective-permute-start(bf16[128,512]{1,0:T(8,128)(2,1)S(1)} %get-tuple-element.88), channel_id=1, source_target_pairs={{0,96},{4,100},{8,104},{12,108},{16,112},{20,116},{24,120},{28,124... | collective-permute-start | bytes 393224 | tf_op jit(solution)/shard_map/ppermute | solution.py:533
  107.9 6.5 %collective-permute-start.13 = (bf16[128,512]{1,0:T(8,128)(2,1)S(1)}, bf16[128,512]{1,0:T(8,128)(2,1)S(1)}, u32[]{:S(2)}, u32[]{:S(2)}) collective-permute-start(bf16[128,512]{1,0:T(8,128)(2,1)S(1)} %get-tuple-element.89), channel_id=1, source_target_pairs={{0,64},{4,68},{8,72},{12,76},{16,80},{20,84},{24,88},{28,92},{32,9... | collective-permute-start | bytes 393224 | tf_op jit(solution)/shard_map/ppermute | solution.py:533
  110.0 5.9 %collective-permute-start.24 = (bf16[288,256]{1,0:T(8,128)(2,1)S(1)}, bf16[288,256]{1,0:T(8,128)(2,1)S(1)}, u32[]{:S(2)}, u32[]{:S(2)}) collective-permute-start(bf16[288,256]{1,0:T(8,128)(2,1)S(1)} %merge.1.refs_0_), channel_id=1, source_target_pairs={{0,2},{2,0},{1,3},{3,1},{4,6},{6,4},{5,7},{7,5},{8,10},{10,8},{9,1... | collective-permute-start | bytes 442376 | tf_op jit(solution)/shard_map/ppermute | solution.py:549
  114.6 7.4 %collective-permute-start.15 = (bf16[256,512]{1,0:T(8,128)(2,1)S(1)}, bf16[256,512]{1,0:T(8,128)(2,1)S(1)}, u32[]{:S(2)}, u32[]{:S(2)}) collective-permute-start(bf16[256,512]{1,0:T(8,128)(2,1)S(1)} %totals.1.mine_ref), channel_id=1, source_target_pairs={{0,4},{4,0},{8,12},{12,8},{16,20},{20,16},{24,28},{28,24},{32,36},... | collective-permute-start | bytes 786440 | tf_op jit(solution)/shard_map/ppermute | solution.py:533
  116.4 14.0 %collective-permute-start.25 = (f32[288,256]{1,0:T(8,128)S(1)}, f32[288,256]{1,0:T(8,128)S(1)}, u32[]{:S(2)}, u32[]{:S(2)}) collective-permute-start(f32[288,256]{1,0:T(8,128)S(1)} %get-tuple-element.100.refs_1_), channel_id=1, source_target_pairs={{0,1},{1,0},{2,3},{3,2},{4,5},{5,4},{6,7},{7,6},{8,9},{9,8},{10,11... | collective-permute-start | bytes 884744 | tf_op jit(solution)/shard_map/ppermute | solution.py:545
  122.0 7.0 %collective-permute-start.18 = (bf16[128,512]{1,0:T(8,128)(2,1)S(1)}, bf16[128,512]{1,0:T(8,128)(2,1)S(1)}, u32[]{:S(2)}, u32[]{:S(2)}) collective-permute-start(bf16[128,512]{1,0:T(8,128)(2,1)S(1)} %get-tuple-element.95.refs_0_), channel_id=1, source_target_pairs={{0,16},{4,20},{8,24},{12,28},{16,0},{20,4},{24,8},{28,12},{32,48},... | collective-permute-start | bytes 393224 | tf_op jit(solution)/shard_map/ppermute | solution.py:533
  122.1 10.1 %collective-permute-start.17 = (bf16[128,512]{1,0:T(8,128)(2,1)S(1)}, bf16[128,512]{1,0:T(8,128)(2,1)S(1)}, u32[]{:S(2)}, u32[]{:S(2)}) collective-permute-start(bf16[128,512]{1,0:T(8,128)(2,1)S(1)} %get-tuple-element.95.refs_0_), channel_id=1, source_target_pairs={{0,24},{4,28},{8,0},{12,4},{16,8},{20,12},{24,16},{28,20},{32,56},... | collective-permute-start | bytes 393224 | tf_op jit(solution)/shard_map/ppermute | solution.py:533
  126.7 5.5 %collective-permute-start.16 = (bf16[128,512]{1,0:T(8,128)(2,1)S(1)}, bf16[128,512]{1,0:T(8,128)(2,1)S(1)}, u32[]{:S(2)}, u32[]{:S(2)}) collective-permute-start(bf16[128,512]{1,0:T(8,128)(2,1)S(1)} %get-tuple-element.95.refs_0_), channel_id=1, source_target_pairs={{0,8},{4,12},{8,16},{12,20},{16,24},{20,28},{24,0},{28,4},{32,40},... | collective-permute-start | bytes 393224 | tf_op jit(solution)/shard_map/ppermute | solution.py:533
  127.2 5.3 %collective-permute-start.21 = (bf16[128,512]{1,0:T(8,128)(2,1)S(1)}, bf16[128,512]{1,0:T(8,128)(2,1)S(1)}, u32[]{:S(2)}, u32[]{:S(2)}) collective-permute-start(bf16[128,512]{1,0:T(8,128)(2,1)S(1)} %get-tuple-element.96.refs_4_), channel_id=1, source_target_pairs={{0,64},{4,68},{8,72},{12,76},{16,80},{20,84},{24,88},{28,92},{32,9... | collective-permute-start | bytes 393224 | tf_op jit(solution)/shard_map/ppermute | solution.py:533
  129.1 5.3 %collective-permute-start.20 = (bf16[128,512]{1,0:T(8,128)(2,1)S(1)}, bf16[128,512]{1,0:T(8,128)(2,1)S(1)}, u32[]{:S(2)}, u32[]{:S(2)}) collective-permute-start(bf16[128,512]{1,0:T(8,128)(2,1)S(1)} %get-tuple-element.96.refs_4_), channel_id=1, source_target_pairs={{0,96},{4,100},{8,104},{12,108},{16,112},{20,116},{24,120},{28,124... | collective-permute-start | bytes 393224 | tf_op jit(solution)/shard_map/ppermute | solution.py:533
  130.5 6.1 %collective-permute-start.19 = (bf16[128,512]{1,0:T(8,128)(2,1)S(1)}, bf16[128,512]{1,0:T(8,128)(2,1)S(1)}, u32[]{:S(2)}, u32[]{:S(2)}) collective-permute-start(bf16[128,512]{1,0:T(8,128)(2,1)S(1)} %get-tuple-element.96.refs_4_), channel_id=1, source_target_pairs={{0,32},{4,36},{8,40},{12,44},{16,48},{20,52},{24,56},{28,60},{32,6... | collective-permute-start | bytes 393224 | tf_op jit(solution)/shard_map/ppermute | solution.py:533
  136.7 12.6 %collective-permute-start.31 = (bf16[512,512]{1,0:T(8,128)(2,1)S(1)}, bf16[512,512]{1,0:T(8,128)(2,1)S(1)}, u32[]{:S(2)}, u32[]{:S(2)}) collective-permute-start(bf16[512,512]{1,0:T(8,128)(2,1)S(1)} %get-tuple-element.108.refs_0_), channel_id=1, source_target_pairs={{0,64},{4,68},{8,72},{12,76},{16,80},{20,84},{24,88},{28,92},{32,9... | collective-permute-start | bytes 1572872 | tf_op jit(solution)/shard_map/ppermute | solution.py:533
  136.7 23.1 %collective-permute-start.30 = (bf16[512,512]{1,0:T(8,128)(2,1)S(1)}, bf16[512,512]{1,0:T(8,128)(2,1)S(1)}, u32[]{:S(2)}, u32[]{:S(2)}) collective-permute-start(bf16[512,512]{1,0:T(8,128)(2,1)S(1)} %get-tuple-element.108.refs_0_), channel_id=1, source_target_pairs={{0,96},{4,100},{8,104},{12,108},{16,112},{20,116},{24,120},{28,124... | collective-permute-start | bytes 1572872 | tf_op jit(solution)/shard_map/ppermute | solution.py:533
  137.7 25.6 %collective-permute-start.29 = (bf16[512,512]{1,0:T(8,128)(2,1)S(1)}, bf16[512,512]{1,0:T(8,128)(2,1)S(1)}, u32[]{:S(2)}, u32[]{:S(2)}) collective-permute-start(bf16[512,512]{1,0:T(8,128)(2,1)S(1)} %get-tuple-element.108.refs_0_), channel_id=1, source_target_pairs={{0,32},{4,36},{8,40},{12,44},{16,48},{20,52},{24,56},{28,60},{32,6... | collective-permute-start | bytes 1572872 | tf_op jit(solution)/shard_map/ppermute | solution.py:533
  138.3 27.7 %collective-permute-start.28 = (bf16[512,512]{1,0:T(8,128)(2,1)S(1)}, bf16[512,512]{1,0:T(8,128)(2,1)S(1)}, u32[]{:S(2)}, u32[]{:S(2)}) collective-permute-start(bf16[512,512]{1,0:T(8,128)(2,1)S(1)} %get-tuple-element.106.refs_0_), channel_id=1, source_target_pairs={{0,16},{4,20},{8,24},{12,28},{16,0},{20,4},{24,8},{28,12},{32,48},... | collective-permute-start | bytes 1572872 | tf_op jit(solution)/shard_map/ppermute | solution.py:533
  140.4 25.6 %collective-permute-start.27 = (bf16[512,512]{1,0:T(8,128)(2,1)S(1)}, bf16[512,512]{1,0:T(8,128)(2,1)S(1)}, u32[]{:S(2)}, u32[]{:S(2)}) collective-permute-start(bf16[512,512]{1,0:T(8,128)(2,1)S(1)} %get-tuple-element.106.refs_0_), channel_id=1, source_target_pairs={{0,24},{4,28},{8,0},{12,4},{16,8},{20,12},{24,16},{28,20},{32,56},... | collective-permute-start | bytes 1572872 | tf_op jit(solution)/shard_map/ppermute | solution.py:533
  149.2 16.8 %collective-permute-start.26 = (bf16[512,512]{1,0:T(8,128)(2,1)S(1)}, bf16[512,512]{1,0:T(8,128)(2,1)S(1)}, u32[]{:S(2)}, u32[]{:S(2)}) collective-permute-start(bf16[512,512]{1,0:T(8,128)(2,1)S(1)} %get-tuple-element.106.refs_0_), channel_id=1, source_target_pairs={{0,8},{4,12},{8,16},{12,20},{16,24},{20,28},{24,0},{28,4},{32,40},... | collective-permute-start | bytes 1572872 | tf_op jit(solution)/shard_map/ppermute | solution.py:533
  (14 other events, 426.6 us)
